TPU v7x, 256 devices: a whole 4x4x8 slice. The times are simulated.
256 devices in a mesh: dp: 8 (over z), seq: 32 (over x, y, core).
Axes of the slice: x: 4, y: 4, z: 8, core: 2. Of those that a mesh axis runs over, the one named last changes fastest.
Arguments:
- tokens: bfloat16 [16, 2048, 768], P('dp', 'seq'), may hold values from -6 to 6
- lengths: int32 [16], P('dp'), may hold values from 128 to 2048, as said below
- w_value: bfloat16 [768, 768], P('seq'), may hold values from -0.21875 to 0.21875
- w_out: bfloat16 [768, 768], P('seq'), may hold values from -0.625 to 0.625
- w_up: bfloat16 [768, 3072], P('seq'), may hold values from -0.21875 to 0.21875
- w_down: bfloat16 [3072, 768], P('seq'), may hold values from -0.109375 to 0.109375
- gain_mix: float32 [768], replicated, may hold values from 0.1 to 1.9
- gain_ffn: float32 [768], replicated, may hold values from 0.1 to 1.9
- mix_table: bfloat16 [12, 2048, 2048], P(None, 'seq'), may hold values from -9 to 9
- out_grad: bfloat16 [16, 2048, 768], P('dp', 'seq'), may hold values from -6 to 6
Outputs:
- output: bfloat16 [16, 2048, 768], P('dp', 'seq')
- input_grad: float32 [16, 2048, 768], P('dp', 'seq')
- value_weight_grad: float32 [768, 768], P('seq')
- out_weight_grad: float32 [768, 768], P('seq')
- up_weight_grad: float32 [768, 3072], P('seq')
- down_weight_grad: float32 [3072, 768], P('seq')
- mix_gain_grad: float32 [768], P('seq')
- ffn_gain_grad: float32 [768], P('seq')
- table_grad: float32 [12, 2048, 2048], P(None, 'seq', 'dp')
Inputs may be any that keep to these rules, and one draw needn't show every extreme that they name: `lengths`: within each group of 2 items held by one index of dp, one item, which one drawn from the seed, has length 2048.
All inputs are finite; a program needn't handle non-finite values.
Results may differ from a plain program's by a relative error of at most 0.0095.
Values may be sent and summed in bfloat16 or wider, within the bound.
A program may use at most 128 MiB of HBM per device.

v0:
```python
import jax
import jax.numpy as jnp
from jax import lax
from jax.sharding import PartitionSpec as P

D = 768
HEADS = 12
HEAD_DIM = 64


EPS = 1e-06


def combined_all(value, axis, join):
    pieces = jax.tree.map(lambda part: lax.all_gather(part, axis), value)
    head = jax.tree.map(lambda part: part[0], pieces)
    tail = jax.tree.map(lambda part: part[1:], pieces)
    running, _ = lax.scan(lambda running, section: (join(running, section), None), head, tail)
    return running


def norm_forward(value, gain):
    scale = lax.rsqrt(jnp.mean(value * value, axis=-1, keepdims=True) + EPS)
    return (value * scale * gain, scale)


def norm_backward(value, scale, gain, normed_grad):
    weighted = normed_grad * gain
    inner = jnp.mean(weighted * value, axis=-1, keepdims=True)
    value_grad = scale * weighted - value * (scale * scale * scale) * inner
    gain_grad = jnp.sum(normed_grad * value * scale, axis=(0, 1))
    return (value_grad, gain_grad)


def column_stats(scores, col_ok):
    masked = jnp.where(col_ok[:, :, None], scores[None], -1e30)
    row_top = jnp.max(masked, axis=1)
    exponent = jnp.where(col_ok[:, :, None], jnp.exp(masked - row_top[:, None, :]), 0.0)
    return (row_top, jnp.sum(exponent, axis=1))


def combine_stats(first, second):
    row_top = jnp.maximum(first[0], second[0])
    row_total = first[1] * jnp.exp(first[0] - row_top) + second[1] * jnp.exp(second[0] - row_top)
    return (row_top, row_total)


def column_probs(scores, row_top, row_total, row_ok, col_ok):
    valid_pair = col_ok[:, :, None] & row_ok[:, None, :]
    exponent = jnp.exp(jnp.minimum(scores[None] - row_top[:, None, :], 0.0))
    return jnp.where(valid_pair, exponent / row_total[:, None, :], 0.0)


def head_slice(value, head_index):
    return lax.dynamic_slice_in_dim(value, head_index * HEAD_DIM, HEAD_DIM, 2)


def head_table(value, head_index):
    return lax.dynamic_index_in_dim(value, head_index, 0, False).astype(jnp.float32)


def join_heads(value):
    return jnp.transpose(value, (1, 2, 0, 3)).reshape(
        value.shape[1], value.shape[2], value.shape[0] * value.shape[3]
    )


def column_terms(mix_table, row_tops, row_totals, grads_all, values, all_ok, local_ok, head_index):
    weights = column_probs(
        head_table(mix_table, head_index),
        row_tops[head_index],
        row_totals[head_index],
        all_ok,
        local_ok,
    )
    prob_grad = jnp.einsum(
        "bid,bjd->bji",
        head_slice(grads_all, head_index),
        head_slice(values, head_index),
        preferred_element_type=jnp.float32,
    )
    return (weights, prob_grad)


def column_first(mix_table, row_tops, row_totals, grads_all, values, all_ok, local_ok, head_ids):

    def first_pass(head_index):
        weights, prob_grad = column_terms(
            mix_table, row_tops, row_totals, grads_all, values, all_ok, local_ok, head_index
        )
        row_delta = jnp.sum(weights * prob_grad, axis=1)
        piece = jnp.einsum(
            "bji,bid->bjd",
            weights.astype(jnp.bfloat16),
            head_slice(grads_all, head_index),
            preferred_element_type=jnp.float32,
        )
        return (row_delta, piece)

    row_deltas, pieces = lax.map(first_pass, head_ids)
    return (row_deltas, join_heads(pieces))


def column_second(
    mix_table, row_tops, row_totals, grads_all, values, all_ok, local_ok, head_ids, row_deltas
):

    def second_pass(head_index):
        weights, prob_grad = column_terms(
            mix_table, row_tops, row_totals, grads_all, values, all_ok, local_ok, head_index
        )
        return jnp.sum(weights * (prob_grad - row_deltas[head_index][:, None, :]), axis=0)

    return lax.map(second_pass, head_ids)


def per_device(
    tokens, lengths, w_value, w_out, w_up, w_down, gain_mix, gain_ffn, mix_table, out_grad
):
    batch_size = tokens.shape[0]
    local_len = tokens.shape[1]
    full_len = local_len * lax.axis_size("seq")
    local_pos = lax.axis_index("seq") * local_len + jnp.arange(local_len)
    all_pos = jnp.arange(full_len)
    local_ok = local_pos[None, :] < lengths[:, None]
    all_ok = all_pos[None, :] < lengths[:, None]
    head_ids = jnp.arange(HEADS)
    w_value, w_out, w_up, w_down = (
        lax.all_gather(w_value, "seq", axis=0, tiled=True),
        lax.all_gather(w_out, "seq", axis=0, tiled=True),
        lax.all_gather(w_up, "seq", axis=0, tiled=True),
        lax.all_gather(w_down, "seq", axis=0, tiled=True),
    )
    inputs = tokens.astype(jnp.float32)
    normed, scale_mix = norm_forward(inputs, gain_mix)
    normed_low = normed.astype(jnp.bfloat16)
    values = jnp.dot(normed_low, w_value, preferred_element_type=jnp.float32).astype(jnp.bfloat16)

    def local_stats(head_index):
        return column_stats(head_table(mix_table, head_index), local_ok)

    row_tops, row_totals = lax.map(local_stats, head_ids)
    row_tops, row_totals = combined_all((row_tops, row_totals), "seq", combine_stats)

    def add_head(head_index, partial_value):
        weights = column_probs(
            head_table(mix_table, head_index),
            row_tops[head_index],
            row_totals[head_index],
            all_ok,
            local_ok,
        )
        piece = jnp.einsum(
            "bji,bjd->bid",
            weights.astype(jnp.bfloat16),
            head_slice(values, head_index),
            preferred_element_type=jnp.float32,
        )
        return lax.dynamic_update_slice_in_dim(partial_value, piece, head_index * HEAD_DIM, 2)

    partial_value = lax.fori_loop(
        0, HEADS, add_head, jnp.zeros((batch_size, full_len, D), jnp.float32)
    )
    mixed = lax.psum_scatter(partial_value, "seq", scatter_dimension=1, tiled=True)
    mixed_low = mixed.astype(jnp.bfloat16)
    middle = inputs + jnp.dot(mixed_low, w_out, preferred_element_type=jnp.float32)
    normed_ffn, scale_ffn = norm_forward(middle, gain_ffn)
    normed_ffn_low = normed_ffn.astype(jnp.bfloat16)
    hidden_pre = jnp.dot(normed_ffn_low, w_up, preferred_element_type=jnp.float32)
    hidden = jax.nn.gelu(hidden_pre).astype(jnp.bfloat16)
    output = (middle + jnp.dot(hidden, w_down, preferred_element_type=jnp.float32)).astype(
        jnp.bfloat16
    )
    down_weight_grad = jnp.einsum(
        "blf,bld->fd", hidden, out_grad, preferred_element_type=jnp.float32
    )
    hidden_grad = jnp.einsum("bld,fd->blf", out_grad, w_down, preferred_element_type=jnp.float32)
    _, gelu_back = jax.vjp(jax.nn.gelu, hidden_pre)
    pre_grad = gelu_back(hidden_grad)[0].astype(jnp.bfloat16)
    up_weight_grad = jnp.einsum(
        "bld,blf->df", normed_ffn_low, pre_grad, preferred_element_type=jnp.float32
    )
    ffn_normed_grad = jnp.einsum("blf,df->bld", pre_grad, w_up, preferred_element_type=jnp.float32)
    middle_norm_grad, ffn_gain_grad = norm_backward(middle, scale_ffn, gain_ffn, ffn_normed_grad)
    middle_grad = out_grad.astype(jnp.float32) + middle_norm_grad
    branch_grad = middle_grad.astype(jnp.bfloat16)
    out_weight_grad = jnp.einsum(
        "bld,ble->de", mixed_low, branch_grad, preferred_element_type=jnp.float32
    )
    mixed_grad = jnp.einsum(
        "ble,de->bld", branch_grad, w_out, preferred_element_type=jnp.float32
    ).astype(jnp.bfloat16)
    grads_all = lax.all_gather(mixed_grad, "seq", axis=1, tiled=True)
    row_deltas, value_grad = column_first(
        mix_table, row_tops, row_totals, grads_all, values, all_ok, local_ok, head_ids
    )
    row_deltas = lax.psum(row_deltas, "seq")
    table_cols = column_second(
        mix_table, row_tops, row_totals, grads_all, values, all_ok, local_ok, head_ids, row_deltas
    )
    value_low = value_grad.astype(jnp.bfloat16)
    value_weight_grad = jnp.einsum(
        "bld,ble->de", normed_low, value_low, preferred_element_type=jnp.float32
    )
    normed_grad = jnp.einsum("ble,de->bld", value_low, w_value, preferred_element_type=jnp.float32)
    input_norm_grad, mix_gain_grad = norm_backward(inputs, scale_mix, gain_mix, normed_grad)
    input_grad = middle_grad + input_norm_grad
    table_grad = lax.psum_scatter(table_cols, "dp", scatter_dimension=2, tiled=True)
    grad_value_w, grad_out_w, grad_up_w, grad_down_w, grad_gain_mix, grad_gain_ffn = (
        lax.psum_scatter(value_weight_grad, "seq", scatter_dimension=0, tiled=True),
        lax.psum_scatter(out_weight_grad, "seq", scatter_dimension=0, tiled=True),
        lax.psum_scatter(up_weight_grad, "seq", scatter_dimension=0, tiled=True),
        lax.psum_scatter(down_weight_grad, "seq", scatter_dimension=0, tiled=True),
        lax.psum_scatter(mix_gain_grad, "seq", scatter_dimension=0, tiled=True),
        lax.psum_scatter(ffn_gain_grad, "seq", scatter_dimension=0, tiled=True),
    )
    summed = lax.psum(
        (grad_value_w, grad_out_w, grad_up_w, grad_down_w, grad_gain_mix, grad_gain_ffn), "dp"
    )
    return (
        output,
        input_grad,
        summed[0],
        summed[1],
        summed[2],
        summed[3],
        summed[4],
        summed[5],
        table_grad,
    )


def solution(mesh):
    return jax.shard_map(
        per_device,
        mesh=mesh,
        in_specs=(
            P("dp", "seq", None),
            P("dp"),
            P("seq", None),
            P("seq", None),
            P("seq", None),
            P("seq", None),
            P(),
            P(),
            P(None, "seq", None),
            P("dp", "seq", None),
        ),
        out_specs=(
            P("dp", "seq", None),
            P("dp", "seq", None),
            P("seq", None),
            P("seq", None),
            P("seq", None),
            P("seq", None),
            P("seq"),
            P("seq"),
            P(None, "seq", "dp"),
        ),
        check_vma=False,
    )
```

profile of v0, /device:TPU:1, one launch (start us, length us, event | category | flops | bytes accessed | tf_op | source)
XLA Modules:
  0.0 1242.1 jit_solution(1580426381467598607)
XLA Ops:
  8.2 57.5 %while.67 = (s32[]{:T(128)}, f32[12,2,2048]{2,1,0:T(2,128)S(1)}, f32[12,2,2048]{2,1,0:T(2,128)S(1)}, s32[12]{0:T(128)S(1)}, bf16[12,64,2048]{2,1,0:T(8,128)(2,1)...) while((s32[]{:T(128)}, f32[12,2,2048]{2,1,0:T(2,128)S(1)}, ...), condition=%wide.region_3.4_spmd.clone, body=%wide.region_0.3_spmd.clone.sunk | while | flops 1695877 | bytes 1950499 | solution.py:142
  72.6 52.3 %all-gather.20.cloned.1.call-done = f32[384,2,2048]{2,1,0:T(2,128)} async-done(((f32[12,2,2048]{2,1,0:T(2,128)}), f32[384,2,2048]{2,1,0:T(2,128)}) %all-gather.20.cloned.1.call-update) | async-done | bytes 6291472 | tf_op jit(solution)/shard_map/all_gather | solution.py:15
  124.9 8.1 slice.22
  133.1 48.2 %all-gather.22.cloned.1.call-done = f32[384,2,2048]{2,1,0:T(2,128)} async-done(((f32[12,2,2048]{2,1,0:T(2,128)}), f32[384,2,2048]{2,1,0:T(2,128)}) %all-gather.22.cloned.1.call-update) | async-done | bytes 6291472 | tf_op jit(solution)/shard_map/all_gather | solution.py:15
  181.3 8.2 slice.23
  189.4 42.8 %while.66 = (s32[]{:T(128)}, f32[12,2,2048]{2,1,0:T(2,128)S(1)}, f32[12,2,2048]{2,1,0:T(2,128)S(1)}, f32[31,12,2,2048]{3,2,1,0:T(2,128)}, f32[31,12,2,2048]{3,2,1,0:T(2,128)}, /*index=5*/s32[]{:T(128)}) while((s32[]{:T(128)}, f32[12,2,2048]{2,1,0:T(2,128)S(1)}, f32[12,2,2048]{2,1,0:T(2,128)S(1)}, f32[31,12,2,2048]{3,2,1,0:T(2,128)}, ...), condition=%wide.region_5.6_spmd, body=%wide.region_4.5_spmd.sunk | while | flops 294914 | bytes 1179721 | solution.py:18
  232.3 6.1 broadcast_in_dim.97
  238.4 31.9 %while.68 = (s32[]{:T(128)}, f32[2,2048,768]{1,2,0:T(8,128)}, bf16[12,64,2048]{2,1,0:T(8,128)(2,1)}, f32[12,2,2048]{2,1,0:T(2,128)S(1)}, f32[12,2,2048]{2,1,0:T(...) while((s32[]{:T(128)}, f32[2,2048,768]{1,2,0:T(8,128)}, ...), condition=%wide.region_8.9_spmd.clone.clone, body=%wide.region_7.8_spmd.clone.clone.sunk | while | flops 35262596 | bytes 2504763 | solution.py:161
  270.4 19.4 %copy.38 = f32[2,2048,768]{2,0,1:T(2,128)} copy(f32[2,2048,768]{1,2,0:T(8,128)} %get-tuple-element.328) | data formatting | bytes 25165824 | tf_op jit(solution)/shard_map/while | solution.py:161
  289.8 185.0 %all-reduce.13 = bf16[2,2048,768]{2,0,1:T(2,128)(2,1)} all-reduce(f32[2,2048,768]{2,0,1:T(2,128)} %copy.38), channel_id=4, replica_groups=mesh['dp'=8,'seq'=32] {'seq'}, use_global_device_ids=true, to_apply=%region_9.10.clone | all-reduce | flops 3145728 | bytes 18874368
  478.2 3.2 fusion.55
  481.4 4.4 fusion.63
  485.8 2.4 multiply_reduce_fusion
  492.8 6.3 convolution_bitcast_fusion.2
  499.2 5.2 convolution_bitcast_fusion.1
  504.5 42.5 %all-gather.18.cloned.1.call-done = bf16[2,2048,768]{2,1,0:T(8,128)(2,1)} async-done(((bf16[2,64,768]{2,1,0:T(8,128)(2,1)}), bf16[2,2048,768]{2,1,0:T(8,128)(2,1)}) %all-gather.18.cloned.1.call-update) | async-done | bytes 6291472 | tf_op jit(solution)/shard_map/all_gather | solution.py:193
  547.0 8.8 copy.40
  555.8 97.7 %while.69 = (s32[]{:T(128)}, f32[12,2,2048]{2,1,0:T(2,128)S(1)}, bf16[12,2,64,64]{3,2,1,0:T(8,128)(2,1)}, s32[12]{0:T(128)S(1)}, bf16[12,64,2048]{2,1,0:T(8,128)...) while((s32[]{:T(128)}, f32[12,2,2048]{2,1,0:T(2,128)S(1)}, ...), condition=%wide.region_14.15_spmd.clone.clone, body=%wide.region_12.14_spmd.clone.clone.sunk | while | flops 70647944 | bytes 3181329 | solution.py:100
  568.4 2.1 fusion.126
  576.5 2.1 fusion.126
  584.7 2.1 fusion.126
  601.0 2.1 fusion.126
  609.1 2.1 fusion.126
  656.5 2.9 convolution_bitcast_fusion.4
  660.1 81.7 %reduce-scatter.10.cloned.1.call-done = f32[24,3072]{1,0:T(8,128)} async-done(((f32[768,3072]{1,0:T(8,128)}), f32[24,3072]{1,0:T(8,128)}) %reduce-scatter.10.cloned.1.call-update) | async-done | bytes 294928 | tf_op jit(solution)/shard_map/reduce_scatter | solution.py:212
  741.9 106.4 %reduce-scatter.12.cloned.1.call-done = f32[96,768]{1,0:T(8,128)} async-done(((f32[3072,768]{1,0:T(8,128)}), f32[96,768]{1,0:T(8,128)}) %reduce-scatter.12.cloned.1.call-update) | async-done | bytes 294928 | tf_op jit(solution)/shard_map/reduce_scatter | solution.py:213
  848.3 90.7 %reduce-scatter.6.cloned.1.call-done = f32[24,768]{1,0:T(8,128)} async-done(((f32[768,768]{1,0:T(8,128)}), f32[24,768]{1,0:T(8,128)}) %reduce-scatter.6.cloned.1.call-update) | async-done | bytes 73744 | tf_op jit(solution)/shard_map/reduce_scatter | solution.py:210
  939.3 113.7 %all-reduce.10.cloned.1.call-done = f32[12,2,2048]{2,1,0:T(2,128)} async-done(((f32[12,2,2048]{2,1,0:T(2,128)}), f32[12,2,2048]{2,1,0:T(2,128)}) %all-reduce.10.cloned.1.call-update) | async-done | bytes 196624 | tf_op jit(solution)/shard_map/psum | solution.py:197
  1053.0 91.4 %while.70 = (s32[]{:T(128)}, f32[12,64,2048]{2,1,0:T(8,128)}, s32[12]{0:T(128)S(1)}, bf16[12,64,2048]{2,1,0:T(8,128)(2,1)}, f32[12,2,2048]{2,1,0:T(2,128)S(1)}, ...) while((s32[]{:T(128)}, f32[12,64,2048]{2,1,0:T(8,128)}, ...), condition=%wide.region_33.34_spmd.clone.clone, body=%wide.region_31.33_spmd.clone.clone.sunk | while | flops 35655816 | bytes 3598605 | solution.py:114
  1145.0 4.2 fusion.76
  1149.8 64.0 %all-reduce.3 = (f32[768]{0:T(1024)S(1)}, f32[768]{0:T(1024)S(1)}) all-reduce(f32[768]{0:T(1024)S(1)} %get-tuple-element.631, f32[768]{0:T(1024)S(1)} %copy-done.16), channel_id=9, replica_groups=mesh['dp'=8,'seq'=32] {'seq'}, use_global_device_ids=true, to_apply=%region_25.26.clone | all-reduce | flops 1536 | bytes 12288
  1214.0 14.2 %all-reduce.4 = (f32[24]{0:T(128)}, f32[24]{0:T(128)}) all-reduce(f32[24]{0:T(128)S(1)} %dynamic-slice.3, f32[24]{0:T(128)S(1)} %dynamic-slice.5), channel_id=1, replica_groups=mesh['dp'=8,'seq'=32] {'dp'}, use_global_device_ids=true, to_apply=%region_26.27 | all-reduce | flops 48 | bytes 384 | tf_op jit(solution)/shard_map/psum | solution.py:217
  (466 shorter events, 250.9 us)
Async XLA Ops:
  7.2 63.8 %all-gather.10.cloned.1.call-start = ((), (), s32[]{:S(2)}) async-start(), calls=%async_computation.5 | async-start | bytes 1216512 | tf_op jit(solution)/shard_map/all_gather | solution.py:129
  7.9 117.0 %all-gather.20.cloned.1.call-start = ((), (), s32[]{:S(2)}) async-start(), calls=%async_computation.16 | async-start | bytes 6488064 | tf_op jit(solution)/shard_map/all_gather | solution.py:15
  8.1 60.8 %copy-start.1 = (bf16[2,64,768]{2,1,0:T(8,128)(2,1)S(1)}, bf16[2,64,768]{2,1,0:T(8,128)(2,1)}, u32[]{:S(2)}) copy-start(bf16[2,64,768]{2,1,0:T(8,128)(2,1)} %param.20) | copy-start | bytes 589828
  8.1 61.5 %copy-start.19 = (u32[256]{0:T(256)S(1)}, u32[256]{0:T(256)}, u32[]{:S(2)}) copy-start(u32[256]{0:T(256)} %constant.153) | copy-start | bytes 3076
  8.1 62.8 %copy-start.13 = (f32[768]{0:T(1024)S(1)}, f32[768]{0:T(1024)}, u32[]{:S(2)}) copy-start(f32[768]{0:T(1024)} %param.26) | copy-start | bytes 9220
  66.4 114.8 %all-gather.22.cloned.1.call-start = ((), (), s32[]{:S(2)}) async-start(), calls=%async_computation.17 | async-start | bytes 6488064 | tf_op jit(solution)/shard_map/all_gather | solution.py:15
  67.2 408.7 %all-gather.12.cloned.1.call-start = ((), (), s32[]{:S(2)}) async-start(), calls=%async_computation.6 | async-start | bytes 1216512 | tf_op jit(solution)/shard_map/all_gather | solution.py:130
  67.7 410.4 %all-gather.14.cloned.1.call-start = ((), (), s32[]{:S(2)}) async-start(), calls=%async_computation.7 | async-start | bytes 4866048 | tf_op jit(solution)/shard_map/all_gather | solution.py:131
  68.3 413.1 %all-gather.16.cloned.1.call-start = ((), (), s32[]{:S(2)}) async-start(), calls=%async_computation.8 | async-start | bytes 4866048 | tf_op jit(solution)/shard_map/all_gather | solution.py:132
  68.9 478.1 %all-gather.18.cloned.1.call-start = ((), (), s32[]{:S(2)}) async-start(), calls=%async_computation.9 | async-start | bytes 6488064 | tf_op jit(solution)/shard_map/all_gather | solution.py:193
  69.7 63.4 %copy-start.14 = (f32[2,64]{1,0:T(2,128)}, f32[2,64]{1,0:T(2,128)S(1)}, u32[]{:S(2)}) copy-start(f32[2,64]{1,0:T(2,128)S(1)} %get-tuple-element.736) | copy-start | bytes 1540
  133.1 56.4 %slice-start = ((f32[384,2,2048]{2,1,0:T(2,128)}), f32[12,2,2048]{2,1,0:T(2,128)S(1)}, s32[]{:S(2)}) async-start(f32[384,2,2048]{2,1,0:T(2,128)} %all-gather.20.cloned.1.call-done), calls=%async_computation.19 | async-start | bytes 393216 | tf_op jit(solution)/shard_map/slice | solution.py:16
  181.3 8.2 slice-start.1
  232.3 6.1 copy-start.12
  270.4 19.4 %copy-start.20 = (s32[64]{0:T(128)}, s32[64]{0:T(128)S(1)}, u32[]{:S(2)}) copy-start(s32[64]{0:T(128)S(1)} %get-tuple-element.1291) | copy-start | bytes 772
  474.8 3.4 copy-start.10
  478.2 3.3 copy-start.9
  481.4 4.4 copy-start
  485.8 2.4 copy-start.4
  490.8 169.4 %reduce-scatter.8.cloned.1.call-start = ((), (), s32[]{:S(2)}) async-start(), calls=%async_computation.11 | async-start | bytes 2433024 | tf_op jit(solution)/shard_map/reduce_scatter | solution.py:211
  492.8 249.1 %reduce-scatter.10.cloned.1.call-start = ((), (), s32[]{:S(2)}) async-start(), calls=%async_computation.12 | async-start | bytes 9732096 | tf_op jit(solution)/shard_map/reduce_scatter | solution.py:212
  499.1 349.2 %reduce-scatter.12.cloned.1.call-start = ((), (), s32[]{:S(2)}) async-start(), calls=%async_computation.13 | async-start | bytes 9732096 | tf_op jit(solution)/shard_map/reduce_scatter | solution.py:213
  504.4 51.4 %copy-start.21 = (s32[64]{0:T(128)S(1)}, s32[64]{0:T(128)}, u32[]{:S(2)}) copy-start(s32[64]{0:T(128)} %copy-done.20) | copy-start | bytes 772
  504.4 434.6 %reduce-scatter.6.cloned.1.call-start = ((), (), s32[]{:S(2)}) async-start(), calls=%async_computation.10 | async-start | bytes 2433024 | tf_op jit(solution)/shard_map/reduce_scatter | solution.py:210
  653.5 3.0 copy-start.15
  659.4 393.5 %copy-start.22 = (s32[64]{0:T(128)S(1)}, s32[64]{0:T(128)}, u32[]{:S(2)}) copy-start(s32[64]{0:T(128)} %copy-done.20) | copy-start | bytes 772
  659.5 393.5 %all-reduce.10.cloned.1.call-start = ((), (), s32[]{:S(2)}) async-start(), calls=%async_computation.14 | async-start | bytes 393216 | tf_op jit(solution)/shard_map/psum | solution.py:197
  660.0 569.1 %all-reduce.12.cloned.1.call-start = ((), (), s32[]{:S(2)}) async-start(), calls=%async_computation.18 | async-start | bytes 1474560 | tf_op jit(solution)/shard_map/psum | solution.py:217
  939.0 290.1 %reduce-scatter.14.cloned.1.call-start = ((), (), s32[]{:S(2)}) async-start(), calls=%async_computation.15 | async-start | bytes 7077888 | tf_op jit(solution)/shard_map/reduce_scatter | solution.py:208
  1145.0 4.2 copy-start.2
  1145.0 4.2 copy-start.5
  1149.2 79.0 %copy-start.17 = (f32[2,64]{1,0:T(2,128)S(1)}, f32[2,64]{1,0:T(2,128)}, u32[]{:S(2)}) copy-start(f32[2,64]{1,0:T(2,128)} %get-tuple-element.735) | copy-start | bytes 1540
  (7 other events, 7.2 us)
Sparse Core Ops, SparseCore 0:
  10.6 52.2 all-gather.9
  66.5 58.3 all-gather.19
  128.0 53.1 all-gather.21
  183.7 47.0 all-gather.11
  233.2 51.2 all-gather.13
  286.8 63.6 all-gather.15
  490.9 56.0 all-gather.17
  550.8 83.8 reduce-scatter.7
  639.3 102.4 reduce-scatter.9
  745.8 102.5 reduce-scatter.11
  852.7 86.2 reduce-scatter.5
  942.7 110.2 all-reduce.9
  1055.8 70.0 all-reduce.11
  1144.5 74.6 reduce-scatter.13
where the time goes:
time: 1250 us; the launch traced here: 1240 us
  waiting for transfers between devices  539 us (43%)
  blocking collectives  263 us (21%)
  matrix products  119 us (10%)
  other arithmetic  113 us (9%)
  local copies, waits for them, and re-layouts  105 us (8%)
  loops' own time  87.2 us (7%)
  between operations  15.5 us (1%)
    unnamed x2, blocking collectives  249 us
    psum x1, waiting for transfers between devices, per_device(): row_deltas = lax.psum(row_deltas, 'seq')  114 us
    reduce_scatter x1, waiting for transfers between devices, per_device(): lax.psum_scatter(down_weight_grad, 'seq', scatter_dimension=0, tiled=True)  106 us
    all_gather x2, waiting for transfers between devices, combined_all(): pieces = jax.tree.map(lambda part: lax.all_gather(part, axis), value)  101 us
    reduce_scatter x1, waiting for transfers between devices, per_device(): lax.psum_scatter(value_weight_grad, 'seq', scatter_dimension=0, tiled=True)  90.7 us
    reduce_scatter x1, waiting for transfers between devices, per_device(): lax.psum_scatter(up_weight_grad, 'seq', scatter_dimension=0, tiled=True)  81.7 us
    add x31, other arithmetic, combine_stats(): first[1] * jnp.exp(first[0] - row_top)  42.5 us
    all_gather x1, waiting for transfers between devices, per_device(): grads_all = lax.all_gather(mixed_grad, 'seq', axis=1, tiled=True)  42.5 us
  transfers between devices with their start and end apart: 14, of which 7 were waited for; matrix products, arithmetic and copies ran while one was open for 26% of the time, Pallas kernels for 0%

commit v1 on v0

v1 whole, which is shorter than its diff:
```python
import jax
import jax.numpy as jnp
from jax import lax
from jax.experimental import pallas as pl
from jax.experimental.pallas import tpu as pltpu
from jax.sharding import PartitionSpec as P

D = 768
HALF = 384
HEADS = 12
HH = 6
EPS = 1e-06
MESH = pl.DeviceIdType.MESH
BF = jnp.bfloat16
F32 = jnp.float32
OFFS = (1, 3, 2)
ROWS = 144
GELU_C = 0.7978845608028654
GELU_A = 0.044715


def here():
    s = lax.axis_index("seq")
    return lax.axis_index("dp"), s // 8, (s // 2) % 4, s % 2


def at(z, x, y, c):
    return (z, (x * 4 + y) * 2 + c)


def remote(src, dst, sems, idx, device):
    return pltpu.make_async_remote_copy(
        src_ref=src,
        dst_ref=dst,
        send_sem=sems.at[(0,) + idx],
        recv_sem=sems.at[(1,) + idx],
        device_id=device,
        device_id_type=MESH,
    )


def along(first, k):
    z, x, y, c = here()
    if first == "x":
        return at(z, lax.rem(x + k, 4), y, c)
    return at(z, x, lax.rem(y + k, 4), c)


OTHER = {"x": "y", "y": "x"}


def own_at(first):
    _, x, y, _ = here()
    return x if first == "x" else y


def gather_one(buf, first, sems):
    _, x, y, _ = here()
    return [
        remote(buf.at[x, y], buf.at[x, y], sems, (0, i), along(first, k))
        for i, k in enumerate(OFFS)
    ]


def gather_two(buf, first, sems):
    _, x, y, _ = here()
    view = buf.at[:, y] if first == "x" else buf.at[x]
    return [
        remote(view, view, sems, (1, i), along(OTHER[first], k)) for i, k in enumerate(OFFS)
    ]


def scatter_one(src, rcv, first, sems):
    mine = own_at(first)
    out = []
    for i, k in enumerate(OFFS):
        to = lax.rem(mine + k, 4)
        part = src.at[to] if first == "x" else src.at[:, to]
        out.append(remote(part, rcv.at[mine], sems, (0, i), along(first, k)))
    return out


def scatter_sum(src, rcv, mid, first):
    mine = own_at(first)
    for j in range(4):
        own = src[mine, j] if first == "x" else src[j, mine]
        total = own.astype(F32)
        for k in OFFS:
            total = total + rcv[lax.rem(mine + k, 4), j].astype(F32)
        mid[j] = total.astype(BF)


def scatter_two(mid, rcv, first, sems):
    second = OTHER[first]
    mine = own_at(second)
    return [
        remote(mid.at[lax.rem(mine + k, 4)], rcv.at[mine], sems, (1, i), along(second, k))
        for i, k in enumerate(OFFS)
    ]


def scatter_end(mid, rcv, first):
    mine = own_at(OTHER[first])
    total = mid[mine].astype(F32)
    for k in OFFS:
        total = total + rcv[lax.rem(mine + k, 4)].astype(F32)
    return total


def start(copies):
    for copy in copies:
        copy.start()


def wait_recv(copies):
    for copy in copies:
        copy.wait_recv()


def wait_send(copies):
    for copy in copies:
        copy.wait_send()


def signal(device):
    pl.semaphore_signal(
        pltpu.get_barrier_semaphore(), inc=1, device_id=device, device_id_type=MESH
    )


def meet(with_z):
    z, x, y, c = here()
    count = 0
    for k in range(1, 4):
        signal(at(z, lax.rem(x + k, 4), y, c))
        signal(at(z, x, lax.rem(y + k, 4), c))
        count += 2
    signal(at(z, x, y, 1 - c))
    count += 1
    if with_z:
        for k in range(1, 8):
            signal(at(lax.rem(z + k, 8), x, y, c))
            count += 1
    pl.semaphore_wait(pltpu.get_barrier_semaphore(), count)


def dot(a, b):
    return jnp.dot(a, b, preferred_element_type=F32)


def dot_nt(a, b):
    return lax.dot_general(a, b, (((1,), (1,)), ((), ())), preferred_element_type=F32)


def flip(a):
    return jnp.transpose(a)


def rms_of(v):
    return lax.rsqrt(jnp.mean(v * v, axis=-1, keepdims=True) + EPS)


def front(
    tokens, out_grad, pre, w_down, table, mask, gain_mix, gain_ffn,
    out, mgrad, gch, vals, e_out, normed, tok_o, wv_o, dwu, dwd, dwo, gain_o,
    pre_s, tok, og, tab, wv, wo_all, wu0, wu1, wd0, wd1,
    ux, uy, rx, ry, mx, my, rx2, ry2, mt, rr, mix, vt, middle, nf, hid, pgr, act, part, part_r, fng, fng_r,
    s_sib, s_ag, s_u, s_loc,
):
    z, x, y, c = here()
    sib = at(z, x, y, 1 - c)
    wo = wo_all.at[c]
    meet(False)

    def to_sib(src, dst, i):
        return remote(src, dst, s_sib, (i,), sib)

    swap_pre = to_sib(pre.at[1 - c], pre_s.at[c], 0)
    swap_tok = to_sib(tokens, tok.at[:, c], 1)
    swap_tab = to_sib(table.at[pl.ds(6 * (1 - c), 6)], tab.at[:, c], 2)
    swap_og = to_sib(out_grad, og.at[:, c], 3)
    own_tab = pltpu.make_async_copy(table.at[pl.ds(6 * c, 6)], tab.at[:, c], s_loc)
    start([swap_pre, swap_tok, swap_tab, own_tab, swap_og])
    pre_s[c] = pre[c]
    tok[:, c] = tokens[...]
    og[:, c] = out_grad[...]
    wd0[x, y] = w_down[0:48]
    wd1[x, y] = w_down[48:96]
    swap_pre.wait_recv()
    shard = pre_s[...].reshape(48, 2304).astype(BF)
    wv[x, y] = shard[:, 0:HALF]
    wo[x, y] = shard[:, HALF:D]
    wu0[x, y] = shard[:, D : 2 * D]
    wu1[x, y] = shard[:, 2 * D : 3 * D]
    bufs = ((wv, "x"), (wo, "y"), (wu0, "x"), (wu1, "y"), (wd0, "x"), (wd1, "y"))
    g1 = [gather_one(buf, first, s_ag.at[:, i]) for i, (buf, first) in enumerate(bufs)]
    g2 = [gather_two(buf, first, s_ag.at[:, i]) for i, (buf, first) in enumerate(bufs)]
    for i in range(6):
        start(g1[i])
    swap_tok.wait_recv()
    values = tok[...].reshape(256, D).astype(F32)
    normed[...] = (values * rms_of(values) * gain_mix[...]).astype(BF)
    tok_o[...] = tok[...]
    for i in range(2):
        wait_recv(g1[i])
        start(g2[i])
    swap_tab.wait_recv()
    own_tab.wait()

    def exps(h, carry):
        e_out[h] = jnp.exp(tab[h].reshape(128, 2048).astype(F32)).astype(BF)
        return carry

    lax.fori_loop(0, HH, exps, 0)
    wait_recv(g2[0])
    wv_o[...] = wv[...].reshape(D, HALF)
    v = dot(normed[...], wv_o[...]).astype(BF).astype(F32)
    lane_mask = jnp.concatenate([mask[0:1], mask[1:2]], axis=1)
    vall = flip(v) * lane_mask
    ones = jnp.concatenate([mask[...], jnp.zeros((8, 128), F32)], axis=0)
    for h in range(HH):
        block = jnp.concatenate(
            [vall[64 * h : 64 * h + 64, 0:128], vall[64 * h : 64 * h + 64, 128:256]], axis=0
        )
        vt[h] = jnp.concatenate([block, ones], axis=0).astype(BF)
        vals[h] = flip(block).astype(BF)

    s1x = scatter_one(ux, rx, "x", s_u.at[:, 0])
    s1y = scatter_one(uy, ry, "y", s_u.at[:, 1])
    for i, k in enumerate(OFFS + (0,)):
        xx = lax.rem(x + k, 4)
        yy = lax.rem(y + k, 4)

        def head_x(h, carry, xx=xx):
            u = dot(vt[h], e_out[h, :, pl.ds(pl.multiple_of(512 * xx, 512), 512)])
            for j in range(4):
                ux[xx, j, h] = u[:, 128 * j : 128 * j + 128].astype(BF)
            return carry

        def head_y(h, carry, yy=yy):
            for j in range(4):
                cols = pl.ds(pl.multiple_of(512 * j + 128 * yy, 128), 128)
                uy[j, yy, h] = dot(vt[h + 3], e_out[h + 3, :, cols]).astype(BF)
            return carry

        lax.fori_loop(0, 3, head_x, 0)
        if i < 3:
            s1x[i].start()
        lax.fori_loop(0, 3, head_y, 0)
        if i < 3:
            s1y[i].start()
    for i in (2, 3):
        wait_recv(g1[i])
        start(g2[i])
    wait_recv(g2[1])
    swap_wo = to_sib(wo, wo, 4)
    swap_wo.start()
    s2x = scatter_two(mx, rx2, "x", s_u.at[:, 0])
    s2y = scatter_two(my, ry2, "y", s_u.at[:, 1])
    wait_recv(s1x)
    scatter_sum(ux, rx, mx, "x")
    start(s2x)
    wait_recv(s1y)
    scatter_sum(uy, ry, my, "y")
    start(s2y)
    for i in (4, 5):
        wait_recv(g1[i])
        start(g2[i])

    for half, (copies, mid, rcv, first) in enumerate(((s2x, mx, rx2, "x"), (s2y, my, ry2, "y"))):
        wait_recv(copies)
        total = scatter_end(mid, rcv, first)
        for hh in range(3):
            h = half * 3 + hh
            for b in range(2):
                r = mask[b : b + 1] / total[hh, 128 + b : 129 + b]
                rr[b, h : h + 1] = r
                mt[b, 64 * h : 64 * h + 64] = total[hh, 64 * b : 64 * b + 64] * r
    for b in range(2):
        mix[c, b] = flip(mt[b]).astype(BF)
    swap_mix = to_sib(mix.at[c], mix.at[c], 5)
    swap_mix.start()
    swap_wo.wait_recv()
    swap_mix.wait_recv()
    mixed = [mix[i].reshape(256, HALF) for i in range(2)]
    for cc in range(2):
        w = wo_all[cc].reshape(D, HALF)
        cols = slice(HALF * cc, HALF * cc + HALF)
        middle[:, cols] = (
            tok[...].reshape(256, D)[:, cols].astype(F32)
            + dot(mixed[0], w[0:HALF])
            + dot(mixed[1], w[HALF:D])
        )
    mid_v = middle[...]
    rms = rms_of(mid_v)
    nf[...] = (mid_v * rms * gain_ffn[...]).astype(BF)
    nft = flip(nf[...])
    swap_og.wait_recv()
    grad = og[...].reshape(256, D)
    for hf, (up, down) in enumerate(((wu0, wd0), (wu1, wd1))):
        wait_recv(g2[2 + hf])
        hp = dot(nf[...], up[...].reshape(D, D))
        t = jnp.tanh(GELU_C * (hp + GELU_A * hp * hp * hp))
        hid[hf] = (0.5 * hp * (1.0 + t)).astype(BF)
        act[hf] = 0.5 * (1.0 + t) + 0.5 * hp * (1.0 - t * t) * (
            GELU_C * (1.0 + 3.0 * GELU_A * hp * hp)
        )
    for hf, (up, down) in enumerate(((wu0, wd0), (wu1, wd1))):
        wait_recv(g2[4 + hf])
        w = down[...].reshape(D, D)
        pgr[hf] = (act[hf] * dot_nt(grad, w)).astype(BF)
        more = dot_nt(pgr[hf], up[...].reshape(D, D)).reshape(2, 2, 64, D)
        fng[...] = more if hf == 0 else fng[...] + more
    swap_fng = to_sib(fng, fng_r, 6)
    swap_fng.start()
    for hf, (up, down) in enumerate(((wu0, wd0), (wu1, wd1))):
        more = dot(hid[hf], down[...].reshape(D, D)).reshape(2, 2, 64, D)
        part[...] = more if hf == 0 else part[...] + more
    swap_part = to_sib(part.at[:, 1 - c], part_r, 7)
    swap_part.start()
    for hf in range(2):
        dwu[hf] = dot(nft, pgr[hf]).astype(BF).reshape(4, 4, 48, D)
        dwd[hf] = dot(flip(hid[hf]), grad).astype(BF).reshape(4, 4, 48, D)
    swap_fng.wait_recv()
    full = (fng[...] + fng_r[...]).reshape(256, D)
    mid_v = middle[...]
    rms = rms_of(mid_v)
    gain_o[...] = jnp.sum(full * mid_v * rms, axis=0, keepdims=True)
    weighted = full * gain_ffn[...]
    inner = jnp.mean(weighted * mid_v, axis=-1, keepdims=True)
    mg = grad.astype(F32) + rms * weighted - mid_v * (rms * rms * rms) * inner
    swap_fng.wait_send()
    fng[...] = mg.reshape(2, 2, 64, D)
    bg = mg.astype(BF)
    nf[...] = bg
    mgrad[...] = fng[:, c]
    swap_part.wait_recv()
    fng_r[...] = middle[...].reshape(2, 2, 64, D)
    out[...] = (fng_r[:, c] + (part[:, c] + part_r[...])).astype(BF)
    cols = pl.ds(pl.multiple_of(HALF * c, 128), HALF)
    bg_c = nf[:, cols]
    for i in range(2):
        dwo[i] = dot(flip(mixed[i]), bg_c).astype(BF).reshape(2, 4, 48, HALF)
    xg = jnp.zeros((256, HALF), F32)
    for cc in range(2):
        w = wo_all[cc, pl.ds(2 * c, 2)].reshape(HALF, HALF)
        xg = xg + dot_nt(bg[:, HALF * cc : HALF * cc + HALF], w)
    for b in range(2):
        xgt = flip(xg[128 * b : 128 * b + 128])
        for h in range(HH):
            rows = xgt[64 * h : 64 * h + 64]
            r = rr[b, h : h + 1]
            delta = jnp.sum(rows * mt[b, 64 * h : 64 * h + 64], axis=0, keepdims=True) * r
            gch[h, 64 * b : 64 * b + 64] = (rows * r).astype(BF)
            mt[b, 64 * h : 64 * h + 1] = delta
    for h in range(HH):
        d0 = mt[0, 64 * h : 64 * h + 1]
        d1 = mt[1, 64 * h : 64 * h + 1]
        h0 = d0.astype(BF).astype(F32)
        h1 = d1.astype(BF).astype(F32)
        gch[h, 128:144] = jnp.concatenate(
            [h0, h1, d0 - h0, d1 - h1, jnp.zeros((12, 128), F32)], axis=0
        ).astype(BF)
    swap_pre.wait_send()
    swap_tok.wait_send()
    swap_tab.wait_send()
    swap_og.wait_send()
    swap_wo.wait_send()
    swap_mix.wait_send()
    swap_part.wait_send()
    for group in g1 + g2 + [s1x, s1y, s2x, s2y]:
        wait_send(group)


def back(
    gch, vals, e, mask, mask_cols, normed, tok, wv, dwu, dwd, dwo, gain_f, gain_mix, mgrad,
    tg, input_grad, res,
    gx, gy, ru, ru2, mu, rl, rl2, ml, dwv, gs, gr, up_s, up_r, dn_s, dn_r, tgf, tg_r, vgt, ng, ng_r, ig, sums, zr, zs, zf,
    s_g, s_w, s_l, s_gain, s_up, s_dn, s_sib, s_z,
):
    z, x, y, c = here()
    sib = at(z, x, y, 1 - c)
    up = at(lax.rem(z + 1, 8), x, y, c)
    down = at(lax.rem(z + 7, 8), x, y, c)
    meet(True)
    gx[x, y] = gch[0:3]
    gy[x, y] = gch[3:6]
    a1x = gather_one(gx, "x", s_g.at[:, 0])
    a1y = gather_one(gy, "y", s_g.at[:, 1])
    a2x = gather_two(gx, "x", s_g.at[:, 0])
    a2y = gather_two(gy, "y", s_g.at[:, 1])
    start(a1x)
    start(a1y)
    wait_recv(a1x)
    start(a2x)
    wait_recv(a1y)
    start(a2y)
    lots = ((dwu.at[0], "x"), (dwu.at[1], "y"), (dwd.at[0], "x"), (dwd.at[1], "y"))
    w1 = [scatter_one(src, ru.at[i], first, s_w.at[:, i]) for i, (src, first) in enumerate(lots)]
    w2 = [scatter_two(mu.at[i], ru2.at[i], first, s_w.at[:, i]) for i, (_, first) in enumerate(lots)]
    l1o = scatter_one(dwo, rl.at[0], "x", s_l.at[:, 0])
    for group in w1:
        start(group)
    start(l1o)
    wait_recv(a2x)
    wait_recv(a2y)

    def table_part(d, hf):
        buf = gx if hf == 0 else gy
        out = []
        for hh in range(3):
            h = 3 * hf + hh
            row = []
            for i in range(2):
                k = 2 * d + i
                g = buf[k // 4, lax.rem(k, 4), hh]
                cols = pl.ds(pl.multiple_of(256 * d + 128 * i, 128), 128)
                extra = g[128:144].astype(F32)
                s = dot(vals[h], g[0:128])
                s = s - mask_cols[0] * (extra[0:1] + extra[2:3])
                s = s - mask_cols[1] * (extra[1:2] + extra[3:4])
                row.append(s * e[h, :, cols].astype(F32))
            out.append(jnp.concatenate(row, axis=1))
        return out

    def ring(send, recv, sems, t, hf, device):
        return remote(send.at[t, hf], recv.at[t, hf], sems, (t, hf), device)

    ups = [[ring(up_s, up_r, s_up, t, hf, up) for hf in range(2)] for t in range(4)]
    dns = [[ring(dn_s, dn_r, s_dn, t, hf, down) for hf in range(2)] for t in range(3)]

    def step(t):
        for copies, send, recv, d in (
            (ups, up_s, up_r, lax.rem(z + 4 - t, 8)),
            (dns, dn_s, dn_r, lax.rem(z + 5 + t, 8)),
        ):
            if t == 3 and copies is dns:
                continue
            for hf in range(2):
                if t > 0:
                    copies[t - 1][hf].wait_recv()
                parts = table_part(d, hf)
                for hh in range(3):
                    p = parts[hh]
                    if t > 0:
                        p = p + recv[t - 1, hf, hh].astype(F32)
                    send[t, hf, hh] = p.astype(BF)
                copies[t][hf].start()

    step(0)
    for h in range(HH):
        buf = gx if h < 3 else gy
        total = jnp.zeros((128, 128), F32)
        for k in range(16):
            total = total + dot_nt(buf[k // 4, k % 4, h % 3, 0:128], e[h, :, 128 * k : 128 * k + 128])
        for b in range(2):
            vgt[b, 64 * h : 64 * h + 64] = total[64 * b : 64 * b + 64] * mask[b : b + 1]
    vg = jnp.concatenate([flip(vgt[b]) for b in range(2)], axis=0).astype(BF)
    dwv[...] = dot(flip(normed[...]), vg).astype(BF).reshape(4, 4, 48, HALF)
    l1v = scatter_one(dwv, rl.at[1], "y", s_l.at[:, 1])
    start(l1v)
    part = dot_nt(vg, wv[...])
    ig[...] = part
    swap_ng = remote(ig, ng_r, s_sib, (0,), sib)
    swap_ng.start()
    step(1)
    swap_ng.wait_recv()
    full = ig[...] + ng_r[...]
    xv = tok[...].reshape(256, D).astype(F32)
    rms = rms_of(xv)
    gain_m = jnp.sum(full * xv * rms, axis=0, keepdims=True)
    weighted = full * gain_mix[...]
    inner = jnp.mean(weighted * xv, axis=-1, keepdims=True)
    ng[...] = (rms * weighted - xv * (rms * rms * rms) * inner).reshape(2, 2 * 64, D)
    input_grad[...] = mgrad[...] + ng[:, pl.ds(pl.multiple_of(64 * c, 64), 64)]
    gains = jnp.concatenate([gain_f[...], gain_m], axis=0)
    high = gains.astype(BF).astype(F32)
    gs[...] = jnp.concatenate([high, gains - high, jnp.zeros((12, D), F32)], axis=0).astype(BF)
    gr[x, y] = gs[...]
    gain1 = gather_one(gr, "x", s_gain)
    gain2 = gather_two(gr, "x", s_gain)
    start(gain1)
    for i, (src, first) in enumerate(lots):
        wait_recv(w1[i])
        scatter_sum(src, ru.at[i], mu.at[i], first)
        start(w2[i])
    step(2)
    l2 = [
        scatter_two(ml.at[0], rl2.at[0], "x", s_l.at[:, 0]),
        scatter_two(ml.at[1], rl2.at[1], "y", s_l.at[:, 1]),
    ]
    wait_recv(l1o)
    scatter_sum(dwo, rl.at[0], ml.at[0], "x")
    start(l2[0])
    wait_recv(l1v)
    scatter_sum(dwv, rl.at[1], ml.at[1], "y")
    start(l2[1])
    wait_recv(gain1)
    start(gain2)
    step(3)
    for i, (src, first) in enumerate(lots):
        wait_recv(w2[i])
        sums[48 * i : 48 * i + 48] = scatter_end(mu.at[i], ru2.at[i], first).astype(BF)
    wait_recv(l2[0])
    sums[192:240, 0:HALF] = scatter_end(ml.at[0], rl2.at[0], "x").astype(BF)
    wait_recv(l2[1])
    sums[192:240, HALF:D] = scatter_end(ml.at[1], rl2.at[1], "y").astype(BF)
    wait_recv(gain2)
    gsum = gr[...].reshape(16, 16, D).astype(F32)
    gtot = jnp.sum(gsum, axis=0)
    gains = gtot[0:2] + gtot[2:4]
    high = gains.astype(BF).astype(F32)
    sums[240:256] = jnp.concatenate([high, gains - high, jnp.zeros((12, D), F32)], axis=0).astype(BF)
    z1 = [
        remote(
            sums.at[pl.ds(pl.multiple_of(32 * lax.rem(z + k, 8), 32), 32)],
            zr.at[z], s_z, (0, k), at(lax.rem(z + k, 8), x, y, c),
        )
        for k in range(1, 8)
    ]
    start(z1)
    own = table_part(z, 0) + table_part(z, 1)
    for hf in range(2):
        ups[3][hf].wait_recv()
        dns[2][hf].wait_recv()
        for hh in range(3):
            p = own[3 * hf + hh] + (
                up_r[3, hf, hh].astype(F32) + dn_r[2, hf, hh].astype(F32)
            )
            tgf[3 * hf + hh] = p.reshape(2, 64, 256)
    swap_tg = remote(tgf.at[:, 1 - c], tg_r, s_sib, (1,), sib)
    swap_tg.start()
    mine = sums[pl.ds(pl.multiple_of(32 * z, 32), 32)].astype(F32)
    wait_recv(z1)
    for k in range(1, 8):
        mine = mine + zr[lax.rem(z + k, 8)].astype(F32)
    zs[z] = mine.astype(BF)
    z2 = [
        remote(zs.at[z], zs.at[z], s_z, (1, k), at(lax.rem(z + k, 8), x, y, c))
        for k in range(1, 8)
    ]
    start(z2)
    tg[c] = tgf[:, c]
    swap_tg.wait_recv()
    tg[1 - c] = tg_r[...]
    wait_recv(z2)
    zf[c] = zs[...]
    swap_res = remote(zs, zf.at[c], s_sib, (2,), sib)
    swap_res.start()
    swap_res.wait_recv()
    res[...] = zf[...].reshape(2, 256, D)
    for group in [a1x, a1y, a2x, a2y, l1o, l1v, gain1, gain2, z1, z2] + w1 + w2 + l2 + ups + dns:
        wait_send(group)
    swap_ng.wait_send()
    swap_tg.wait_send()
    swap_res.wait_send()


def vmem(shape, kind=BF):
    return pltpu.VMEM(shape, kind)


def dma(*shape):
    return pltpu.SemaphoreType.DMA(shape)


IN_VMEM = pl.BlockSpec(memory_space=pltpu.VMEM)


def per_device(tokens, lengths, w_value, w_out, w_up, w_down, gain_mix, gain_ffn, mix_table, out_grad):
    s = lax.axis_index("seq")
    c = s % 2
    positions = (s // 2) * 128 + jnp.arange(128)
    ok = (positions[None, :] < lengths[:, None]).astype(F32)
    mask = jnp.concatenate([ok, jnp.zeros((6, 128), F32)], axis=0)
    mask_cols = jnp.broadcast_to(ok[:, :, None], (2, 128, 128))
    pre = jnp.concatenate(
        [
            w_value.reshape(24, 2, HALF).transpose(1, 0, 2),
            w_out.reshape(24, 2, HALF).transpose(1, 0, 2),
            w_up.reshape(24, 16, 2, 2, 48).transpose(2, 0, 3, 1, 4).reshape(2, 24, 1536),
        ],
        axis=2,
    ).astype(F32)
    sd = jax.ShapeDtypeStruct
    outs = pl.pallas_call(
        front,
        name="front",
        out_shape=[
            sd((2, 64, D), BF), sd((2, 64, D), F32), sd((HH, ROWS, 128), BF), sd((HH, 128, 128), BF),
            sd((HH, 128, 2048), BF), sd((256, D), BF), sd((2, 2, 64, D), BF), sd((D, HALF), BF),
            sd((2, 4, 4, 48, D), BF), sd((2, 4, 4, 48, D), BF), sd((2, 2, 4, 48, HALF), BF), sd((1, D), F32),
        ],
        in_specs=[IN_VMEM] * 4 + [pl.BlockSpec(memory_space=pl.ANY)] + [IN_VMEM] * 3,
        out_specs=[IN_VMEM] * 12,
        scratch_shapes=[
            vmem((2, 24, 2304), F32), vmem((2, 2, 64, D)), vmem((2, 2, 64, D)), vmem((HH, 2, 64, 2048)),
            vmem((4, 4, 48, HALF)), vmem((2, 4, 4, 48, HALF)),
            vmem((4, 4, 48, D)), vmem((4, 4, 48, D)), vmem((4, 4, 48, D)), vmem((4, 4, 48, D)),
            vmem((4, 4, 3, ROWS, 128)), vmem((4, 4, 3, ROWS, 128)),
            vmem((4, 4, 3, ROWS, 128)), vmem((4, 4, 3, ROWS, 128)),
            vmem((4, 3, ROWS, 128)), vmem((4, 3, ROWS, 128)), vmem((4, 3, ROWS, 128)), vmem((4, 3, ROWS, 128)),
            vmem((2, HALF, 128), F32), vmem((2, 8, 128), F32), vmem((2, 2, 128, HALF)), vmem((HH, ROWS, 128)),
            vmem((256, D), F32), vmem((256, D)), vmem((2, 256, D)), vmem((2, 256, D)), vmem((2, 256, D), F32),
            vmem((2, 2, 64, D), F32), vmem((2, 64, D), F32), vmem((2, 2, 64, D), F32), vmem((2, 2, 64, D), F32),
            dma(2, 8), dma(2, 6, 2, 3), dma(2, 2, 2, 3), pltpu.SemaphoreType.DMA,
        ],
        compiler_params=pltpu.CompilerParams(
            collective_id=0, has_side_effects=True, vmem_limit_bytes=60 << 20
        ),
    )(tokens, out_grad, pre, w_down, mix_table, mask, gain_mix.reshape(1, D), gain_ffn.reshape(1, D))
    out, mgrad, gch, vals, e, normed, tok, wv, dwu, dwd, dwo, gain_f = outs
    tg, input_grad, res = pl.pallas_call(
        back,
        name="back",
        out_shape=[sd((2, HH, 64, 256), F32), sd((2, 64, D), F32), sd((2, 256, D), BF)],
        in_specs=[IN_VMEM] * 14,
        out_specs=[IN_VMEM] * 3,
        scratch_shapes=[
            vmem((4, 4, 3, ROWS, 128)), vmem((4, 4, 3, ROWS, 128)),
            vmem((4, 4, 4, 48, D)), vmem((4, 4, 48, D)), vmem((4, 4, 48, D)),
            vmem((2, 4, 4, 48, HALF)), vmem((2, 4, 48, HALF)), vmem((2, 4, 48, HALF)), vmem((4, 4, 48, HALF)),
            vmem((16, D)), vmem((4, 4, 16, D)),
            vmem((4, 2, 3, 128, 256)), vmem((4, 2, 3, 128, 256)), vmem((3, 2, 3, 128, 256)), vmem((3, 2, 3, 128, 256)),
            vmem((HH, 2, 64, 256), F32), vmem((HH, 64, 256), F32),
            vmem((2, HALF, 128), F32), vmem((2, 128, D), F32), vmem((256, D), F32), vmem((256, D), F32),
            vmem((256, D)), vmem((8, 32, D)), vmem((8, 32, D)), vmem((2, 8, 32, D)),
            dma(2, 2, 2, 3), dma(2, 4, 2, 3), dma(2, 2, 2, 3), dma(2, 2, 3), dma(2, 4, 2), dma(2, 3, 2),
            dma(2, 3), dma(2, 2, 8),
        ],
        compiler_params=pltpu.CompilerParams(
            collective_id=1, has_side_effects=True, vmem_limit_bytes=60 << 20
        ),
    )(
        gch, vals, e, mask, mask_cols, normed, tok, wv, dwu, dwd,
        dwo.reshape(4, 4, 48, HALF), gain_f, gain_mix.reshape(1, D), mgrad,
    )
    own = lax.dynamic_index_in_dim(res, c, 0, False).astype(F32)
    rows = lax.dynamic_slice_in_dim(res[:, 0:96].reshape(2, 2, 48, D), 24 * c, 24, 2).astype(F32)
    up_grad = rows.reshape(2, 2, 24, 16, 48).transpose(2, 3, 0, 1, 4).reshape(24, 3072)
    down_grad = own[96:192]
    pair = lax.dynamic_slice_in_dim(res[:, 192:240], 24 * c, 24, 1).astype(F32)
    out_w = jnp.concatenate([pair[0, :, 0:HALF], pair[1, :, 0:HALF]], axis=1)
    value_w = jnp.concatenate([pair[0, :, HALF:D], pair[1, :, HALF:D]], axis=1)
    gains = lax.dynamic_slice_in_dim(own[240:242] + own[242:244], 24 * s, 24, 1)
    return (
        out, input_grad, value_w, out_w, up_grad, down_grad, gains[1], gains[0],
        tg.reshape(HEADS, 64, 256),
    )


def solution(mesh):
    return jax.shard_map(
        per_device,
        mesh=mesh,
        in_specs=(
            P("dp", "seq", None),
            P("dp"),
            P("seq", None),
            P("seq", None),
            P("seq", None),
            P("seq", None),
            P(),
            P(),
            P(None, "seq", None),
            P("dp", "seq", None),
        ),
        out_specs=(
            P("dp", "seq", None),
            P("dp", "seq", None),
            P("seq", None),
            P("seq", None),
            P("seq", None),
            P("seq", None),
            P("seq"),
            P("seq"),
            P(None, "seq", "dp"),
        ),
        check_vma=False,
    )
```

time: 1250 us -> 217 us (0.17)
  waiting for transfers between devices: 539 us -> 0 us
  blocking collectives: 263 us -> 0 us
  Pallas kernels: 0 us -> 197 us
  matrix products: 119 us -> 0 us
  other arithmetic: 113 us -> 4.03 us
  local copies, waits for them, and re-layouts: 105 us -> 15 us
  loops' own time: 87.2 us -> 0 us
  between operations: 15.5 us -> 0.79 us
    reduce_scatter x5 -> x0, waiting for transfers between devices: 279 us -> none  [the longest x1 106 us: per_device(): lax.psum_scatter(down_weight_grad, 'seq', scatter_dimension=0, tiled=True)]
    unnamed x2 -> x0, blocking collectives: 249 us -> none
    pallas_call x0 -> x2, Pallas kernels: none -> 197 us  [the longest x1 109 us: per_device(): pl.pallas_call(back, name='back', out_shape=[sd((2, HH, 64, 256), F32), s...]
    all_gather x7 -> x0, waiting for transfers between devices: 143 us -> none  [the longest x2 101 us: combined_all(): pieces = jax.tree.map(lambda part: lax.all_gather(part, axis), value)]
    dot_general x60 -> x0, matrix products: 119 us -> none  [the longest x24 39.7 us: column_terms(): jnp.einsum('bid,bjd->bji', head_slice(grads_all, head_index), head_slice(...]
    psum x2 -> x0, waiting for transfers between devices: 114 us -> none  [the longest x1 114 us: per_device(): row_deltas = lax.psum(row_deltas, 'seq')]
    another operation x5 -> x0, loops' own time: 87.2 us -> none  [the longest x1 31.6 us: column_first(): row_deltas, pieces = lax.map(first_pass, head_ids)]
    add x34 -> x2, other arithmetic: 43.6 us -> 0.08 us  [the longest x1 0.07 us: per_device(): gains = lax.dynamic_slice_in_dim(own[240:242] + own[242:244], 24 * s, 24, 1)]
  transfers between devices with their start and end apart: 14 -> 0, of which waited for: 7 -> 0; matrix products, arithmetic and copies ran while one was open for 26% -> 0% of each run, Pallas kernels for 0% -> 0%
where the time goes in v1:
time: 217 us
  Pallas kernels  197 us (91%)
  local copies, waits for them, and re-layouts  15 us (7%)
  other arithmetic  4.03 us (2%)
    pallas_call x1, Pallas kernels, per_device(): pl.pallas_call(back, name='back', out_shape=[sd((2, HH, 64, 256), F32), s...  109 us
    pallas_call x1, Pallas kernels, per_device(): pl.pallas_call(front, name='front', out_shape=[sd((2, 64, D), BF), sd((2,...  88.5 us

profile of v1, /device:TPU:1, one launch (start us, length us, event | category | flops | bytes accessed | tf_op | source)
XLA Modules:
  0.0 216.8 jit_solution(16515279182281958355)
XLA Ops:
  0.7 0.7 compare_convert_fusion
  1.4 1.3 reshape.102.gain_mix
  2.7 1.3 reshape.103.gain_ffn
  3.9 0.6 concatenate.13.mask
  4.5 0.8 bitcast_bitcast_fusion
  5.3 0.8 broadcast_in_dim.2.mask_cols
  6.1 1.3 reshape.100
  7.4 0.1 copy.32
  7.5 0.5 reshape.101
  8.0 0.8 maximum_convert_fusion.pre
  8.8 88.5 %front.1 = (bf16[2,64,768]{2,1,0:T(8,128)(2,1)}, f32[2,64,768]{2,1,0:T(8,128)}, bf16[6,144,128]{2,1,0:T(8,128)(2,1)}, bf16[6,128,128]{2,1,0:T(8,128)(2,1)}, bf16...) custom-call(bf16[2,64,768]{2,1,0:T(8,128)(2,1)} %tokens.1, ...), custom_call_target="tpu_custom_call" | custom-call | tf_op jit(solution)/shard_map/front/pallas_call | solution.py:586
  97.3 108.5 %back.1 = (f32[2,6,64,256]{3,2,1,0:T(8,128)}, f32[2,64,768]{2,1,0:T(8,128)}, bf16[2,256,768]{2,1,0:T(8,128)(2,1)}) custom-call(bf16[6,144,128]{2,1,0:T(8,128)(2,1)} %get-tuple-element.25.gch, bf16[6,128,128]{2,1,0:T(8,128)(2,1)} %get-tuple-element.26.vals, bf16[6,128,2048]{2,1,0:T(8,128)(2,1)} %get-tuple-element.27.e, f32[8,128]{1,0:T(8,128)} %concatenate.13.mask, ...), custom_call_target="tpu_custom_call" | custom-call | tf_op jit(solution)/shard_map/back/pallas_call | solution.py:613
  205.9 0.9 slice.40
  206.8 0.6 pad_maximum_fusion.1
  207.5 0.6 pad_maximum_fusion
  208.1 0.0 copy-start.2
  208.1 1.0 slice.45
  209.1 0.0 copy-start.1
  209.1 1.1 dynamic-slice_convert_fusion
  210.2 0.0 copy-start
  210.3 0.7 slice_bitcast_fusion
  211.0 0.1 fusion
  211.1 0.5 slice_bitcast_fusion.5
  211.6 0.4 reshape.114
  212.1 0.6 copy.31
  212.7 1.8 reshape.111
  214.5 0.0 copy-done.2
  214.5 0.7 copy.36
  215.2 0.0 copy-done.1
  215.2 0.7 copy.37
  215.9 0.0 copy-done
  215.9 0.9 copy.38
  (5 shorter events, 0.1 us)
Async XLA Ops:
  208.1 6.4 %copy-start.2 = (bf16[2,64,768]{2,1,0:T(8,128)(2,1)S(1)}, bf16[2,64,768]{2,1,0:T(8,128)(2,1)}, u32[]{:S(2)}) copy-start(bf16[2,64,768]{2,1,0:T(8,128)(2,1)} %get-tuple-element.58) | copy-start | bytes 589828
  209.1 6.1 %copy-start.1 = (f32[2,64,768]{2,1,0:T(8,128)S(1)}, f32[2,64,768]{2,1,0:T(8,128)}, u32[]{:S(2)}) copy-start(f32[2,64,768]{2,1,0:T(8,128)} %get-tuple-element.59) | copy-start | bytes 1179652
  210.2 5.7 %copy-start = (f32[2,6,64,256]{3,2,1,0:T(8,128)S(1)}, f32[2,6,64,256]{3,2,1,0:T(8,128)}, u32[]{:S(2)}) copy-start(f32[2,6,64,256]{3,2,1,0:T(8,128)} %get-tuple-element.38) | copy-start | bytes 2359300

commit v2 on v1

v2 whole, which is shorter than its diff:
```python
import jax
import jax.numpy as jnp
from jax import lax
from jax.experimental import pallas as pl
from jax.experimental.pallas import tpu as pltpu
from jax.sharding import PartitionSpec as P

D = 768
HALF = 384
HEADS = 12
HH = 6
EPS = 1e-06
MESH = pl.DeviceIdType.MESH
BF = jnp.bfloat16
F32 = jnp.float32
OFFS = (1, 3, 2)
ROWS = 144
GELU_C = 0.7978845608028654
GELU_A = 0.044715


def here():
    s = lax.axis_index("seq")
    return lax.axis_index("dp"), s // 8, (s // 2) % 4, s % 2


def at(z, x, y, c):
    return (z, (x * 4 + y) * 2 + c)


def remote(src, dst, sems, idx, device):
    return pltpu.make_async_remote_copy(
        src_ref=src,
        dst_ref=dst,
        send_sem=sems.at[(0,) + idx],
        recv_sem=sems.at[(1,) + idx],
        device_id=device,
        device_id_type=MESH,
    )


def along(first, k):
    z, x, y, c = here()
    if first == "x":
        return at(z, lax.rem(x + k, 4), y, c)
    return at(z, x, lax.rem(y + k, 4), c)


OTHER = {"x": "y", "y": "x"}


def own_at(first):
    _, x, y, _ = here()
    return x if first == "x" else y


def gather_one(buf, first, sems):
    _, x, y, _ = here()
    return [
        remote(buf.at[x, y], buf.at[x, y], sems, (0, i), along(first, k))
        for i, k in enumerate(OFFS)
    ]


def gather_two(buf, first, sems):
    _, x, y, _ = here()
    view = buf.at[:, y] if first == "x" else buf.at[x]
    return [
        remote(view, view, sems, (1, i), along(OTHER[first], k)) for i, k in enumerate(OFFS)
    ]


def scatter_one(src, rcv, first, sems):
    mine = own_at(first)
    out = []
    for i, k in enumerate(OFFS):
        to = lax.rem(mine + k, 4)
        part = src.at[to] if first == "x" else src.at[:, to]
        out.append(remote(part, rcv.at[i], sems, (0, i), along(first, k)))
    return out


def scatter_sum(src, rcv, mid, first):
    mine = own_at(first)
    for j in range(4):
        own = src[mine, j] if first == "x" else src[j, mine]
        total = own.astype(F32)
        for i in range(3):
            total = total + rcv[i, j].astype(F32)
        mid[j] = total.astype(BF)


def scatter_two(mid, rcv, first, sems):
    second = OTHER[first]
    mine = own_at(second)
    return [
        remote(mid.at[lax.rem(mine + k, 4)], rcv.at[i], sems, (1, i), along(second, k))
        for i, k in enumerate(OFFS)
    ]


def scatter_end(mid, rcv, first):
    total = mid[own_at(OTHER[first])].astype(F32)
    for i in range(3):
        total = total + rcv[i].astype(F32)
    return total


def start(copies):
    for copy in copies:
        copy.start()


def wait_recv(copies):
    for copy in copies:
        copy.wait_recv()


def wait_send(copies):
    for copy in copies:
        copy.wait_send()


def signal(device):
    pl.semaphore_signal(
        pltpu.get_barrier_semaphore(), inc=1, device_id=device, device_id_type=MESH
    )


def greet():
    z, x, y, c = here()
    count = 0
    for k in range(1, 4):
        signal(at(z, lax.rem(x + k, 4), y, c))
        signal(at(z, x, lax.rem(y + k, 4), c))
        count += 2
    signal(at(z, x, y, 1 - c))
    count += 1
    for k in range(1, 8):
        signal(at(lax.rem(z + k, 8), x, y, c))
        count += 1
    return count


def meet(count):
    pl.semaphore_wait(pltpu.get_barrier_semaphore(), count)


def dot(a, b):
    return jnp.dot(a, b, preferred_element_type=F32)


def dot_nt(a, b):
    return lax.dot_general(a, b, (((1,), (1,)), ((), ())), preferred_element_type=F32)


def flip(a):
    return jnp.transpose(a)


def rms_of(v):
    return lax.rsqrt(jnp.mean(v * v, axis=-1, keepdims=True) + EPS)


def layer(
    lengths, tokens, out_grad, w_value, w_out, w_up, w_down, gain_mix, gain_ffn, table,
    out, input_grad, d_value, d_out, d_up, d_down, gsum, tg,
    perm, pre, got, tok, og, e, wv, wo_all, wz,
    ux, uy, rx, ry, mx, my, rx2, ry2, mt, rr, mix, vt, vals, mcol, normed, middle, nf, bgs, hid, pgr, act,
    part, part_r, fng, fng_r, mgrad, dwu, dwda, dwdb, dwo, dwv, gx, gy,
    ru, rd, rl, mu, md, ml, ru2, rd2, rl2, gs, gr, up_s, up_r, dn_s, dn_r, tgs, tg_r, vgt, ng_r,
    sums, zr, zr2, zs, zs2, post,
    s_sib, s_ag, s_wz, s_u, s_loc, s_g, s_w, s_gain, s_up, s_dn, s_z,
):
    z, x, y, c = here()
    sib = at(z, x, y, 1 - c)
    up = at(lax.rem(z + 1, 8), x, y, c)
    down = at(lax.rem(z + 7, 8), x, y, c)
    wo = wo_all.at[c]

    def to_sib(src, dst, i):
        return remote(src, dst, s_sib, (i,), sib)

    count = greet()
    own_tab = pltpu.make_async_copy(table.at[pl.ds(6 * c, 6)], e.at[:, c], s_loc)
    own_tab.start()
    col = lax.broadcasted_iota(jnp.int32, (1, D), 1)
    odd = jnp.where(col >= HALF, 1, 0)
    low = col - HALF * odd
    half = jnp.where(low >= 192, 1, 0)
    low = low - 192 * half
    quad = jnp.where(low >= 48, 1, 0) + jnp.where(low >= 96, 1, 0) + jnp.where(low >= 144, 1, 0)
    origin = low + 144 * quad + 96 * odd + 48 * half
    perm[...] = jnp.where(lax.broadcasted_iota(jnp.int32, (D, D), 0) == origin, 1.0, 0.0).astype(BF)
    block = pl.multiple_of(D * lax.rem(z, 4), D)
    mine = dot(w_up[:, pl.ds(block, D)], perm[...])
    for cc in range(2):
        cols = slice(HALF * cc, HALF * cc + HALF)
        pre[cc, :, 0:HALF] = w_out[:, cols].astype(F32)
        pre[cc, :, HALF:D] = w_value[:, cols].astype(F32)
        pre[cc, :, D : D + HALF] = mine[:, cols]
    meet(count)
    swap_pre = to_sib(pre.at[1 - c], got.at[c], 0)
    swap_tok = to_sib(tokens, tok.at[:, c], 1)
    swap_tab = to_sib(table.at[pl.ds(6 * (1 - c), 6)], e.at[:, c], 2)
    swap_og = to_sib(out_grad, og.at[:, c], 3)
    start([swap_pre, swap_tok, swap_tab, swap_og])
    got[c] = pre[c]
    tok[:, c] = tokens[...]
    og[:, c] = out_grad[...]
    wz_x = wz.at[z, :, :, pl.ds(0, 32)]
    wz_y = wz.at[z, :, :, pl.ds(32, 16)]
    bufs = ((wv, "x"), (wo, "y"), (wz_x, "x"), (wz_y, "y"))
    g1 = [gather_one(buf, first, s_ag.at[:, i]) for i, (buf, first) in enumerate(bufs)]
    g2 = [gather_two(buf, first, s_ag.at[:, i]) for i, (buf, first) in enumerate(bufs)]
    swap_pre.wait_recv()
    shard = got[...].reshape(48, D + HALF).astype(BF)
    wo[x, y] = shard[:, 0:HALF]
    wv[x, y] = shard[:, HALF:D]

    @pl.when(z < 4)
    def _():
        wz[z, x, y] = shard[:, D : D + HALF]

    @pl.when(z >= 4)
    def _():
        rows = pl.ds(pl.multiple_of(48 * (lax.rem(z, 4) // 2), 16), 48)
        cols = pl.ds(pl.multiple_of(HALF * lax.rem(z, 2), 128), HALF)
        wz[z, x, y] = w_down[rows, cols]

    for i in range(4):
        start(g1[i])

    def slab(t, half, sign):
        return wz.at[lax.rem(z + 8 - sign * t, 8), pl.ds(2 * half, 2)]

    wz_up = [[remote(slab(t, h, 1), slab(t, h, 1), s_wz, (0, t, h), up) for h in range(2)] for t in range(4)]
    wz_dn = [[remote(slab(t, h, -1), slab(t, h, -1), s_wz, (1, t, h), down) for h in range(2)] for t in range(4)]

    def pass_on(t, h):
        wz_up[t - 1][h].wait_recv()
        if t < 3 or h == 0:
            wz_up[t][h].start()
        wz_dn[t - 1][h].wait_recv()
        if t < 3 or h == 1:
            wz_dn[t][h].start()

    for i in range(4):
        wait_recv(g1[i])
        start(g2[i])
    swap_tok.wait_recv()
    values = tok[...].reshape(256, D).astype(F32)
    gm = gain_mix[...].reshape(1, D)
    gf = gain_ffn[...].reshape(1, D)
    normed[...] = (values * rms_of(values) * gm).astype(BF)
    place = (4 * x + y) * 128
    lane = lax.broadcasted_iota(jnp.int32, (1, 128), 1) + place
    row = lax.broadcasted_iota(jnp.int32, (128, 128), 0) + place
    masks = [jnp.where(lane < lengths[b], 1.0, 0.0) for b in range(2)]
    for b in range(2):
        mcol[b] = jnp.where(row < lengths[b], 1.0, 0.0)
    swap_tab.wait_recv()
    own_tab.wait()

    def exps(h, carry):
        e[h] = jnp.exp(e[h].astype(F32)).astype(BF)
        return carry

    lax.fori_loop(0, HH, exps, 0)
    wait_recv(g2[2])
    wait_recv(g2[3])
    for h in range(2):
        wz_up[0][h].start()
        wz_dn[0][h].start()
    wait_recv(g2[0])
    v = dot(normed[...], wv[...].reshape(D, HALF)).astype(BF).astype(F32)
    vall = flip(v) * jnp.concatenate(masks, axis=1)
    ones = jnp.concatenate(masks + [jnp.zeros((14, 128), F32)], axis=0)
    for h in range(HH):
        block = jnp.concatenate(
            [vall[64 * h : 64 * h + 64, 0:128], vall[64 * h : 64 * h + 64, 128:256]], axis=0
        )
        vt[h] = jnp.concatenate([block, ones], axis=0).astype(BF)
        vals[h] = flip(block).astype(BF)

    s1x = scatter_one(ux, rx, "x", s_u.at[:, 0])
    s1y = scatter_one(uy, ry, "y", s_u.at[:, 1])
    for i, k in enumerate(OFFS + (0,)):
        xx = lax.rem(x + k, 4)
        yy = lax.rem(y + k, 4)

        def head_x(h, carry, xx=xx):
            cols = pl.ds(pl.multiple_of(512 * xx, 512), 512)
            u = dot(vt[h], e[h, :, :, cols].reshape(128, 512))
            for j in range(4):
                ux[xx, j, h] = u[:, 128 * j : 128 * j + 128].astype(BF)
            return carry

        def head_y(h, carry, yy=yy):
            for j in range(4):
                cols = pl.ds(pl.multiple_of(512 * j + 128 * yy, 128), 128)
                uy[j, yy, h] = dot(vt[h + 3], e[h + 3, :, :, cols].reshape(128, 128)).astype(BF)
            return carry

        lax.fori_loop(0, 3, head_x, 0)
        if i < 3:
            s1x[i].start()
        lax.fori_loop(0, 3, head_y, 0)
        if i < 3:
            s1y[i].start()
    pass_on(1, 0)
    wait_recv(g2[1])
    swap_wo = to_sib(wo, wo, 5)
    swap_wo.start()
    pass_on(1, 1)
    pass_on(2, 0)
    s2x = scatter_two(mx, rx2, "x", s_u.at[:, 0])
    s2y = scatter_two(my, ry2, "y", s_u.at[:, 1])
    wait_recv(s1x)
    scatter_sum(ux, rx, mx, "x")
    start(s2x)
    wait_recv(s1y)
    scatter_sum(uy, ry, my, "y")
    start(s2y)
    pass_on(2, 1)
    pass_on(3, 0)
    for half, (copies, mid, rcv, first) in enumerate(((s2x, mx, rx2, "x"), (s2y, my, ry2, "y"))):
        wait_recv(copies)
        total = scatter_end(mid, rcv, first)
        for hh in range(3):
            h = half * 3 + hh
            for b in range(2):
                r = masks[b] / total[hh, 128 + b : 129 + b]
                rr[b, h : h + 1] = r
                mt[b, 64 * h : 64 * h + 64] = total[hh, 64 * b : 64 * b + 64] * r
    for b in range(2):
        mix[c, b] = flip(mt[b]).astype(BF)
    swap_mix = to_sib(mix.at[c], mix.at[c], 6)
    swap_mix.start()
    swap_wo.wait_recv()
    swap_mix.wait_recv()
    mixed = [mix[i].reshape(256, HALF) for i in range(2)]
    for cc in range(2):
        w = wo_all[cc].reshape(D, HALF)
        cols = slice(HALF * cc, HALF * cc + HALF)
        middle[:, cols] = (
            tok[...].reshape(256, D)[:, cols].astype(F32)
            + dot(mixed[0], w[0:HALF])
            + dot(mixed[1], w[HALF:D])
        )
    mid_v = middle[...]
    rms = rms_of(mid_v)
    nf[...] = (mid_v * rms * gf).astype(BF)
    swap_og.wait_recv()
    grad = og[...].reshape(256, D)
    pass_on(3, 1)
    wz_up[3][0].wait_recv()
    wz_dn[3][1].wait_recv()
    for hf in range(2):
        hp = jnp.concatenate([dot(nf[...], wz[2 * hf + i].reshape(D, HALF)) for i in range(2)], axis=1)
        t = jnp.tanh(GELU_C * (hp + GELU_A * hp * hp * hp))
        hid[hf] = (0.5 * hp * (1.0 + t)).astype(BF)
        act[hf] = 0.5 * (1.0 + t) + 0.5 * hp * (1.0 - t * t) * (
            GELU_C * (1.0 + 3.0 * GELU_A * hp * hp)
        )

    def down_rows(m, b):
        return jnp.concatenate([wz[4 + b, m].reshape(192, HALF), wz[6 + b, m].reshape(192, HALF)], axis=0)

    lots = (
        (dwda, rd.at[0], md.at[0], rd2.at[0], "x"),
        (dwdb, rd.at[1], md.at[1], rd2.at[1], "y"),
        (dwu.at[0], ru.at[0], mu.at[0], ru2.at[0], "x"),
        (dwu.at[1], ru.at[1], mu.at[1], ru2.at[1], "y"),
        (dwo, rl.at[0], ml.at[0], rl2.at[0], "x"),
        (dwv, rl.at[1], ml.at[1], rl2.at[1], "y"),
    )
    w1 = [scatter_one(lot[0], lot[1], lot[4], s_w.at[:, i]) for i, lot in enumerate(lots)]
    w2 = [scatter_two(lot[2], lot[3], lot[4], s_w.at[:, i]) for i, lot in enumerate(lots)]
    for hf in range(2):
        for i in range(2):
            m = 2 * hf + i
            cols = slice(HALF * i, HALF * i + HALF)
            hg = dot_nt(grad[:, 0:HALF], down_rows(m, 0)) + dot_nt(grad[:, HALF:D], down_rows(m, 1))
            pgr[hf, :, cols] = (act[hf, :, cols] * hg).astype(BF)
            more = dot_nt(pgr[hf, :, cols], wz[m].reshape(D, HALF)).reshape(2, 2, 64, D)
            fng[...] = more if m == 0 else fng[...] + more
    swap_fng = to_sib(fng, fng_r, 7)
    swap_fng.start()
    for hf in range(2):
        dwd = dot(flip(hid[hf]), grad).astype(BF)
        for i in range(2):
            for a in range(2):
                for q in range(4):
                    base = HALF * i + 192 * a + 48 * q
                    dwda[2 * hf + i, q, 48 * a : 48 * a + 48] = dwd[base : base + 48, 0:HALF]
                    dwdb[2 * hf + i, q, 48 * a : 48 * a + 48] = dwd[base : base + 48, HALF:D]
    swap_fng.wait_recv()
    full = (fng[...] + fng_r[...]).reshape(256, D)
    mid_v = middle[...]
    rms = rms_of(mid_v)
    gain_f = jnp.sum(full * mid_v * rms, axis=0, keepdims=True)
    weighted = full * gf
    inner = jnp.mean(weighted * mid_v, axis=-1, keepdims=True)
    mg = grad.astype(F32) + rms * weighted - mid_v * (rms * rms * rms) * inner
    mgrad[...] = mg.reshape(2, 2, 64, D)
    bg = mg.astype(BF)
    bgs[...] = bg
    xg = jnp.zeros((256, HALF), F32)
    for cc in range(2):
        w = wo_all[cc, pl.ds(2 * c, 2)].reshape(HALF, HALF)
        xg = xg + dot_nt(bg[:, HALF * cc : HALF * cc + HALF], w)
    deltas = []
    for b in range(2):
        xgt = flip(xg[128 * b : 128 * b + 128])
        for h in range(HH):
            rows = xgt[64 * h : 64 * h + 64]
            r = rr[b, h : h + 1]
            deltas.append(jnp.sum(rows * mt[b, 64 * h : 64 * h + 64], axis=0, keepdims=True) * r)
            own = gx if h < 3 else gy
            own[x, y, h % 3, 64 * b : 64 * b + 64] = (rows * r).astype(BF)
    for h in range(HH):
        d0, d1 = deltas[h], deltas[HH + h]
        h0 = d0.astype(BF).astype(F32)
        h1 = d1.astype(BF).astype(F32)
        own = gx if h < 3 else gy
        own[x, y, h % 3, 128:144] = jnp.concatenate(
            [h0, h1, d0 - h0, d1 - h1, jnp.zeros((12, 128), F32)], axis=0
        ).astype(BF)
    a1x = gather_one(gx, "x", s_g.at[:, 0])
    a1y = gather_one(gy, "y", s_g.at[:, 1])
    a2x = gather_two(gx, "x", s_g.at[:, 0])
    a2y = gather_two(gy, "y", s_g.at[:, 1])
    start(a1x)
    start(a1y)
    dwu[0] = dot(flip(nf[...]), pgr[0]).astype(BF).reshape(4, 4, 48, D)
    wait_recv(a1x)
    start(a2x)
    wait_recv(a1y)
    start(a2y)
    start(w1[0])
    start(w1[1])
    dwu[1] = dot(flip(nf[...]), pgr[1]).astype(BF).reshape(4, 4, 48, D)
    start(w1[2])
    start(w1[3])
    bg_c = bgs[:, pl.ds(pl.multiple_of(HALF * c, 128), HALF)]
    for i in range(2):
        dwo[pl.ds(2 * i, 2)] = dot(flip(mixed[i]), bg_c).astype(BF).reshape(2, 4, 48, HALF)
    start(w1[4])
    for hf in range(2):
        down_w = [jnp.concatenate([down_rows(2 * hf, b), down_rows(2 * hf + 1, b)], axis=0) for b in range(2)]
        more = jnp.concatenate([dot(hid[hf], w) for w in down_w], axis=1).reshape(2, 2, 64, D)
        part[...] = more if hf == 0 else part[...] + more
    swap_part = to_sib(part.at[:, 1 - c], part_r, 8)
    swap_part.start()
    swap_fng.wait_send()
    fng[...] = middle[...].reshape(2, 2, 64, D)
    swap_part.wait_recv()
    out[...] = (fng[:, c] + (part[:, c] + part_r[...])).astype(BF)
    wait_recv(a2x)
    wait_recv(a2y)

    def table_part(d, hf):
        buf = gx if hf == 0 else gy
        result = []
        for hh in range(3):
            h = 3 * hf + hh
            pair = []
            for i in range(2):
                k = 2 * d + i
                g = buf[k // 4, lax.rem(k, 4), hh]
                cols = pl.ds(pl.multiple_of(256 * d + 128 * i, 128), 128)
                extra = g[128:144].astype(F32)
                s = dot(vals[h], g[0:128])
                s = s - mcol[0] * (extra[0:1] + extra[2:3])
                s = s - mcol[1] * (extra[1:2] + extra[3:4])
                pair.append(s * e[h, :, :, cols].reshape(128, 128).astype(F32))
            result.append(jnp.concatenate(pair, axis=1))
        return result

    def ring(send, recv, sems, t, hf, device):
        return remote(send.at[hf, t], recv.at[hf, t], sems, (hf, t), device)

    ups = [[ring(up_s, up_r, s_up, t, hf, up) for t in range(4 - hf)] for hf in range(2)]
    dns = [[ring(dn_s, dn_r, s_dn, t, hf, down) for t in range(3 + hf)] for hf in range(2)]

    def step(t):
        for copies, send, recv, hf, d in (
            (ups[0], up_s, up_r, 0, lax.rem(z + 12 - t, 8)),
            (dns[1], dn_s, dn_r, 1, lax.rem(z + 4 + t, 8)),
            (ups[1], up_s, up_r, 1, lax.rem(z + 11 - t, 8)),
            (dns[0], dn_s, dn_r, 0, lax.rem(z + 5 + t, 8)),
        ):
            if t >= len(copies):
                continue
            parts = table_part(d, hf)
            if t > 0:
                copies[t - 1].wait_recv()
            for hh in range(3):
                p = parts[hh]
                if t > 0:
                    p = p + recv[hf, t - 1, hh].astype(F32)
                send[hf, t, hh] = p.astype(BF)
            copies[t].start()

    step(0)
    for h in range(HH):
        buf = gx if h < 3 else gy
        total = jnp.zeros((128, 128), F32)
        for k in range(16):
            total = total + dot_nt(
                buf[k // 4, k % 4, h % 3, 0:128], e[h, :, :, 128 * k : 128 * k + 128].reshape(128, 128)
            )
        for b in range(2):
            vgt[b, 64 * h : 64 * h + 64] = total[64 * b : 64 * b + 64] * masks[b]
    vg = jnp.concatenate([flip(vgt[b]) for b in range(2)], axis=0).astype(BF)
    dwv[...] = dot(flip(normed[...]), vg).astype(BF).reshape(4, 4, 48, HALF)
    start(w1[5])
    swap_part.wait_send()
    part[...] = dot_nt(vg, wv[...].reshape(D, HALF)).reshape(2, 2, 64, D)
    swap_ng = to_sib(part, ng_r, 9)
    swap_ng.start()
    step(1)
    swap_ng.wait_recv()
    full = (part[...] + ng_r[...]).reshape(256, D)
    xv = tok[...].reshape(256, D).astype(F32)
    rms = rms_of(xv)
    gain_m = jnp.sum(full * xv * rms, axis=0, keepdims=True)
    weighted = full * gm
    inner = jnp.mean(weighted * xv, axis=-1, keepdims=True)
    fng[...] = (rms * weighted - xv * (rms * rms * rms) * inner).reshape(2, 2, 64, D)
    input_grad[...] = mgrad[:, c] + fng[:, c]
    gains = jnp.concatenate([gain_m, gain_f], axis=0)
    high = gains.astype(BF).astype(F32)
    gs[...] = jnp.concatenate([high, gains - high, jnp.zeros((12, D), F32)], axis=0).astype(BF)
    gr[x, y] = gs[...]
    gain1 = gather_one(gr, "x", s_gain)
    gain2 = gather_two(gr, "x", s_gain)
    start(gain1)

    def middle_sum(i):
        wait_recv(w1[i])
        src, rcv, mid, _, first = lots[i]
        scatter_sum(src, rcv, mid, first)
        start(w2[i])

    def last_sum(i, rows, cols):
        wait_recv(w2[i])
        _, _, mid, rcv, first = lots[i]
        sums[rows, cols] = scatter_end(mid, rcv, first).astype(BF)

    def spread(base, rows, buf, i):
        def chunk(d):
            return sums.at[
                pl.ds(pl.multiple_of(base + rows * (d // 2), 16), rows),
                pl.ds(pl.multiple_of(HALF * lax.rem(d, 2), 128), HALF),
            ]

        return [
            remote(
                chunk(lax.rem(z + k, 8)), buf.at[k - 1], s_z, (i, k - 1), at(lax.rem(z + k, 8), x, y, c)
            )
            for k in range(1, 8)
        ]

    def collect(base, rows, buf, res, i):
        total = sums[
            pl.ds(pl.multiple_of(base + rows * (z // 2), 16), rows),
            pl.ds(pl.multiple_of(HALF * lax.rem(z, 2), 128), HALF),
        ].astype(F32)
        for k in range(7):
            total = total + buf[k].astype(F32)
        res[z] = total.astype(BF)
        return [
            remote(res.at[z], res.at[z], s_z, (i, k - 1), at(lax.rem(z + k, 8), x, y, c))
            for k in range(1, 8)
        ]

    middle_sum(0)
    middle_sum(1)
    step(2)
    middle_sum(2)
    middle_sum(3)
    middle_sum(4)
    middle_sum(5)
    wait_recv(gain1)
    start(gain2)
    step(3)
    last_sum(0, slice(96, 192), slice(0, HALF))
    last_sum(1, slice(96, 192), slice(HALF, D))
    last_sum(2, slice(0, 48), slice(0, D))
    last_sum(3, slice(48, 96), slice(0, D))
    z1 = spread(0, 48, zr, 0)
    start(z1)
    last_sum(4, slice(192, 240), slice(0, HALF))
    last_sum(5, slice(192, 240), slice(HALF, D))
    wait_recv(gain2)
    gtot = jnp.sum(gr[...].reshape(16, 16, D).astype(F32), axis=0)
    gains = gtot[0:2] + gtot[2:4]
    high = gains.astype(BF).astype(F32)
    sums[240:256] = jnp.concatenate([high, gains - high, jnp.zeros((12, D), F32)], axis=0).astype(BF)
    z3 = spread(192, 16, zr2, 1)
    start(z3)
    own = [table_part(z, hf) for hf in range(2)]
    swap_tg = to_sib(tgs, tg_r, 10)
    for hf in range(2):
        ups[hf][-1].wait_recv()
        dns[hf][-1].wait_recv()
        for hh in range(3):
            p = own[hf][hh] + (
                up_r[hf, 3 - hf, hh].astype(F32) + dn_r[hf, 2 + hf, hh].astype(F32)
            )
            act[0, 0:128, 0:256] = p
            tg[c, 3 * hf + hh] = act[0, pl.ds(pl.multiple_of(64 * c, 64), 64), 0:256]
            tgs[3 * hf + hh] = act[0, pl.ds(pl.multiple_of(64 * (1 - c), 64), 64), 0:256]
    swap_tg.start()
    wait_recv(z1)
    z2 = collect(0, 48, zr, zs, 2)
    start(z2)
    wait_recv(z3)
    z4 = collect(192, 16, zr2, zs2, 3)
    start(z4)
    swap_tg.wait_recv()
    tg[1 - c] = tg_r[...]
    wait_recv(z2)
    wait_recv(z4)
    for d in range(8):
        cols = slice(HALF * (d % 2), HALF * (d % 2) + HALF)
        act[0, 48 * (d // 2) : 48 * (d // 2) + 48, cols] = zs[d].astype(F32)
        act[0, 192 + 16 * (d // 2) : 208 + 16 * (d // 2), cols] = zs2[d].astype(F32)
    for cc, ref in ((c, post.at[0]), (1 - c, post.at[1])):
        base = pl.multiple_of(24 * cc, 8)
        ref[:, 0:D] = act[0, pl.ds(base, 24)]
        ref[:, D : 2 * D] = act[0, pl.ds(base + 48, 24)]
        ref[:, 2 * D : 3 * D] = act[0, pl.ds(base + 192, 24)]
    swap_post = to_sib(post.at[1], post.at[2], 11)
    swap_post.start()
    d_down[...] = act[0, 96:192]
    gsum[...] = jnp.concatenate(
        [act[0, 240:242] + act[0, 242:244], jnp.zeros((6, D), F32)], axis=0
    )
    swap_post.wait_recv()
    first_core = (c == 0).astype(F32)
    pair = (
        post[0] * first_core + post[2] * (1.0 - first_core),
        post[2] * first_core + post[0] * (1.0 - first_core),
    )
    for m in range(4):
        block = jnp.concatenate([p[:, HALF * m : HALF * m + HALF] for p in pair], axis=1).astype(BF)
        d_up[:, D * m : D * m + D] = dot_nt(block, perm[...])
    for cc in range(2):
        cols = slice(HALF * cc, HALF * cc + HALF)
        d_out[:, cols] = pair[cc][:, 2 * D : 2 * D + HALF]
        d_value[:, cols] = pair[cc][:, 2 * D + HALF : 3 * D]
    for copy in (
        swap_pre, swap_tok, swap_tab, swap_og, swap_wo, swap_mix, swap_ng, swap_tg, swap_post
    ):
        copy.wait_send()
    for group in g1 + g2 + w1 + w2 + ups + dns + wz_up[:3] + wz_dn[:3] + [
        wz_up[3][:1], wz_dn[3][1:],
        s1x, s1y, s2x, s2y, a1x, a1y, a2x, a2y, gain1, gain2, z1, z2, z3, z4
    ]:
        wait_send(group)


def finish(out, input_grad, d_value, d_out, d_up, d_down, gsum, tg, *outs):
    for src, dst in zip((out, input_grad, d_value, d_out, d_up, d_down, tg), outs):
        dst[...] = src[...]
    s = lax.axis_index("seq")
    row = lax.broadcasted_iota(jnp.int32, (D, 128), 0)
    lane = lax.broadcasted_iota(jnp.int32, (D, 128), 1)
    pick = jnp.where(row == lane + 24 * s, 1.0, 0.0)
    for i in range(2):
        got = jnp.dot(gsum[...], pick, precision=lax.Precision.HIGHEST, preferred_element_type=F32)
        outs[7 + i][...] = got[i, 0:24]


def vmem(*shape, kind=BF):
    return pltpu.VMEM(shape, kind)


def dma(*shape):
    return pltpu.SemaphoreType.DMA(shape)


IN_VMEM = pl.BlockSpec(memory_space=pltpu.VMEM)


def per_device(tokens, lengths, w_value, w_out, w_up, w_down, gain_mix, gain_ffn, mix_table, out_grad):
    sd = jax.ShapeDtypeStruct
    shapes = [
        sd((2, 64, D), BF), sd((2, 64, D), F32), sd((24, D), F32), sd((24, D), F32), sd((24, 4 * D), F32),
        sd((96, D), F32), sd((8, D), F32), sd((2, HH, 64, 256), F32),
    ]
    raw = pl.pallas_call(
        layer,
        name="layer",
        out_shape=shapes,
        in_specs=[pl.BlockSpec(memory_space=pltpu.SMEM)] + [IN_VMEM] * 8 + [pl.BlockSpec(memory_space=pl.ANY)],
        out_specs=[IN_VMEM] * 8,
        scratch_shapes=[
            vmem(D, D), vmem(2, 24, D + HALF, kind=F32), vmem(2, 24, D + HALF, kind=F32),
            vmem(2, 2, 64, D), vmem(2, 2, 64, D), vmem(HH, 2, 64, 2048),
            vmem(4, 4, 48, HALF), vmem(2, 4, 4, 48, HALF), vmem(8, 4, 4, 48, HALF),
            vmem(4, 4, 3, ROWS, 128), vmem(4, 4, 3, ROWS, 128), vmem(3, 4, 3, ROWS, 128), vmem(3, 4, 3, ROWS, 128),
            vmem(4, 3, ROWS, 128), vmem(4, 3, ROWS, 128), vmem(3, 3, ROWS, 128), vmem(3, 3, ROWS, 128),
            vmem(2, HALF, 128, kind=F32), vmem(2, 8, 128, kind=F32), vmem(2, 2, 128, HALF), vmem(HH, ROWS, 128),
            vmem(HH, 128, 128), vmem(2, 128, 128, kind=F32), vmem(256, D), vmem(256, D, kind=F32), vmem(256, D),
            vmem(256, D), vmem(2, 256, D), vmem(2, 256, D), vmem(2, 256, D, kind=F32),
            vmem(2, 2, 64, D, kind=F32), vmem(2, 64, D, kind=F32), vmem(2, 2, 64, D, kind=F32),
            vmem(2, 2, 64, D, kind=F32), vmem(2, 2, 64, D, kind=F32),
            vmem(2, 4, 4, 48, D), vmem(4, 4, 96, HALF), vmem(4, 4, 96, HALF), vmem(4, 4, 48, HALF),
            vmem(4, 4, 48, HALF), vmem(4, 4, 3, ROWS, 128), vmem(4, 4, 3, ROWS, 128),
            vmem(2, 3, 4, 48, D), vmem(2, 3, 4, 96, HALF), vmem(2, 3, 4, 48, HALF),
            vmem(2, 4, 48, D), vmem(2, 4, 96, HALF), vmem(2, 4, 48, HALF),
            vmem(2, 3, 48, D), vmem(2, 3, 96, HALF), vmem(2, 3, 48, HALF),
            vmem(16, D), vmem(4, 4, 16, D),
            vmem(2, 4, 3, 128, 256), vmem(2, 4, 3, 128, 256), vmem(2, 4, 3, 128, 256), vmem(2, 4, 3, 128, 256),
            vmem(HH, 64, 256, kind=F32), vmem(HH, 64, 256, kind=F32), vmem(2, HALF, 128, kind=F32),
            vmem(2, 2, 64, D, kind=F32), vmem(256, D), vmem(7, 48, HALF), vmem(7, 16, HALF), vmem(8, 48, HALF), vmem(8, 16, HALF),
            vmem(3, 24, 3 * D, kind=F32),
            dma(2, 12), dma(2, 4, 2, 3), dma(2, 2, 4, 2), dma(2, 2, 2, 3), pltpu.SemaphoreType.DMA, dma(2, 2, 2, 3),
            dma(2, 6, 2, 3), dma(2, 2, 3), dma(2, 2, 4), dma(2, 2, 4), dma(2, 4, 7),
        ],
        compiler_params=pltpu.CompilerParams(
            collective_id=0, has_side_effects=True, vmem_limit_bytes=63 << 20
        ),
    )(lengths, tokens, out_grad, w_value, w_out, w_up, w_down, gain_mix, gain_ffn, mix_table)
    out, input_grad, d_value, d_out, d_up, d_down, tg, mix_gain, ffn_gain = pl.pallas_call(
        finish,
        name="finish",
        out_shape=shapes[:6] + [shapes[7], sd((24,), F32), sd((24,), F32)],
        in_specs=[IN_VMEM] * 8,
        out_specs=[IN_VMEM] * 9,
    )(*raw)
    return (
        out, input_grad, d_value, d_out, d_up, d_down, mix_gain, ffn_gain, tg.reshape(HEADS, 64, 256),
    )


def solution(mesh):
    return jax.shard_map(
        per_device,
        mesh=mesh,
        in_specs=(
            P("dp", "seq", None),
            P("dp"),
            P("seq", None),
            P("seq", None),
            P("seq", None),
            P("seq", None),
            P(),
            P(),
            P(None, "seq", None),
            P("dp", "seq", None),
        ),
        out_specs=(
            P("dp", "seq", None),
            P("dp", "seq", None),
            P("seq", None),
            P("seq", None),
            P("seq", None),
            P("seq", None),
            P("seq"),
            P("seq"),
            P(None, "seq", "dp"),
        ),
        check_vma=False,
    )
```

time: 217 us -> 184 us (0.85)
  local copies, waits for them, and re-layouts: 15 us -> 0 us
  Pallas kernels: 197 us -> 183 us
  other arithmetic: 4.03 us -> 0 us
    pallas_call x2, Pallas kernels: 197 us -> 183 us  [the longest x1 180 us: per_device(): pl.pallas_call(layer, name='layer', out_shape=shapes, in_specs=[pl.BlockS...]
    reshape x8 -> x0, local copies, waits for them, and re-layouts: 7.29 us -> none  [the longest x3 2.85 us: per_device(): rows.reshape(2, 2, 24, 16, 48).transpose(2, 3, 0, 1, 4).reshape(24, 3072)]
    slice x4 -> x0, local copies, waits for them, and re-layouts: 2.69 us -> none  [the longest x1 1.02 us: per_device(): res[:, 0:96].reshape(2, 2, 48, D)]
    convert_element_type x4 -> x0, other arithmetic: 2.65 us -> none  [the longest x1 1.1 us: per_device(): own = lax.dynamic_index_in_dim(res, c, 0, False).astype(F32)]
    unnamed x9 -> x0, local copies, waits for them, and re-layouts: 2.31 us -> none
where the time goes in v2:
time: 184 us
  Pallas kernels  183 us (99%)
    pallas_call x1, Pallas kernels, per_device(): pl.pallas_call(layer, name='layer', out_shape=shapes, in_specs=[pl.BlockS...  180 us

profile of v2, /device:TPU:1, one launch (start us, length us, event | category | flops | bytes accessed | tf_op | source)
XLA Modules:
  0.0 184.0 jit_solution(17776614092946492126)
XLA Ops:
  0.6 180.0 %layer.1 = (bf16[2,64,768]{2,1,0:T(8,128)(2,1)}, f32[2,64,768]{2,1,0:T(8,128)}, f32[24,768]{1,0:T(8,128)}, f32[24,768]{1,0:T(8,128)}, f32[24,3072]{1,0:T(8,128)}...) custom-call(s32[2]{0:T(128)} %lengths.1, bf16[2,64,768]{2,1,0:T(8,128)(2,1)} %tokens.1, ...), custom_call_target="tpu_custom_call" | custom-call | tf_op jit(solution)/shard_map/layer/pallas_call | solution.py:695
  180.7 3.3 %finish.1 = (bf16[2,64,768]{2,1,0:T(8,128)(2,1)}, f32[2,64,768]{2,1,0:T(8,128)}, f32[24,768]{1,0:T(8,128)}, f32[24,768]{1,0:T(8,128)}, f32[24,3072]{1,0:T(8,128)...) custom-call(bf16[2,64,768]{2,1,0:T(8,128)(2,1)} %get-tuple-element.26.out, ...), custom_call_target="tpu_custom_call" | custom-call | tf_op jit(solution)/shard_map/finish/pallas_call | solution.py:729

commit v3 on v2

--- a/solution.py
+++ b/solution.py
@@ -14,7 +14,7 @@
 BF = jnp.bfloat16
 F32 = jnp.float32
 OFFS = (1, 3, 2)
-ROWS = 144
+ROWS = 400
 GELU_C = 0.7978845608028654
 GELU_A = 0.044715
 
@@ -167,10 +167,11 @@
     out, input_grad, d_value, d_out, d_up, d_down, gsum, tg,
     perm, pre, got, tok, og, e, wv, wo_all, wz,
     ux, uy, rx, ry, mx, my, rx2, ry2, mt, rr, mix, vt, vals, mcol, normed, middle, nf, bgs, hid, pgr, act,
-    part, part_r, fng, fng_r, mgrad, dwu, dwda, dwdb, dwo, dwv, gx, gy,
-    ru, rd, rl, mu, md, ml, ru2, rd2, rl2, gs, gr, up_s, up_r, dn_s, dn_r, tgs, tg_r, vgt, ng_r,
-    sums, zr, zr2, zs, zs2, post,
-    s_sib, s_ag, s_wz, s_u, s_loc, s_g, s_w, s_gain, s_up, s_dn, s_z,
+    part, part_r, fng, fng_r, mgrad, dwu, dwd, dws, dwo, dwv, gx, gy,
+    ru, rl, mu, ml, ru2, rl2, dfar, dnear, dlast, dsum, gs, gr, up_s, up_r, dn_s, dn_r, tgs, tg_r, vgt, ng_r,
+    up_sum, rest, zr_up, zr_rest, half_up, half_down, half_rest, other_up, other_down, other_rest,
+    zs_up, zs_down, zs_rest, post,
+    s_sib, s_ag, s_wz, s_u, s_loc, s_g, s_w, s_d, s_gain, s_up, s_dn, s_z,
 ):
     z, x, y, c = here()
     sib = at(z, x, y, 1 - c)
@@ -192,60 +193,48 @@
     quad = jnp.where(low >= 48, 1, 0) + jnp.where(low >= 96, 1, 0) + jnp.where(low >= 144, 1, 0)
     origin = low + 144 * quad + 96 * odd + 48 * half
     perm[...] = jnp.where(lax.broadcasted_iota(jnp.int32, (D, D), 0) == origin, 1.0, 0.0).astype(BF)
-    block = pl.multiple_of(D * lax.rem(z, 4), D)
-    mine = dot(w_up[:, pl.ds(block, D)], perm[...])
+    par = lax.rem(z, 2)
     for cc in range(2):
         cols = slice(HALF * cc, HALF * cc + HALF)
         pre[cc, :, 0:HALF] = w_out[:, cols].astype(F32)
         pre[cc, :, HALF:D] = w_value[:, cols].astype(F32)
-        pre[cc, :, D : D + HALF] = mine[:, cols]
+    for i in range(2):
+        mine = dot(w_up[:, pl.ds(pl.multiple_of(D * (2 * par + i), D), D)], perm[...])
+        for cc in range(2):
+            pre[cc, :, D + HALF * i : D + HALF * i + HALF] = mine[:, HALF * cc : HALF * cc + HALF]
     meet(count)
     swap_pre = to_sib(pre.at[1 - c], got.at[c], 0)
     swap_tok = to_sib(tokens, tok.at[:, c], 1)
     swap_tab = to_sib(table.at[pl.ds(6 * (1 - c), 6)], e.at[:, c], 2)
     swap_og = to_sib(out_grad, og.at[:, c], 3)
-    start([swap_pre, swap_tok, swap_tab, swap_og])
+    swap_pre.start()
     got[c] = pre[c]
     tok[:, c] = tokens[...]
     og[:, c] = out_grad[...]
-    wz_x = wz.at[z, :, :, pl.ds(0, 32)]
-    wz_y = wz.at[z, :, :, pl.ds(32, 16)]
-    bufs = ((wv, "x"), (wo, "y"), (wz_x, "x"), (wz_y, "y"))
+    for b in range(2):
+        rows = pl.ds(pl.multiple_of(48 * par, 16), 48)
+        wz[4 + 2 * par + b, x, y] = w_down[rows, HALF * b : HALF * b + HALF]
+    bufs = (
+        (wv, "x"), (wo, "y"), (wz.at[2 * par], "x"), (wz.at[2 * par + 1], "y"),
+        (wz.at[4 + 2 * par], "x"), (wz.at[5 + 2 * par], "y"),
+    )
     g1 = [gather_one(buf, first, s_ag.at[:, i]) for i, (buf, first) in enumerate(bufs)]
     g2 = [gather_two(buf, first, s_ag.at[:, i]) for i, (buf, first) in enumerate(bufs)]
     swap_pre.wait_recv()
-    shard = got[...].reshape(48, D + HALF).astype(BF)
+    shard = got[...].reshape(48, 2 * D).astype(BF)
     wo[x, y] = shard[:, 0:HALF]
     wv[x, y] = shard[:, HALF:D]
-
-    @pl.when(z < 4)
-    def _():
-        wz[z, x, y] = shard[:, D : D + HALF]
-
-    @pl.when(z >= 4)
-    def _():
-        rows = pl.ds(pl.multiple_of(48 * (lax.rem(z, 4) // 2), 16), 48)
-        cols = pl.ds(pl.multiple_of(HALF * lax.rem(z, 2), 128), HALF)
-        wz[z, x, y] = w_down[rows, cols]
-
-    for i in range(4):
+    for i in range(2):
+        wz[2 * par + i, x, y] = shard[:, D + HALF * i : D + HALF * i + HALF]
+    for i in range(6):
         start(g1[i])
-
-    def slab(t, half, sign):
-        return wz.at[lax.rem(z + 8 - sign * t, 8), pl.ds(2 * half, 2)]
-
-    wz_up = [[remote(slab(t, h, 1), slab(t, h, 1), s_wz, (0, t, h), up) for h in range(2)] for t in range(4)]
-    wz_dn = [[remote(slab(t, h, -1), slab(t, h, -1), s_wz, (1, t, h), down) for h in range(2)] for t in range(4)]
-
-    def pass_on(t, h):
-        wz_up[t - 1][h].wait_recv()
-        if t < 3 or h == 0:
-            wz_up[t][h].start()
-        wz_dn[t - 1][h].wait_recv()
-        if t < 3 or h == 1:
-            wz_dn[t][h].start()
-
-    for i in range(4):
+    start([swap_tok, swap_tab, swap_og])
+    share = [
+        remote(wz.at[4 * i + 2 * par + j], wz.at[4 * i + 2 * par + j], s_wz, (i, j), (up, down)[j])
+        for i in range(2)
+        for j in range(2)
+    ]
+    for i in range(6):
         wait_recv(g1[i])
         start(g2[i])
     swap_tok.wait_recv()
@@ -267,20 +256,16 @@
         return carry
 
     lax.fori_loop(0, HH, exps, 0)
-    wait_recv(g2[2])
-    wait_recv(g2[3])
-    for h in range(2):
-        wz_up[0][h].start()
-        wz_dn[0][h].start()
     wait_recv(g2[0])
     v = dot(normed[...], wv[...].reshape(D, HALF)).astype(BF).astype(F32)
     vall = flip(v) * jnp.concatenate(masks, axis=1)
-    ones = jnp.concatenate(masks + [jnp.zeros((14, 128), F32)], axis=0)
     for h in range(HH):
         block = jnp.concatenate(
             [vall[64 * h : 64 * h + 64, 0:128], vall[64 * h : 64 * h + 64, 128:256]], axis=0
         )
-        vt[h] = jnp.concatenate([block, ones], axis=0).astype(BF)
+        place = [jnp.zeros((2, 128), F32)] * (h % 3) + masks
+        place = place + [jnp.zeros((14 - 2 * (h % 3), 128), F32)]
+        vt[h] = jnp.concatenate([block] + place, axis=0).astype(BF)
         vals[h] = flip(block).astype(BF)
 
     s1x = scatter_one(ux, rx, "x", s_u.at[:, 0])
@@ -289,31 +274,36 @@
         xx = lax.rem(x + k, 4)
         yy = lax.rem(y + k, 4)
 
-        def head_x(h, carry, xx=xx):
-            cols = pl.ds(pl.multiple_of(512 * xx, 512), 512)
+        cols = pl.ds(pl.multiple_of(512 * xx, 512), 512)
+        extra = jnp.zeros((16, 512), F32)
+        for h in range(3):
             u = dot(vt[h], e[h, :, :, cols].reshape(128, 512))
+            extra = extra + u[128:144]
             for j in range(4):
-                ux[xx, j, h] = u[:, 128 * j : 128 * j + 128].astype(BF)
-            return carry
-
-        def head_y(h, carry, yy=yy):
-            for j in range(4):
-                cols = pl.ds(pl.multiple_of(512 * j + 128 * yy, 128), 128)
-                uy[j, yy, h] = dot(vt[h + 3], e[h + 3, :, :, cols].reshape(128, 128)).astype(BF)
-            return carry
-
-        lax.fori_loop(0, 3, head_x, 0)
+                ux[xx, j, 128 * h : 128 * h + 128] = u[0:128, 128 * j : 128 * j + 128].astype(BF)
+        for j in range(4):
+            ux[xx, j, 384:400] = extra[:, 128 * j : 128 * j + 128].astype(BF)
         if i < 3:
             s1x[i].start()
-        lax.fori_loop(0, 3, head_y, 0)
+        for j in range(4):
+            cols = pl.ds(pl.multiple_of(512 * j + 128 * yy, 128), 128)
+            extra = jnp.zeros((16, 128), F32)
+            for h in range(3):
+                u = dot(vt[h + 3], e[h + 3, :, :, cols].reshape(128, 128))
+                extra = extra + u[128:144]
+                uy[j, yy, 128 * h : 128 * h + 128] = u[0:128].astype(BF)
+            uy[j, yy, 384:400] = extra.astype(BF)
         if i < 3:
             s1y[i].start()
-    pass_on(1, 0)
+    for i in (0, 1):
+        wait_recv(g2[2 + i])
+        share[i].start()
     wait_recv(g2[1])
     swap_wo = to_sib(wo, wo, 5)
     swap_wo.start()
-    pass_on(1, 1)
-    pass_on(2, 0)
+    for i in (2, 3):
+        wait_recv(g2[2 + i])
+        share[i].start()
     s2x = scatter_two(mx, rx2, "x", s_u.at[:, 0])
     s2y = scatter_two(my, ry2, "y", s_u.at[:, 1])
     wait_recv(s1x)
@@ -322,17 +312,15 @@
     wait_recv(s1y)
     scatter_sum(uy, ry, my, "y")
     start(s2y)
-    pass_on(2, 1)
-    pass_on(3, 0)
     for half, (copies, mid, rcv, first) in enumerate(((s2x, mx, rx2, "x"), (s2y, my, ry2, "y"))):
         wait_recv(copies)
         total = scatter_end(mid, rcv, first)
         for hh in range(3):
             h = half * 3 + hh
             for b in range(2):
-                r = masks[b] / total[hh, 128 + b : 129 + b]
+                r = masks[b] / total[384 + 2 * hh + b : 385 + 2 * hh + b]
                 rr[b, h : h + 1] = r
-                mt[b, 64 * h : 64 * h + 64] = total[hh, 64 * b : 64 * b + 64] * r
+                mt[b, 64 * h : 64 * h + 64] = total[128 * hh + 64 * b : 128 * hh + 64 * b + 64] * r
     for b in range(2):
         mix[c, b] = flip(mt[b]).astype(BF)
     swap_mix = to_sib(mix.at[c], mix.at[c], 6)
@@ -353,9 +341,8 @@
     nf[...] = (mid_v * rms * gf).astype(BF)
     swap_og.wait_recv()
     grad = og[...].reshape(256, D)
-    pass_on(3, 1)
-    wz_up[3][0].wait_recv()
-    wz_dn[3][1].wait_recv()
+    share[0].wait_recv()
+    share[1].wait_recv()
     for hf in range(2):
         hp = jnp.concatenate([dot(nf[...], wz[2 * hf + i].reshape(D, HALF)) for i in range(2)], axis=1)
         t = jnp.tanh(GELU_C * (hp + GELU_A * hp * hp * hp))
@@ -368,15 +355,31 @@
         return jnp.concatenate([wz[4 + b, m].reshape(192, HALF), wz[6 + b, m].reshape(192, HALF)], axis=0)
 
     lots = (
-        (dwda, rd.at[0], md.at[0], rd2.at[0], "x"),
-        (dwdb, rd.at[1], md.at[1], rd2.at[1], "y"),
         (dwu.at[0], ru.at[0], mu.at[0], ru2.at[0], "x"),
         (dwu.at[1], ru.at[1], mu.at[1], ru2.at[1], "y"),
-        (dwo, rl.at[0], ml.at[0], rl2.at[0], "x"),
-        (dwv, rl.at[1], ml.at[1], rl2.at[1], "y"),
+        (dws, rl.at[0], ml.at[0], rl2.at[0], "x"),
+        (dwo, rl.at[1], ml.at[1], rl2.at[1], "y"),
+        (
+            dwv.at[:, :, pl.ds(0, 32)], rl.at[2, :, :, pl.ds(0, 32)], ml.at[2, :, pl.ds(0, 32)],
+            rl2.at[2, :, pl.ds(0, 32)], "x",
+        ),
+        (
+            dwv.at[:, :, pl.ds(32, 16)], rl.at[2, :, :, pl.ds(32, 16)], ml.at[2, :, pl.ds(32, 16)],
+            rl2.at[2, :, pl.ds(32, 16)], "y",
+        ),
     )
     w1 = [scatter_one(lot[0], lot[1], lot[4], s_w.at[:, i]) for i, lot in enumerate(lots)]
     w2 = [scatter_two(lot[2], lot[3], lot[4], s_w.at[:, i]) for i, lot in enumerate(lots)]
+
+    def dw_part(shift, h):
+        return dwd.at[lax.rem(z + 8 + shift, 4), pl.ds(2 * h, 2)]
+
+    ways = (up, down)
+    far = [remote(dw_part(2 - 4 * h, h), dfar.at[h], s_d, (0, h), ways[h]) for h in range(2)]
+    near = [remote(dw_part(2 * h - 1, h), dnear.at[h], s_d, (1, h), ways[1 - h]) for h in range(2)]
+    last = [remote(dsum.at[h], dlast.at[h], s_d, (2, h), ways[h]) for h in range(2)]
+    share[2].wait_recv()
+    share[3].wait_recv()
     for hf in range(2):
         for i in range(2):
             m = 2 * hf + i
@@ -388,13 +391,15 @@
     swap_fng = to_sib(fng, fng_r, 7)
     swap_fng.start()
     for hf in range(2):
-        dwd = dot(flip(hid[hf]), grad).astype(BF)
+        grad_w = dot(flip(hid[hf]), grad).astype(BF)
         for i in range(2):
             for a in range(2):
                 for q in range(4):
                     base = HALF * i + 192 * a + 48 * q
-                    dwda[2 * hf + i, q, 48 * a : 48 * a + 48] = dwd[base : base + 48, 0:HALF]
-                    dwdb[2 * hf + i, q, 48 * a : 48 * a + 48] = dwd[base : base + 48, HALF:D]
+                    for b in range(2):
+                        dwd[2 * a + b, 2 * hf + i, q] = grad_w[base : base + 48, HALF * b : HALF * b + HALF]
+    start(far)
+    start(near)
     swap_fng.wait_recv()
     full = (fng[...] + fng_r[...]).reshape(256, D)
     mid_v = middle[...]
@@ -418,15 +423,16 @@
             r = rr[b, h : h + 1]
             deltas.append(jnp.sum(rows * mt[b, 64 * h : 64 * h + 64], axis=0, keepdims=True) * r)
             own = gx if h < 3 else gy
-            own[x, y, h % 3, 64 * b : 64 * b + 64] = (rows * r).astype(BF)
-    for h in range(HH):
-        d0, d1 = deltas[h], deltas[HH + h]
-        h0 = d0.astype(BF).astype(F32)
-        h1 = d1.astype(BF).astype(F32)
-        own = gx if h < 3 else gy
-        own[x, y, h % 3, 128:144] = jnp.concatenate(
-            [h0, h1, d0 - h0, d1 - h1, jnp.zeros((12, 128), F32)], axis=0
-        ).astype(BF)
+            base = 128 * (h % 3) + 64 * b
+            own[x, y, base : base + 64] = (rows * r).astype(BF)
+    for own, first in ((gx, 0), (gy, 3)):
+        rows = []
+        for h in range(first, first + 3):
+            d0, d1 = deltas[h], deltas[HH + h]
+            h0 = d0.astype(BF).astype(F32)
+            h1 = d1.astype(BF).astype(F32)
+            rows = rows + [h0, h1, d0 - h0, d1 - h1]
+        own[x, y, 384:400] = jnp.concatenate(rows + [jnp.zeros((4, 128), F32)], axis=0).astype(BF)
     a1x = gather_one(gx, "x", s_g.at[:, 0])
     a1y = gather_one(gy, "y", s_g.at[:, 1])
     a2x = gather_two(gx, "x", s_g.at[:, 0])
@@ -438,15 +444,17 @@
     start(a2x)
     wait_recv(a1y)
     start(a2y)
+    dwu[1] = dot(flip(nf[...]), pgr[1]).astype(BF).reshape(4, 4, 48, D)
     start(w1[0])
     start(w1[1])
-    dwu[1] = dot(flip(nf[...]), pgr[1]).astype(BF).reshape(4, 4, 48, D)
-    start(w1[2])
-    start(w1[3])
+    for h in range(2):
+        far[h].wait_recv()
+        dsum[h] = (dw_part(1 - 2 * h, h)[...].astype(F32) + dfar[h].astype(F32)).astype(BF)
+        last[h].start()
     bg_c = bgs[:, pl.ds(pl.multiple_of(HALF * c, 128), HALF)]
     for i in range(2):
         dwo[pl.ds(2 * i, 2)] = dot(flip(mixed[i]), bg_c).astype(BF).reshape(2, 4, 48, HALF)
-    start(w1[4])
+    start(w1[3])
     for hf in range(2):
         down_w = [jnp.concatenate([down_rows(2 * hf, b), down_rows(2 * hf + 1, b)], axis=0) for b in range(2)]
         more = jnp.concatenate([dot(hid[hf], w) for w in down_w], axis=1).reshape(2, 2, 64, D)
@@ -457,6 +465,12 @@
     fng[...] = middle[...].reshape(2, 2, 64, D)
     swap_part.wait_recv()
     out[...] = (fng[:, c] + (part[:, c] + part_r[...])).astype(BF)
+    for h in range(2):
+        near[h].wait_recv()
+        last[h].wait_recv()
+        total = dw_part(0, h)[...].astype(F32) + dnear[h].astype(F32) + dlast[h].astype(F32)
+        dws[pl.ds(2 * h, 2)] = total.astype(BF)
+    start(w1[2])
     wait_recv(a2x)
     wait_recv(a2y)
 
@@ -468,10 +482,10 @@
             pair = []
             for i in range(2):
                 k = 2 * d + i
-                g = buf[k // 4, lax.rem(k, 4), hh]
+                g = buf[k // 4, lax.rem(k, 4), 128 * hh : 128 * hh + 128]
                 cols = pl.ds(pl.multiple_of(256 * d + 128 * i, 128), 128)
-                extra = g[128:144].astype(F32)
-                s = dot(vals[h], g[0:128])
+                extra = buf[k // 4, lax.rem(k, 4), 384:400].astype(F32)[4 * hh : 4 * hh + 4]
+                s = dot(vals[h], g)
                 s = s - mcol[0] * (extra[0:1] + extra[2:3])
                 s = s - mcol[1] * (extra[1:2] + extra[3:4])
                 pair.append(s * e[h, :, :, cols].reshape(128, 128).astype(F32))
@@ -509,12 +523,13 @@
         total = jnp.zeros((128, 128), F32)
         for k in range(16):
             total = total + dot_nt(
-                buf[k // 4, k % 4, h % 3, 0:128], e[h, :, :, 128 * k : 128 * k + 128].reshape(128, 128)
+                buf[k // 4, k % 4, 128 * (h % 3) : 128 * (h % 3) + 128], e[h, :, :, 128 * k : 128 * k + 128].reshape(128, 128)
             )
         for b in range(2):
             vgt[b, 64 * h : 64 * h + 64] = total[64 * b : 64 * b + 64] * masks[b]
     vg = jnp.concatenate([flip(vgt[b]) for b in range(2)], axis=0).astype(BF)
     dwv[...] = dot(flip(normed[...]), vg).astype(BF).reshape(4, 4, 48, HALF)
+    start(w1[4])
     start(w1[5])
     swap_part.wait_send()
     part[...] = dot_nt(vg, wv[...].reshape(D, HALF)).reshape(2, 2, 64, D)
@@ -544,63 +559,79 @@
         scatter_sum(src, rcv, mid, first)
         start(w2[i])
 
-    def last_sum(i, rows, cols):
+    def last_sum(i):
         wait_recv(w2[i])
         _, _, mid, rcv, first = lots[i]
-        sums[rows, cols] = scatter_end(mid, rcv, first).astype(BF)
-
-    def spread(base, rows, buf, i):
-        def chunk(d):
-            return sums.at[
-                pl.ds(pl.multiple_of(base + rows * (d // 2), 16), rows),
-                pl.ds(pl.multiple_of(HALF * lax.rem(d, 2), 128), HALF),
-            ]
-
-        return [
-            remote(
-                chunk(lax.rem(z + k, 8)), buf.at[k - 1], s_z, (i, k - 1), at(lax.rem(z + k, 8), x, y, c)
-            )
-            for k in range(1, 8)
-        ]
-
-    def collect(base, rows, buf, res, i):
-        total = sums[
-            pl.ds(pl.multiple_of(base + rows * (z // 2), 16), rows),
-            pl.ds(pl.multiple_of(HALF * lax.rem(z, 2), 128), HALF),
-        ].astype(F32)
-        for k in range(7):
-            total = total + buf[k].astype(F32)
-        res[z] = total.astype(BF)
-        return [
-            remote(res.at[z], res.at[z], s_z, (i, k - 1), at(lax.rem(z + k, 8), x, y, c))
-            for k in range(1, 8)
-        ]
+        return scatter_end(mid, rcv, first)
+
+    def z_send(src, dst, i, j, k):
+        return remote(src, dst, s_z, (i, j), at(lax.rem(z + k, 8), x, y, c))
+
+    q = lax.rem(z, 4)
+
+    def up_part(d):
+        return up_sum.at[:, pl.ds(pl.multiple_of(HALF * lax.rem(d, 4), 128), HALF)]
+
+    def rest_part(d):
+        return rest.at[pl.ds(pl.multiple_of(16 * lax.rem(d, 4), 16), 16)]
+
+    def z_first(part, buf, i, ks):
+        return [z_send(part(z + k), buf.at[j], i, j, k) for j, k in enumerate(ks)]
+
+    def z_half(part, buf, res):
+        total = part(z)[...].astype(F32)
+        for j in range(3):
+            total = total + buf[j].astype(F32)
+        res[...] = total.astype(BF)
+
+    def z_swap(half, other, i):
+        return z_send(half, other, i, 3, 4)
+
+    def z_last(half, other, full, i, ks):
+        full[q] = (half[...].astype(F32) + other[...].astype(F32)).astype(BF)
+        return [z_send(full.at[q], full.at[q], i, 4 + j, k) for j, k in enumerate(ks)]
 
     middle_sum(0)
     middle_sum(1)
     step(2)
     middle_sum(2)
     middle_sum(3)
+    for i in range(2):
+        up_sum[:, D * i : D * i + D] = last_sum(i).astype(BF)
+    z_up1 = z_first(up_part, zr_up, 0, (1, 2, 7))
+    start(z_up1)
     middle_sum(4)
     middle_sum(5)
     wait_recv(gain1)
     start(gain2)
     step(3)
-    last_sum(0, slice(96, 192), slice(0, HALF))
-    last_sum(1, slice(96, 192), slice(HALF, D))
-    last_sum(2, slice(0, 48), slice(0, D))
-    last_sum(3, slice(48, 96), slice(0, D))
-    z1 = spread(0, 48, zr, 0)
-    start(z1)
-    last_sum(4, slice(192, 240), slice(0, HALF))
-    last_sum(5, slice(192, 240), slice(HALF, D))
+    half_down[...] = last_sum(2).astype(BF)
+    z_down2 = z_swap(half_down, other_down, 1)
+    z_down2.start()
+    wait_recv(z_up1)
+    z_half(up_part, zr_up, half_up)
+    z_up2 = z_swap(half_up, other_up, 0)
+    z_up2.start()
+    rest[0:48, 0:HALF] = last_sum(3).astype(BF)
+    rest[0:32, HALF:D] = last_sum(4).astype(BF)
+    rest[32:48, HALF:D] = last_sum(5).astype(BF)
     wait_recv(gain2)
     gtot = jnp.sum(gr[...].reshape(16, 16, D).astype(F32), axis=0)
     gains = gtot[0:2] + gtot[2:4]
     high = gains.astype(BF).astype(F32)
-    sums[240:256] = jnp.concatenate([high, gains - high, jnp.zeros((12, D), F32)], axis=0).astype(BF)
-    z3 = spread(192, 16, zr2, 1)
-    start(z3)
+    rest[48:64] = jnp.concatenate([high, gains - high, jnp.zeros((12, D), F32)], axis=0).astype(BF)
+    z_rest1 = z_first(rest_part, zr_rest, 2, (7, 6, 1))
+    start(z_rest1)
+    z_down2.wait_recv()
+    z_down3 = z_last(half_down, other_down, zs_down, 1, (1, 7, 6))
+    start(z_down3)
+    z_up2.wait_recv()
+    z_up3 = z_last(half_up, other_up, zs_up, 0, (1, 7, 2))
+    start(z_up3)
+    wait_recv(z_rest1)
+    z_half(rest_part, zr_rest, half_rest)
+    z_rest2 = z_swap(half_rest, other_rest, 2)
+    z_rest2.start()
     own = [table_part(z, hf) for hf in range(2)]
     swap_tg = to_sib(tgs, tg_r, 10)
     for hf in range(2):
@@ -614,31 +645,28 @@
             tg[c, 3 * hf + hh] = act[0, pl.ds(pl.multiple_of(64 * c, 64), 64), 0:256]
             tgs[3 * hf + hh] = act[0, pl.ds(pl.multiple_of(64 * (1 - c), 64), 64), 0:256]
     swap_tg.start()
-    wait_recv(z1)
-    z2 = collect(0, 48, zr, zs, 2)
-    start(z2)
-    wait_recv(z3)
-    z4 = collect(192, 16, zr2, zs2, 3)
-    start(z4)
-    swap_tg.wait_recv()
-    tg[1 - c] = tg_r[...]
-    wait_recv(z2)
-    wait_recv(z4)
-    for d in range(8):
-        cols = slice(HALF * (d % 2), HALF * (d % 2) + HALF)
-        act[0, 48 * (d // 2) : 48 * (d // 2) + 48, cols] = zs[d].astype(F32)
-        act[0, 192 + 16 * (d // 2) : 208 + 16 * (d // 2), cols] = zs2[d].astype(F32)
+    z_rest2.wait_recv()
+    z_rest3 = z_last(half_rest, other_rest, zs_rest, 2, (1, 7, 6))
+    start(z_rest3)
+    wait_recv(z_up3)
+    wait_recv(z_down3)
+    for a in range(2):
+        for b in range(2):
+            cols = slice(HALF * b, HALF * b + HALF)
+            act[0, 48 * a : 48 * a + 48, cols] = zs_up[2 * a + b].astype(F32)
+            d_down[48 * a : 48 * a + 48, cols] = zs_down[2 * a + b].astype(F32)
+    wait_recv(z_rest3)
+    act[0, 96:160] = zs_rest[...].reshape(64, D).astype(F32)
     for cc, ref in ((c, post.at[0]), (1 - c, post.at[1])):
         base = pl.multiple_of(24 * cc, 8)
         ref[:, 0:D] = act[0, pl.ds(base, 24)]
         ref[:, D : 2 * D] = act[0, pl.ds(base + 48, 24)]
-        ref[:, 2 * D : 3 * D] = act[0, pl.ds(base + 192, 24)]
+        ref[:, 2 * D : 3 * D] = act[0, pl.ds(base + 96, 24)]
     swap_post = to_sib(post.at[1], post.at[2], 11)
     swap_post.start()
-    d_down[...] = act[0, 96:192]
-    gsum[...] = jnp.concatenate(
-        [act[0, 240:242] + act[0, 242:244], jnp.zeros((6, D), F32)], axis=0
-    )
+    gsum[...] = jnp.concatenate([act[0, 144:146] + act[0, 146:148], jnp.zeros((6, D), F32)], axis=0)
+    swap_tg.wait_recv()
+    tg[1 - c] = tg_r[...]
     swap_post.wait_recv()
     first_core = (c == 0).astype(F32)
     pair = (
@@ -656,9 +684,10 @@
         swap_pre, swap_tok, swap_tab, swap_og, swap_wo, swap_mix, swap_ng, swap_tg, swap_post
     ):
         copy.wait_send()
-    for group in g1 + g2 + w1 + w2 + ups + dns + wz_up[:3] + wz_dn[:3] + [
-        wz_up[3][:1], wz_dn[3][1:],
-        s1x, s1y, s2x, s2y, a1x, a1y, a2x, a2y, gain1, gain2, z1, z2, z3, z4
+    for group in g1 + g2 + w1 + w2 + ups + dns + [
+        share, far, near, last,
+        s1x, s1y, s2x, s2y, a1x, a1y, a2x, a2y, gain1, gain2,
+        z_up1, [z_up2], z_up3, [z_down2], z_down3, z_rest1, [z_rest2], z_rest3,
     ]:
         wait_send(group)
 
@@ -699,28 +728,30 @@
         in_specs=[pl.BlockSpec(memory_space=pltpu.SMEM)] + [IN_VMEM] * 8 + [pl.BlockSpec(memory_space=pl.ANY)],
         out_specs=[IN_VMEM] * 8,
         scratch_shapes=[
-            vmem(D, D), vmem(2, 24, D + HALF, kind=F32), vmem(2, 24, D + HALF, kind=F32),
+            vmem(D, D), vmem(2, 24, 2 * D, kind=F32), vmem(2, 24, 2 * D, kind=F32),
             vmem(2, 2, 64, D), vmem(2, 2, 64, D), vmem(HH, 2, 64, 2048),
             vmem(4, 4, 48, HALF), vmem(2, 4, 4, 48, HALF), vmem(8, 4, 4, 48, HALF),
-            vmem(4, 4, 3, ROWS, 128), vmem(4, 4, 3, ROWS, 128), vmem(3, 4, 3, ROWS, 128), vmem(3, 4, 3, ROWS, 128),
-            vmem(4, 3, ROWS, 128), vmem(4, 3, ROWS, 128), vmem(3, 3, ROWS, 128), vmem(3, 3, ROWS, 128),
-            vmem(2, HALF, 128, kind=F32), vmem(2, 8, 128, kind=F32), vmem(2, 2, 128, HALF), vmem(HH, ROWS, 128),
+            vmem(4, 4, ROWS, 128), vmem(4, 4, ROWS, 128), vmem(3, 4, ROWS, 128), vmem(3, 4, ROWS, 128),
+            vmem(4, ROWS, 128), vmem(4, ROWS, 128), vmem(3, ROWS, 128), vmem(3, ROWS, 128),
+            vmem(2, HALF, 128, kind=F32), vmem(2, 8, 128, kind=F32), vmem(2, 2, 128, HALF), vmem(HH, 144, 128),
             vmem(HH, 128, 128), vmem(2, 128, 128, kind=F32), vmem(256, D), vmem(256, D, kind=F32), vmem(256, D),
             vmem(256, D), vmem(2, 256, D), vmem(2, 256, D), vmem(2, 256, D, kind=F32),
             vmem(2, 2, 64, D, kind=F32), vmem(2, 64, D, kind=F32), vmem(2, 2, 64, D, kind=F32),
             vmem(2, 2, 64, D, kind=F32), vmem(2, 2, 64, D, kind=F32),
-            vmem(2, 4, 4, 48, D), vmem(4, 4, 96, HALF), vmem(4, 4, 96, HALF), vmem(4, 4, 48, HALF),
-            vmem(4, 4, 48, HALF), vmem(4, 4, 3, ROWS, 128), vmem(4, 4, 3, ROWS, 128),
-            vmem(2, 3, 4, 48, D), vmem(2, 3, 4, 96, HALF), vmem(2, 3, 4, 48, HALF),
-            vmem(2, 4, 48, D), vmem(2, 4, 96, HALF), vmem(2, 4, 48, HALF),
-            vmem(2, 3, 48, D), vmem(2, 3, 96, HALF), vmem(2, 3, 48, HALF),
+            vmem(2, 4, 4, 48, D), vmem(4, 4, 4, 48, HALF), vmem(4, 4, 48, HALF), vmem(4, 4, 48, HALF),
+            vmem(4, 4, 48, HALF), vmem(4, 4, ROWS, 128), vmem(4, 4, ROWS, 128),
+            vmem(2, 3, 4, 48, D), vmem(3, 3, 4, 48, HALF), vmem(2, 4, 48, D), vmem(3, 4, 48, HALF),
+            vmem(2, 3, 48, D), vmem(3, 3, 48, HALF),
+            vmem(2, 2, 4, 48, HALF), vmem(2, 2, 4, 48, HALF), vmem(2, 2, 4, 48, HALF), vmem(2, 2, 4, 48, HALF),
             vmem(16, D), vmem(4, 4, 16, D),
             vmem(2, 4, 3, 128, 256), vmem(2, 4, 3, 128, 256), vmem(2, 4, 3, 128, 256), vmem(2, 4, 3, 128, 256),
             vmem(HH, 64, 256, kind=F32), vmem(HH, 64, 256, kind=F32), vmem(2, HALF, 128, kind=F32),
-            vmem(2, 2, 64, D, kind=F32), vmem(256, D), vmem(7, 48, HALF), vmem(7, 16, HALF), vmem(8, 48, HALF), vmem(8, 16, HALF),
+            vmem(2, 2, 64, D, kind=F32), vmem(48, 2 * D), vmem(64, D), vmem(3, 48, HALF), vmem(3, 16, D),
+            vmem(48, HALF), vmem(48, HALF), vmem(16, D), vmem(48, HALF), vmem(48, HALF), vmem(16, D),
+            vmem(4, 48, HALF), vmem(4, 48, HALF), vmem(4, 16, D),
             vmem(3, 24, 3 * D, kind=F32),
-            dma(2, 12), dma(2, 4, 2, 3), dma(2, 2, 4, 2), dma(2, 2, 2, 3), pltpu.SemaphoreType.DMA, dma(2, 2, 2, 3),
-            dma(2, 6, 2, 3), dma(2, 2, 3), dma(2, 2, 4), dma(2, 2, 4), dma(2, 4, 7),
+            dma(2, 12), dma(2, 6, 2, 3), dma(2, 2, 2), dma(2, 2, 2, 3), pltpu.SemaphoreType.DMA, dma(2, 2, 2, 3),
+            dma(2, 6, 2, 3), dma(2, 3, 2), dma(2, 2, 3), dma(2, 2, 4), dma(2, 2, 4), dma(2, 3, 7),
         ],
         compiler_params=pltpu.CompilerParams(
             collective_id=0, has_side_effects=True, vmem_limit_bytes=63 << 20

time: 184 us -> 161 us (0.88)
  Pallas kernels: 183 us -> 160 us
    pallas_call x1, Pallas kernels: 180 us -> 157 us  [per_device(): pl.pallas_call(layer, name='layer', out_shape=shapes, in_specs=[pl.BlockS...]
where the time goes in v3:
time: 161 us
  Pallas kernels  160 us (99%)
    pallas_call x1, Pallas kernels, per_device(): pl.pallas_call(layer, name='layer', out_shape=shapes, in_specs=[pl.BlockS...  157 us
    pallas_call x1, Pallas kernels, per_device(): pl.pallas_call(finish, name='finish', out_shape=shapes[:6] + [shapes[7],...  3.29 us

profile of v3, /device:TPU:1, one launch (start us, length us, event | category | flops | bytes accessed | tf_op | source)
XLA Modules:
  0.0 160.7 jit_solution(2227868452088979210)
XLA Ops:
  0.6 156.7 %layer.1 = (bf16[2,64,768]{2,1,0:T(8,128)(2,1)}, f32[2,64,768]{2,1,0:T(8,128)}, f32[24,768]{1,0:T(8,128)}, f32[24,768]{1,0:T(8,128)}, f32[24,3072]{1,0:T(8,128)}...) custom-call(s32[2]{0:T(128)} %lengths.1, bf16[2,64,768]{2,1,0:T(8,128)(2,1)} %tokens.1, ...), custom_call_target="tpu_custom_call" | custom-call | tf_op jit(solution)/shard_map/layer/pallas_call | solution.py:724
  157.4 3.3 %finish.1 = (bf16[2,64,768]{2,1,0:T(8,128)(2,1)}, f32[2,64,768]{2,1,0:T(8,128)}, f32[24,768]{1,0:T(8,128)}, f32[24,768]{1,0:T(8,128)}, f32[24,3072]{1,0:T(8,128)...) custom-call(bf16[2,64,768]{2,1,0:T(8,128)(2,1)} %get-tuple-element.26.out, ...), custom_call_target="tpu_custom_call" | custom-call | tf_op jit(solution)/shard_map/finish/pallas_call | solution.py:760

commit v4 on v3

v4 whole, which is shorter than its diff:
```python
import jax
import jax.numpy as jnp
from jax import lax
from jax.experimental import pallas as pl
from jax.experimental.pallas import tpu as pltpu
from jax.sharding import PartitionSpec as P

D = 768
HALF = 384
HEADS = 12
HH = 6
EPS = 1e-06
MESH = pl.DeviceIdType.MESH
BF = jnp.bfloat16
F32 = jnp.float32
OFFS = (1, 3, 2)
ROWS = 400
SEMS = 204
GELU_C = 0.7978845608028654
GELU_A = 0.044715


def here():
    s = lax.axis_index("seq")
    return lax.axis_index("dp"), s // 8, (s // 2) % 4, s % 2


def at(z, x, y, c):
    return (z, (x * 4 + y) * 2 + c)


class Pool:
    def __init__(self, ref):
        self.ref, self.used = ref, 0

    def take(self):
        self.used += 1
        return self.ref.at[self.used - 1]


def remote(src, dst, send, recv, device):
    return pltpu.make_async_remote_copy(
        src_ref=src, dst_ref=dst, send_sem=send, recv_sem=recv, device_id=device, device_id_type=MESH
    )


class Batch:
    def __init__(self, pool, pieces, sent, got):
        self.send, self.recv = pool.take(), pool.take()
        self.all_sent, self.all_got = sent, got
        self.copies = [remote(src, dst, self.send, self.recv, device) for src, dst, device in pieces]

    def start(self):
        start(self.copies)

    def wait_recv(self):
        pltpu.make_async_copy(self.all_got, self.all_got, self.recv).wait()

    def wait_send(self):
        pltpu.make_async_copy(self.all_sent, self.all_sent, self.send).wait()


def along(first, k):
    z, x, y, c = here()
    if first == "x":
        return at(z, lax.rem(x + k, 4), y, c)
    return at(z, x, lax.rem(y + k, 4), c)


OTHER = {"x": "y", "y": "x"}


def own_at(first):
    _, x, y, _ = here()
    return x if first == "x" else y


def gather_one(buf, first, pool):
    _, x, y, _ = here()
    three = buf.at[0, pl.ds(0, 3)]
    return Batch(pool, [(buf.at[x, y], buf.at[x, y], along(first, k)) for k in OFFS], three, three)


def gather_two(buf, first, pool):
    _, x, y, _ = here()
    view = buf.at[:, y] if first == "x" else buf.at[x]
    three = buf.at[pl.ds(0, 3)]
    return Batch(pool, [(view, view, along(OTHER[first], k)) for k in OFFS], three, three)


class Bytes:
    def __init__(self, view, sem):
        self.view, self.sem = view, sem

    def wait_recv(self):
        pltpu.make_async_copy(self.view, self.view, self.sem).wait()

    wait_send = wait_recv


class Spread:
    def __init__(self, buf, first, pool):
        second = OTHER[first]
        mine = own_at(second)

        def part(k, half):
            place = lax.rem(mine + k, 4)
            pair = pl.ds(2 * half, 2)
            return buf.at[pair, place] if second == "y" else buf.at[place, pair]

        self.buf, self.send, self.recv = buf, pool.take(), pool.take()

        def send(k, half, way, recv):
            return remote(part(k, half), part(k, half), self.send, recv, along(second, way))

        self.early = [send(0, 0, 1, pool.take()), send(0, 1, 3, pool.take())]
        self.late = [send(0, 1, 1, self.recv), send(0, 0, 3, self.recv)]
        self.on = [send(3, 0, 1, self.recv), send(1, 1, 3, self.recv)]

    def start(self):
        start(self.early + self.late)

    def relay(self):
        for got, copy in zip(self.early, self.on):
            wait_recv([got])
            copy.start()

    def end(self):
        view = self.buf.at[pl.ds(0, 2)]
        wait_recv([Bytes(view, self.recv)])

    def sent(self):
        wait_send([Bytes(self.buf.at[pl.ds(0, 3)], self.send)])


class Sum:
    def __init__(self, src, rcv, first, pool):
        self.src, self.rcv, self.first = src, rcv, first
        self.send, self.recv = pool.take(), pool.take()
        self.mine = own_at(first)

        def send(k, half, slot, way, recv):
            return remote(
                self.part(k, half), rcv.at[slot, pl.ds(2 * half, 2)], self.send, recv, along(first, way)
            )

        self.far = [send(2, 0, 2, 1, pool.take()), send(2, 1, 2, 3, pool.take())]
        self.near = [send(1, 1, 0, 1, self.recv), send(3, 0, 1, 3, self.recv)]
        self.on = [send(1, 0, 0, 1, self.recv), send(3, 1, 1, 3, self.recv)]

    def part(self, k, half):
        place = lax.rem(self.mine + k, 4)
        pair = pl.ds(2 * half, 2)
        return self.src.at[place, pair] if self.first == "x" else self.src.at[pair, place]

    def start(self):
        start(self.far + self.near)

    def relay(self):
        for half in range(2):
            wait_recv([self.far[half]])
            part = self.part(1 + 2 * half, half)
            got = self.rcv[2, 2 * half : 2 * half + 2]
            part[...] = (part[...].astype(F32) + got.astype(F32)).astype(BF)
            self.on[half].start()

    def end(self, mid):
        wait_recv([Bytes(self.rcv.at[pl.ds(0, 2)], self.recv)])
        for j in range(4):
            own = self.src[self.mine, j] if self.first == "x" else self.src[j, self.mine]
            total = own.astype(F32) + self.rcv[0, j].astype(F32) + self.rcv[1, j].astype(F32)
            mid[j] = total.astype(BF)

    def sent(self):
        wait_send([Bytes(self.src.at[pl.ds(0, 3)], self.send)])


def scatter_two(mid, rcv, first, pool):
    second = OTHER[first]
    mine = own_at(second)
    pieces = [(mid.at[lax.rem(mine + k, 4)], rcv.at[i], along(second, k)) for i, k in enumerate(OFFS)]
    return Batch(pool, pieces, mid.at[pl.ds(0, 3)], rcv)


def scatter_end(mid, rcv, first):
    total = mid[own_at(OTHER[first])].astype(F32)
    for i in range(3):
        total = total + rcv[i].astype(F32)
    return total


def start(copies):
    for copy in copies:
        copy.start()


def wait_recv(copies):
    for copy in copies:
        copy.wait_recv()


def wait_send(copies):
    for copy in copies:
        copy.wait_send()


def signal(device):
    pl.semaphore_signal(
        pltpu.get_barrier_semaphore(), inc=1, device_id=device, device_id_type=MESH
    )


def greet():
    z, x, y, c = here()
    count = 0
    for k in range(1, 4):
        signal(at(z, lax.rem(x + k, 4), y, c))
        signal(at(z, x, lax.rem(y + k, 4), c))
        count += 2
    signal(at(z, x, y, 1 - c))
    count += 1
    for k in range(1, 8):
        signal(at(lax.rem(z + k, 8), x, y, c))
        count += 1
    return count


def meet(count):
    pl.semaphore_wait(pltpu.get_barrier_semaphore(), count)


def dot(a, b):
    return jnp.dot(a, b, preferred_element_type=F32)


def dot_nt(a, b):
    return lax.dot_general(a, b, (((1,), (1,)), ((), ())), preferred_element_type=F32)


def flip(a):
    return jnp.transpose(a)


def rms_of(v):
    return lax.rsqrt(jnp.mean(v * v, axis=-1, keepdims=True) + EPS)


def layer(
    lengths, tokens, out_grad, w_value, w_out, w_up, w_down, gain_mix, gain_ffn, table,
    out, input_grad, d_value, d_out, d_up, d_down, gsum, tg,
    perm, pre, got, tok, og, e, wv, wo_all, wz,
    ux, uy, rx, ry, mx, my, rx2, ry2, mt, rr, mix, vt, vals, mcol, normed, middle, nf, bgs, hid, pgr, act,
    part, part_r, fng, fng_r, mgrad, dwu, dwda, dwdb, dws, dwo, dwv, gx, gy,
    rd, rl, md, ml, rd2, rl2, dfar, dnear, dlast, dsum, gs, gr, up_s, up_r, dn_s, dn_r, tgs, tg_r, vgt, ng_r,
    down_sum, rest, zr_down, zr_rest, half_up, half_down, half_rest, other_up, other_down, other_rest,
    zs_up, zs_down, zs_rest, post_up, post_rest,
    out_s, ig_s, down_s, up_s_out, tgo, gsum_s, two_s,
    sems,
):
    z, x, y, c = here()
    sib = at(z, x, y, 1 - c)
    up = at(lax.rem(z + 1, 8), x, y, c)
    down = at(lax.rem(z + 7, 8), x, y, c)
    wo = wo_all.at[c]
    pool = Pool(sems)

    def to_sib(src, dst):
        return remote(src, dst, pool.take(), pool.take(), sib)

    saved = []

    def save(src, dst):
        copy = pltpu.make_async_copy(src, dst, pool.take())
        copy.start()
        saved.append(copy)

    count = greet()
    own_tab = pltpu.make_async_copy(table.at[pl.ds(6 * c, 6)], e.at[:, c], pool.take())
    own_tab.start()
    col = lax.broadcasted_iota(jnp.int32, (1, D), 1)
    odd = jnp.where(col >= HALF, 1, 0)
    low = col - HALF * odd
    half = jnp.where(low >= 192, 1, 0)
    low = low - 192 * half
    quad = jnp.where(low >= 48, 1, 0) + jnp.where(low >= 96, 1, 0) + jnp.where(low >= 144, 1, 0)
    origin = low + 144 * quad + 96 * odd + 48 * half
    perm[...] = jnp.where(lax.broadcasted_iota(jnp.int32, (D, D), 0) == origin, 1.0, 0.0).astype(BF)
    q = lax.rem(z, 4)
    for cc in range(2):
        cols = slice(HALF * cc, HALF * cc + HALF)
        pre[cc, :, 0:HALF] = w_out[:, cols].astype(F32)
        pre[cc, :, HALF:D] = w_value[:, cols].astype(F32)
    par = lax.rem(z, 2)
    for i in range(2):
        mine = dot(w_up[:, pl.ds(pl.multiple_of(D * (2 * par + i), D), D)], perm[...])
        for cc in range(2):
            pre[cc, :, D + HALF * i : D + HALF * i + HALF] = mine[:, HALF * cc : HALF * cc + HALF]
    meet(count)
    swap_pre = to_sib(pre.at[1 - c], got.at[c])
    swap_tok = to_sib(tokens, tok.at[:, c])
    swap_tab = to_sib(table.at[pl.ds(6 * (1 - c), 6)], e.at[:, c])
    swap_og = to_sib(out_grad, og.at[:, c])
    swap_pre.start()
    got[c] = pre[c]
    tok[:, c] = tokens[...]
    og[:, c] = out_grad[...]
    for b in range(2):
        rows = pl.ds(pl.multiple_of(48 * par, 16), 48)
        wz[4 + 2 * par + b, x, y] = w_down[rows, HALF * b : HALF * b + HALF]
    bufs = (
        (wv, "x"), (wo, "y"), (wz.at[2 * par], "x"), (wz.at[2 * par + 1], "y"),
        (wz.at[4 + 2 * par], "x"), (wz.at[5 + 2 * par], "y"),
    )
    g1 = [gather_one(buf, first, pool) for buf, first in bufs]
    g2 = [Spread(buf, first, pool) for buf, first in bufs]
    swap_pre.wait_recv()
    shard = got[...].reshape(48, 2 * D).astype(BF)
    wo[x, y] = shard[:, 0:HALF]
    wv[x, y] = shard[:, HALF:D]
    for i in range(2):
        wz[2 * par + i, x, y] = shard[:, D + HALF * i : D + HALF * i + HALF]
    order = (2, 3, 0, 1, 4, 5)
    for i in order:
        start([g1[i]])
    start([swap_tok, swap_tab, swap_og])

    share = [
        [
            remote(
                wz.at[4 * i + 2 * par + way], wz.at[4 * i + 2 * par + way], pool.take(), pool.take(), (up, down)[way]
            )
            for way in range(2)
        ]
        for i in range(2)
    ]
    for i in order:
        wait_recv([g1[i]])
        g2[i].start()
    swap_tok.wait_recv()
    values = tok[...].reshape(256, D).astype(F32)
    gm = gain_mix[...].reshape(1, D)
    gf = gain_ffn[...].reshape(1, D)
    normed[...] = (values * rms_of(values) * gm).astype(BF)
    place = (4 * x + y) * 128
    lane = lax.broadcasted_iota(jnp.int32, (1, 128), 1) + place
    row = lax.broadcasted_iota(jnp.int32, (128, 128), 0) + place
    masks = [jnp.where(lane < lengths[b], 1.0, 0.0) for b in range(2)]
    for b in range(2):
        mcol[b] = jnp.where(row < lengths[b], 1.0, 0.0)
    swap_tab.wait_recv()
    own_tab.wait()

    def exps(h, carry):
        e[h] = jnp.exp(e[h].astype(F32)).astype(BF)
        return carry

    lax.fori_loop(0, HH, exps, 0)
    for i in order:
        g2[i].relay()
    for way in range(2):
        g2[2 + way].end()
        share[0][way].start()
    g2[0].end()
    v = dot(normed[...], wv[...].reshape(D, HALF)).astype(BF).astype(F32)
    vall = flip(v) * jnp.concatenate(masks, axis=1)
    for h in range(HH):
        block = jnp.concatenate(
            [vall[64 * h : 64 * h + 64, 0:128], vall[64 * h : 64 * h + 64, 128:256]], axis=0
        )
        place = [jnp.zeros((2, 128), F32)] * (h % 3) + masks
        place = place + [jnp.zeros((14 - 2 * (h % 3), 128), F32)]
        vt[h] = jnp.concatenate([block] + place, axis=0).astype(BF)
        vals[h] = flip(block).astype(BF)

    s1x = Sum(ux, rx, "x", pool)
    s1y = Sum(uy, ry, "y", pool)
    for k in (2, 1, 3, 0):
        xx = lax.rem(x + k, 4)
        yy = lax.rem(y + k, 4)

        cols = pl.ds(pl.multiple_of(512 * xx, 512), 512)
        extra = jnp.zeros((16, 512), F32)
        for h in range(3):
            u = dot(vt[h], e[h, :, :, cols].reshape(128, 512))
            extra = extra + u[128:144]
            for j in range(4):
                ux[xx, j, 128 * h : 128 * h + 128] = u[0:128, 128 * j : 128 * j + 128].astype(BF)
        for j in range(4):
            ux[xx, j, 384:400] = extra[:, 128 * j : 128 * j + 128].astype(BF)
        if k == 2:
            start(s1x.far)
        elif k > 0:
            s1x.near[k // 2].start()
        for j in range(4):
            cols = pl.ds(pl.multiple_of(512 * j + 128 * yy, 128), 128)
            extra = jnp.zeros((16, 128), F32)
            for h in range(3):
                u = dot(vt[h + 3], e[h + 3, :, :, cols].reshape(128, 128))
                extra = extra + u[128:144]
                uy[j, yy, 128 * h : 128 * h + 128] = u[0:128].astype(BF)
            uy[j, yy, 384:400] = extra.astype(BF)
        if k == 2:
            start(s1y.far)
        elif k > 0:
            s1y.near[k // 2].start()
    g2[1].end()
    swap_wo = to_sib(wo, wo)
    swap_wo.start()
    for way in range(2):
        g2[4 + way].end()
        share[1][way].start()
    s1x.relay()
    s1y.relay()
    s2x = scatter_two(mx, rx2, "x", pool)
    s2y = scatter_two(my, ry2, "y", pool)
    for pattern in g2:
        pattern.sent()
    wait_send(g1)
    wait_send([swap_pre, swap_tok, swap_tab, swap_og])
    s1x.end(mx)
    start([s2x])
    s1y.end(my)
    start([s2y])
    for half, (copies, mid, rcv, first) in enumerate(((s2x, mx, rx2, "x"), (s2y, my, ry2, "y"))):
        wait_recv([copies])
        total = scatter_end(mid, rcv, first)
        for hh in range(3):
            h = half * 3 + hh
            for b in range(2):
                r = masks[b] / total[384 + 2 * hh + b : 385 + 2 * hh + b]
                rr[b, h : h + 1] = r
                mt[b, 64 * h : 64 * h + 64] = total[128 * hh + 64 * b : 128 * hh + 64 * b + 64] * r
    for b in range(2):
        mix[c, b] = flip(mt[b]).astype(BF)
    swap_mix = to_sib(mix.at[c], mix.at[c])
    swap_mix.start()
    swap_wo.wait_recv()
    swap_mix.wait_recv()
    mixed = [mix[i].reshape(256, HALF) for i in range(2)]
    for cc in range(2):
        w = wo_all[cc].reshape(D, HALF)
        cols = slice(HALF * cc, HALF * cc + HALF)
        middle[:, cols] = (
            tok[...].reshape(256, D)[:, cols].astype(F32)
            + dot(mixed[0], w[0:HALF])
            + dot(mixed[1], w[HALF:D])
        )
    mid_v = middle[...]
    rms = rms_of(mid_v)
    nf[...] = (mid_v * rms * gf).astype(BF)
    swap_og.wait_recv()
    grad = og[...].reshape(256, D)
    wait_recv(share[0])
    for hf in range(2):
        hp = jnp.concatenate([dot(nf[...], wz[2 * hf + i].reshape(D, HALF)) for i in range(2)], axis=1)
        t = jnp.tanh(GELU_C * (hp + GELU_A * hp * hp * hp))
        hid[hf] = (0.5 * hp * (1.0 + t)).astype(BF)
        act[hf] = 0.5 * (1.0 + t) + 0.5 * hp * (1.0 - t * t) * (
            GELU_C * (1.0 + 3.0 * GELU_A * hp * hp)
        )

    def down_rows(m, b):
        return jnp.concatenate([wz[4 + b, m].reshape(192, HALF), wz[6 + b, m].reshape(192, HALF)], axis=0)

    lots = (
        (dwda, rd.at[0], md.at[0], rd2.at[0], "x"),
        (dwdb, rd.at[1], md.at[1], rd2.at[1], "y"),
        (dws, rl.at[0], ml.at[0], rl2.at[0], "x"),
        (dwo, rl.at[1], ml.at[1], rl2.at[1], "y"),
        (
            dwv.at[:, :, pl.ds(0, 32)], rl.at[2, :, :, pl.ds(0, 32)], ml.at[2, :, pl.ds(0, 32)],
            rl2.at[2, :, pl.ds(0, 32)], "x",
        ),
        (
            dwv.at[:, :, pl.ds(32, 16)], rl.at[2, :, :, pl.ds(32, 16)], ml.at[2, :, pl.ds(32, 16)],
            rl2.at[2, :, pl.ds(32, 16)], "y",
        ),
    )
    def middle_sum(i):
        w1[i].end(lots[i][2])
        start([w2[i]])

    def last_sum(i):
        wait_recv([w2[i]])
        _, _, mid, rcv, first = lots[i]
        return scatter_end(mid, rcv, first)

    def z_at(k):
        return at(lax.rem(z + k, 8), x, y, c)

    def down_part(d):
        return down_sum.at[
            pl.ds(pl.multiple_of(48 * (lax.rem(d, 4) // 2), 16), 48),
            pl.ds(pl.multiple_of(HALF * lax.rem(d, 2), 128), HALF),
        ]

    def rest_part(d):
        return rest.at[pl.ds(pl.multiple_of(16 * lax.rem(d, 4), 16), 16)]

    def z_first(part, buf, ks):
        return Batch(pool, [(part(z + k), buf.at[j], z_at(k)) for j, k in enumerate(ks)], buf, buf)

    def z_half(part, buf, res):
        total = part(z)[...].astype(F32)
        for j in range(3):
            total = total + buf[j].astype(F32)
        res[...] = total.astype(BF)

    def z_swap(half, other):
        return remote(half, other, pool.take(), pool.take(), z_at(4))

    def z_last(half, other, full, ks):
        full[q] = (half[...].astype(F32) + other[...].astype(F32)).astype(BF)
        three = full.at[pl.ds(0, 3)]
        return Batch(pool, [(full.at[q], full.at[q], z_at(k)) for k in ks], three, three)

    w1 = [Sum(lot[0], lot[1], lot[4], pool) for lot in lots]
    w2 = [scatter_two(lot[2], lot[3], lot[4], pool) for lot in lots]

    def dw_part(shift, h):
        return dwu.at[lax.rem(z + 8 + shift, 4), pl.ds(2 * h, 2)]

    ways = (up, down)
    far = [remote(dw_part(2 - 4 * h, h), dfar.at[h], pool.take(), pool.take(), ways[h]) for h in range(2)]
    near = [remote(dw_part(2 * h - 1, h), dnear.at[h], pool.take(), pool.take(), ways[1 - h]) for h in range(2)]
    last = [remote(dsum.at[h], dlast.at[h], pool.take(), pool.take(), ways[h]) for h in range(2)]
    wait_recv(share[1])
    s1x.sent()
    s1y.sent()
    wait_send([s2x, s2y] + share[0] + [swap_wo, swap_mix])
    for hf in range(2):
        for i in range(2):
            m = 2 * hf + i
            cols = slice(HALF * i, HALF * i + HALF)
            hg = dot_nt(grad[:, 0:HALF], down_rows(m, 0)) + dot_nt(grad[:, HALF:D], down_rows(m, 1))
            pgr[hf, :, cols] = (act[hf, :, cols] * hg).astype(BF)
            more = dot_nt(pgr[hf, :, cols], wz[m].reshape(D, HALF)).reshape(2, 2, 64, D)
            fng[...] = more if m == 0 else fng[...] + more
    swap_fng = to_sib(fng, fng_r)
    swap_fng.start()
    for hf in range(2):
        grad_w = dot(flip(nf[...]), pgr[hf]).astype(BF)
        for i in range(2):
            dwu[2 * hf + i] = grad_w[:, HALF * i : HALF * i + HALF].reshape(4, 4, 48, HALF)
    start(far)
    swap_fng.wait_recv()
    full = (fng[...] + fng_r[...]).reshape(256, D)
    mid_v = middle[...]
    rms = rms_of(mid_v)
    gain_f = jnp.sum(full * mid_v * rms, axis=0, keepdims=True)
    weighted = full * gf
    inner = jnp.mean(weighted * mid_v, axis=-1, keepdims=True)
    mg = grad.astype(F32) + rms * weighted - mid_v * (rms * rms * rms) * inner
    mgrad[...] = mg.reshape(2, 2, 64, D)
    bg = mg.astype(BF)
    bgs[...] = bg
    xg = jnp.zeros((256, HALF), F32)
    for cc in range(2):
        w = wo_all[cc, pl.ds(2 * c, 2)].reshape(HALF, HALF)
        xg = xg + dot_nt(bg[:, HALF * cc : HALF * cc + HALF], w)
    deltas = []
    for b in range(2):
        xgt = flip(xg[128 * b : 128 * b + 128])
        for h in range(HH):
            rows = xgt[64 * h : 64 * h + 64]
            r = rr[b, h : h + 1]
            deltas.append(jnp.sum(rows * mt[b, 64 * h : 64 * h + 64], axis=0, keepdims=True) * r)
            own = gx if h < 3 else gy
            base = 128 * (h % 3) + 64 * b
            own[x, y, base : base + 64] = (rows * r).astype(BF)
    for own, first in ((gx, 0), (gy, 3)):
        rows = []
        for h in range(first, first + 3):
            d0, d1 = deltas[h], deltas[HH + h]
            h0 = d0.astype(BF).astype(F32)
            h1 = d1.astype(BF).astype(F32)
            rows = rows + [h0, h1, d0 - h0, d1 - h1]
        own[x, y, 384:400] = jnp.concatenate(rows + [jnp.zeros((4, 128), F32)], axis=0).astype(BF)
    parts_g = [
        (buf.at[:, :, pl.ds(base, size)], first)
        for buf in (gx, gy)
        for base, size, first in ((0, 208, "x"), (208, 192, "y"))
    ]
    a1 = [gather_one(buf, first, pool) for buf, first in parts_g]
    a2 = [Spread(buf, first, pool) for buf, first in parts_g]
    start(a1)
    start(near)
    for hf in range(2):
        grad_w = dot(flip(hid[hf]), grad).astype(BF)
        for i in range(2):
            for a in range(2):
                for k in range(4):
                    base = HALF * i + 192 * a + 48 * k
                    dwda[2 * hf + i, k, 48 * a : 48 * a + 48] = grad_w[base : base + 48, 0:HALF]
                    dwdb[2 * hf + i, k, 48 * a : 48 * a + 48] = grad_w[base : base + 48, HALF:D]
    for i in range(2):
        wait_recv([a1[i]])
        a2[i].start()
    bg_c = bgs[:, pl.ds(pl.multiple_of(HALF * c, 128), HALF)]
    for i in range(2):
        dwo[pl.ds(2 * i, 2)] = dot(flip(mixed[i]), bg_c).astype(BF).reshape(2, 4, 48, HALF)
    for hf in range(2):
        down_w = [jnp.concatenate([down_rows(2 * hf, b), down_rows(2 * hf + 1, b)], axis=0) for b in range(2)]
        more = jnp.concatenate([dot(hid[hf], w) for w in down_w], axis=1).reshape(2, 2, 64, D)
        part[...] = more if hf == 0 else part[...] + more
    swap_part = to_sib(part.at[:, 1 - c], part_r)
    swap_part.start()
    for i in range(2):
        a2[i].relay()
    for h in range(2):
        far[h].wait_recv()
        dsum[h] = (dw_part(1 - 2 * h, h)[...].astype(F32) + dfar[h].astype(F32)).astype(BF)
        last[h].start()
    for i in range(2, 4):
        wait_recv([a1[i]])
        a2[i].start()
    swap_fng.wait_send()
    fng[...] = middle[...].reshape(2, 2, 64, D)
    swap_part.wait_recv()
    out_s[...] = (fng[:, c] + (part[:, c] + part_r[...])).astype(BF)
    save(out_s, out)
    wait_send(a1)
    wait_send(far + share[1])
    for i in range(2):
        a2[i].end()

    def table_part(d, hf):
        buf = gx if hf == 0 else gy
        result = []
        for hh in range(3):
            h = 3 * hf + hh
            pair = []
            for i in range(2):
                k = 2 * d + i
                g = buf[k // 4, lax.rem(k, 4), 128 * hh : 128 * hh + 128]
                cols = pl.ds(pl.multiple_of(256 * d + 128 * i, 128), 128)
                extra = buf[k // 4, lax.rem(k, 4), 384:400].astype(F32)[4 * hh : 4 * hh + 4]
                s = dot(vals[h], g)
                s = s - mcol[0] * (extra[0:1] + extra[2:3])
                s = s - mcol[1] * (extra[1:2] + extra[3:4])
                pair.append(s * e[h, :, :, cols].reshape(128, 128).astype(F32))
            result.append(jnp.concatenate(pair, axis=1))
        return result

    def ring(send, recv, count, hf, device):
        sent = pool.take()
        return [
            remote(send.at[hf, t], recv.at[hf, t], sent, pool.take(), device) for t in range(count)
        ], Bytes(send.at[hf, pl.ds(0, count)], sent)

    ups, up_sent = zip(*[ring(up_s, up_r, 4 - hf, hf, up) for hf in range(2)])
    dns, dn_sent = zip(*[ring(dn_s, dn_r, 3 + hf, hf, down) for hf in range(2)])

    def step(t, hf):
        for copies, send, recv, d in (
            (ups[hf], up_s, up_r, lax.rem(z + 12 - hf - t, 8)),
            (dns[hf], dn_s, dn_r, lax.rem(z + 5 - hf + t, 8)),
        ):
            if t >= len(copies):
                continue
            parts = table_part(d, hf)
            if t > 0:
                copies[t - 1].wait_recv()
            for hh in range(3):
                p = parts[hh]
                if t > 0:
                    p = p + recv[hf, t - 1, hh].astype(F32)
                send[hf, t, hh] = p.astype(BF)
            copies[t].start()

    def value_part(hf):
        buf = (gx, gy)[hf]
        for hh in range(3):
            total = jnp.zeros((128, 128), F32)
            for k in range(16):
                cols = slice(128 * k, 128 * k + 128)
                total = total + dot_nt(
                    buf[k // 4, k % 4, 128 * hh : 128 * hh + 128], e[3 * hf + hh, :, :, cols].reshape(128, 128)
                )
            rows = slice(64 * (3 * hf + hh), 64 * (3 * hf + hh) + 64)
            for b in range(2):
                vgt[b, rows] = total[64 * b : 64 * b + 64] * masks[b]

    step(0, 0)
    for i in range(2, 4):
        a2[i].relay()
    w1[0].start()
    w1[1].start()
    value_part(0)
    for h in range(2):
        near[h].wait_recv()
        last[h].wait_recv()
        total = dw_part(0, h)[...].astype(F32) + dnear[h].astype(F32) + dlast[h].astype(F32)
        dws[pl.ds(2 * h, 2)] = total.astype(BF)
    w1[2].start()
    step(1, 0)
    for i in range(2, 4):
        a2[i].end()
    step(0, 1)
    value_part(1)
    vg = jnp.concatenate([flip(vgt[b]) for b in range(2)], axis=0).astype(BF)
    dwv[...] = dot(flip(normed[...]), vg).astype(BF).reshape(4, 4, 48, HALF)
    w1[4].start()
    w1[5].start()
    w1[3].start()
    swap_part.wait_send()
    part[...] = dot_nt(vg, wv[...].reshape(D, HALF)).reshape(2, 2, 64, D)
    swap_ng = to_sib(part, ng_r)
    swap_ng.start()
    w1[0].relay()
    w1[1].relay()
    for pattern in a2:
        pattern.sent()
    step(2, 0)
    w1[2].relay()
    w1[3].relay()
    step(1, 1)
    swap_ng.wait_recv()
    full = (part[...] + ng_r[...]).reshape(256, D)
    xv = tok[...].reshape(256, D).astype(F32)
    rms = rms_of(xv)
    gain_m = jnp.sum(full * xv * rms, axis=0, keepdims=True)
    weighted = full * gm
    inner = jnp.mean(weighted * xv, axis=-1, keepdims=True)
    fng[...] = (rms * weighted - xv * (rms * rms * rms) * inner).reshape(2, 2, 64, D)
    ig_s[...] = mgrad[:, c] + fng[:, c]
    save(ig_s, input_grad)
    gains = jnp.concatenate([gain_m, gain_f], axis=0)
    high = gains.astype(BF).astype(F32)
    gs[...] = jnp.concatenate([high, gains - high, jnp.zeros((12, D), F32)], axis=0).astype(BF)
    gr[x, y] = gs[...]
    gain1 = gather_one(gr, "x", pool)
    gain2 = gather_two(gr, "x", pool)
    start([gain1])

    def rows_of(src, base, cc):
        return src[0, pl.ds(pl.multiple_of(base + 24 * cc, 8), 24)]

    def finish_ring(hf):
        own = table_part(z, hf)
        ups[hf][-1].wait_recv()
        dns[hf][-1].wait_recv()
        for hh in range(3):
            h = 3 * hf + hh
            p = own[hh] + (up_r[hf, 3 - hf, hh].astype(F32) + dn_r[hf, 2 + hf, hh].astype(F32))
            act[1, 0:128, 0:256] = p
            tgo[h] = act[1, pl.ds(pl.multiple_of(64 * c, 64), 64), 0:256]
            tgs[h] = act[1, pl.ds(pl.multiple_of(64 * (1 - c), 64), 64), 0:256]
        swap_tg[hf].start()
        save(tgo.at[pl.ds(3 * hf, 3)], tg.at[c, pl.ds(3 * hf, 3)])

    swap_tg = [
        to_sib(tgs.at[pl.ds(3 * hf, 3)], tg_r.at[pl.ds(3 * hf, 3)]) for hf in range(2)
    ]
    w1[4].relay()
    w1[5].relay()
    step(3, 0)
    middle_sum(0)
    middle_sum(1)
    step(2, 1)
    middle_sum(2)
    middle_sum(3)
    wait_recv([gain1])
    start([gain2])
    middle_sum(4)
    middle_sum(5)
    for i in range(2):
        down_sum[:, HALF * i : HALF * i + HALF] = last_sum(i).astype(BF)
    z_down1 = z_first(down_part, zr_down, (1, 2, 7))
    start([z_down1])
    half_up[...] = last_sum(2).astype(BF)
    z_up2 = z_swap(half_up, other_up)
    z_up2.start()
    for pattern in w1[:3]:
        pattern.sent()
    wait_send(near + last)
    step(3, 1)
    rest[0:48, 0:HALF] = last_sum(3).astype(BF)
    rest[0:32, HALF:D] = last_sum(4).astype(BF)
    rest[32:48, HALF:D] = last_sum(5).astype(BF)
    wait_recv([gain2])
    gtot = jnp.sum(gr[...].reshape(16, 16, D).astype(F32), axis=0)
    gains = gtot[0:2] + gtot[2:4]
    high = gains.astype(BF).astype(F32)
    rest[48:64] = jnp.concatenate([high, gains - high, jnp.zeros((12, D), F32)], axis=0).astype(BF)
    z_rest1 = z_first(rest_part, zr_rest, (7, 6, 1))
    start([z_rest1])
    wait_recv([z_down1])
    z_half(down_part, zr_down, half_down)
    z_down2 = z_swap(half_down, other_down)
    z_down2.start()
    finish_ring(0)
    z_up2.wait_recv()
    z_up3 = z_last(half_up, other_up, zs_up, (1, 7, 2))
    start([z_up3])
    wait_recv([z_rest1])
    z_half(rest_part, zr_rest, half_rest)
    z_rest2 = z_swap(half_rest, other_rest)
    z_rest2.start()
    z_down2.wait_recv()
    z_down3 = z_last(half_down, other_down, zs_down, (1, 7, 6))
    start([z_down3])
    for pattern in w1[3:]:
        pattern.sent()
    wait_send(w2 + [z_down1, z_rest1, gain1, gain2])
    finish_ring(1)
    wait_recv([z_up3])
    for m in range(4):
        act[0, 48 * (m // 2) : 48 * (m // 2) + 48, HALF * (m % 2) : HALF * (m % 2) + HALF] = zs_up[m].astype(F32)
    for cc, ref in ((c, post_up.at[0]), (1 - c, post_up.at[1])):
        ref[:, 0:D] = rows_of(act, 0, cc)
        ref[:, D : 2 * D] = rows_of(act, 48, cc)
    swap_up = to_sib(post_up.at[1], post_up.at[2])
    swap_up.start()
    z_rest2.wait_recv()
    z_rest3 = z_last(half_rest, other_rest, zs_rest, (1, 7, 6))
    start([z_rest3])
    wait_recv([z_down3])
    for m in range(4):
        rows, cols = slice(48 * (m // 2), 48 * (m // 2) + 48), slice(HALF * (m % 2), HALF * (m % 2) + HALF)
        down_s[rows, cols] = zs_down[m].astype(F32)
    save(down_s, d_down)
    first_core = (c == 0).astype(F32)

    def by_core(ref):
        own, got = ref[0], ref[2]
        return own * first_core + got * (1.0 - first_core), got * first_core + own * (1.0 - first_core)

    swap_up.wait_recv()
    pair = by_core(post_up)
    for m in range(4):
        block = jnp.concatenate([p[:, HALF * m : HALF * m + HALF] for p in pair], axis=1).astype(BF)
        up_s_out[:, D * m : D * m + D] = dot_nt(block, perm[...])
    save(up_s_out, d_up)
    wait_recv([z_rest3])
    act[0, 0:64] = zs_rest[...].reshape(64, D).astype(F32)
    for cc, ref in ((c, post_rest.at[0]), (1 - c, post_rest.at[1])):
        ref[...] = rows_of(act, 0, cc)
    swap_rest = to_sib(post_rest.at[1], post_rest.at[2])
    swap_rest.start()
    gsum_s[...] = jnp.concatenate([act[0, 48:50] + act[0, 50:52], jnp.zeros((6, D), F32)], axis=0)
    save(gsum_s, gsum)
    for hf in range(2):
        swap_tg[hf].wait_recv()
        save(tg_r.at[pl.ds(3 * hf, 3)], tg.at[1 - c, pl.ds(3 * hf, 3)])
    swap_rest.wait_recv()
    pair = by_core(post_rest)
    for cc in range(2):
        cols = slice(HALF * cc, HALF * cc + HALF)
        two_s[0, :, cols] = pair[cc][:, 0:HALF]
        two_s[1, :, cols] = pair[cc][:, HALF:D]
    save(two_s.at[0], d_out)
    save(two_s.at[1], d_value)
    for copy in saved:
        copy.wait()
    wait_send(list(up_sent + dn_sent) + swap_tg + [z_up3, z_down3, z_rest3])
    assert pool.used == SEMS, pool.used
    wait_send([swap_ng, swap_up, swap_rest, z_up2, z_down2, z_rest2])


def finish(out, input_grad, d_value, d_out, d_up, d_down, gsum, tg, *outs):
    for src, dst in zip((out, input_grad, d_value, d_out, d_up, d_down, tg), outs):
        dst[...] = src[...]
    s = lax.axis_index("seq")
    row = lax.broadcasted_iota(jnp.int32, (D, 128), 0)
    lane = lax.broadcasted_iota(jnp.int32, (D, 128), 1)
    pick = jnp.where(row == lane + 24 * s, 1.0, 0.0)
    for i in range(2):
        got = jnp.dot(gsum[...], pick, precision=lax.Precision.HIGHEST, preferred_element_type=F32)
        outs[7 + i][...] = got[i, 0:24]


def vmem(*shape, kind=BF):
    return pltpu.VMEM(shape, kind)


IN_VMEM = pl.BlockSpec(memory_space=pltpu.VMEM)
ANY = pl.BlockSpec(memory_space=pl.ANY)


def per_device(tokens, lengths, w_value, w_out, w_up, w_down, gain_mix, gain_ffn, mix_table, out_grad):
    sd = jax.ShapeDtypeStruct
    shapes = [
        sd((2, 64, D), BF), sd((2, 64, D), F32), sd((24, D), F32), sd((24, D), F32), sd((24, 4 * D), F32),
        sd((96, D), F32), sd((8, D), F32), sd((2, HH, 64, 256), F32),
    ]
    raw = pl.pallas_call(
        layer,
        name="layer",
        out_shape=shapes,
        in_specs=[pl.BlockSpec(memory_space=pltpu.SMEM)] + [IN_VMEM] * 8 + [pl.BlockSpec(memory_space=pl.ANY)],
        out_specs=[ANY] * 8,
        scratch_shapes=[
            vmem(D, D), vmem(2, 24, 2 * D, kind=F32), vmem(2, 24, 2 * D, kind=F32),
            vmem(2, 2, 64, D), vmem(2, 2, 64, D), vmem(HH, 2, 64, 2048),
            vmem(4, 4, 48, HALF), vmem(2, 4, 4, 48, HALF), vmem(8, 4, 4, 48, HALF),
            vmem(4, 4, ROWS, 128), vmem(4, 4, ROWS, 128), vmem(3, 4, ROWS, 128), vmem(3, 4, ROWS, 128),
            vmem(4, ROWS, 128), vmem(4, ROWS, 128), vmem(3, ROWS, 128), vmem(3, ROWS, 128),
            vmem(2, HALF, 128, kind=F32), vmem(2, 8, 128, kind=F32), vmem(2, 2, 128, HALF), vmem(HH, 144, 128),
            vmem(HH, 128, 128), vmem(2, 128, 128, kind=F32), vmem(256, D), vmem(256, D, kind=F32), vmem(256, D),
            vmem(256, D), vmem(2, 256, D), vmem(2, 256, D), vmem(2, 256, D, kind=F32),
            vmem(2, 2, 64, D, kind=F32), vmem(2, 64, D, kind=F32), vmem(2, 2, 64, D, kind=F32),
            vmem(2, 2, 64, D, kind=F32), vmem(2, 2, 64, D, kind=F32),
            vmem(4, 4, 4, 48, HALF), vmem(4, 4, 96, HALF), vmem(4, 4, 96, HALF), vmem(4, 4, 48, HALF), vmem(4, 4, 48, HALF),
            vmem(4, 4, 48, HALF), vmem(4, 4, ROWS, 128), vmem(4, 4, ROWS, 128),
            vmem(2, 3, 4, 96, HALF), vmem(3, 3, 4, 48, HALF), vmem(2, 4, 96, HALF), vmem(3, 4, 48, HALF),
            vmem(2, 3, 96, HALF), vmem(3, 3, 48, HALF),
            vmem(2, 2, 4, 48, HALF), vmem(2, 2, 4, 48, HALF), vmem(2, 2, 4, 48, HALF), vmem(2, 2, 4, 48, HALF),
            vmem(16, D), vmem(4, 4, 16, D),
            vmem(2, 4, 3, 128, 256), vmem(2, 4, 3, 128, 256), vmem(2, 4, 3, 128, 256), vmem(2, 4, 3, 128, 256),
            vmem(HH, 64, 256, kind=F32), vmem(HH, 64, 256, kind=F32), vmem(2, HALF, 128, kind=F32),
            vmem(2, 2, 64, D, kind=F32), vmem(96, D), vmem(64, D), vmem(3, 48, HALF), vmem(3, 16, D),
            vmem(48, HALF), vmem(48, HALF), vmem(16, D), vmem(48, HALF), vmem(48, HALF), vmem(16, D),
            vmem(4, 48, HALF), vmem(4, 48, HALF), vmem(4, 16, D),
            vmem(3, 24, 2 * D, kind=F32), vmem(3, 24, D, kind=F32), vmem(2, 64, D), vmem(2, 64, D, kind=F32),
            vmem(96, D, kind=F32), vmem(24, 4 * D, kind=F32), vmem(HH, 64, 256, kind=F32),
            vmem(8, D, kind=F32), vmem(2, 24, D, kind=F32),
            pltpu.SemaphoreType.DMA((SEMS,)),
        ],
        compiler_params=pltpu.CompilerParams(
            collective_id=0, has_side_effects=True, vmem_limit_bytes=63 << 20
        ),
    )(lengths, tokens, out_grad, w_value, w_out, w_up, w_down, gain_mix, gain_ffn, mix_table)
    out, input_grad, d_value, d_out, d_up, d_down, tg, mix_gain, ffn_gain = pl.pallas_call(
        finish,
        name="finish",
        out_shape=shapes[:6] + [shapes[7], sd((24,), F32), sd((24,), F32)],
        in_specs=[IN_VMEM] * 8,
        out_specs=[IN_VMEM] * 9,
    )(*raw)
    return (
        out, input_grad, d_value, d_out, d_up, d_down, mix_gain, ffn_gain, tg.reshape(HEADS, 64, 256),
    )


def solution(mesh):
    return jax.shard_map(
        per_device,
        mesh=mesh,
        in_specs=(
            P("dp", "seq", None),
            P("dp"),
            P("seq", None),
            P("seq", None),
            P("seq", None),
            P("seq", None),
            P(),
            P(),
            P(None, "seq", None),
            P("dp", "seq", None),
        ),
        out_specs=(
            P("dp", "seq", None),
            P("dp", "seq", None),
            P("seq", None),
            P("seq", None),
            P("seq", None),
            P("seq", None),
            P("seq"),
            P("seq"),
            P(None, "seq", "dp"),
        ),
        check_vma=False,
    )
```

time: 161 us -> 141 us (0.88)
  Pallas kernels: 160 us -> 140 us
    pallas_call x1, Pallas kernels: 157 us -> 137 us  [per_device(): pl.pallas_call(layer, name='layer', out_shape=shapes, in_specs=[pl.BlockS...]
where the time goes in v4:
time: 141 us
  Pallas kernels  140 us (99%)
    pallas_call x1, Pallas kernels, per_device(): pl.pallas_call(layer, name='layer', out_shape=shapes, in_specs=[pl.BlockS...  137 us
    pallas_call x1, Pallas kernels, per_device(): pl.pallas_call(finish, name='finish', out_shape=shapes[:6] + [shapes[7],...  3.29 us

profile of v4, /device:TPU:1, one launch (start us, length us, event | category | flops | bytes accessed | tf_op | source)
XLA Modules:
  0.0 140.6 jit_solution(6296099574643966883)
XLA Ops:
  0.6 136.6 %layer.1 = (bf16[2,64,768]{2,1,0:T(8,128)(2,1)}, f32[2,64,768]{2,1,0:T(8,128)}, f32[24,768]{1,0:T(8,128)}, f32[24,768]{1,0:T(8,128)}, f32[24,3072]{1,0:T(8,128)}...) custom-call(s32[2]{0:T(128)} %lengths.1, bf16[2,64,768]{2,1,0:T(8,128)(2,1)} %tokens.1, ...), custom_call_target="tpu_custom_call" | custom-call | tf_op jit(solution)/shard_map/layer/pallas_call | solution.py:887
  137.3 3.3 %finish.1 = (bf16[2,64,768]{2,1,0:T(8,128)(2,1)}, f32[2,64,768]{2,1,0:T(8,128)}, f32[24,768]{1,0:T(8,128)}, f32[24,768]{1,0:T(8,128)}, f32[24,3072]{1,0:T(8,128)...) custom-call(bf16[2,64,768]{2,1,0:T(8,128)(2,1)} %get-tuple-element.26.out, ...), custom_call_target="tpu_custom_call" | custom-call | tf_op jit(solution)/shard_map/finish/pallas_call | solution.py:924

commit v5 on v4

--- a/solution.py
+++ b/solution.py
@@ -15,7 +15,7 @@
 F32 = jnp.float32
 OFFS = (1, 3, 2)
 ROWS = 400
-SEMS = 204
+SEMS = 206
 GELU_C = 0.7978845608028654
 GELU_A = 0.044715
 
@@ -248,7 +248,7 @@
 def layer(
     lengths, tokens, out_grad, w_value, w_out, w_up, w_down, gain_mix, gain_ffn, table,
     out, input_grad, d_value, d_out, d_up, d_down, gsum, tg,
-    perm, pre, got, tok, og, e, wv, wo_all, wz,
+    perm, pre_a, pre_b, got_a, got_b, tok, og, e, wv, wo_all, wz,
     ux, uy, rx, ry, mx, my, rx2, ry2, mt, rr, mix, vt, vals, mcol, normed, middle, nf, bgs, hid, pgr, act,
     part, part_r, fng, fng_r, mgrad, dwu, dwda, dwdb, dws, dwo, dwv, gx, gy,
     rd, rl, md, ml, rd2, rl2, dfar, dnear, dlast, dsum, gs, gr, up_s, up_r, dn_s, dn_r, tgs, tg_r, vgt, ng_r,
@@ -277,6 +277,16 @@
     count = greet()
     own_tab = pltpu.make_async_copy(table.at[pl.ds(6 * c, 6)], e.at[:, c], pool.take())
     own_tab.start()
+    q = lax.rem(z, 4)
+    par = lax.rem(z, 2)
+    for cc in range(2):
+        cols = slice(HALF * cc, HALF * cc + HALF)
+        pre_a[cc, :, 0:HALF] = w_out[:, cols].astype(F32)
+        pre_a[cc, :, HALF:D] = w_value[:, cols].astype(F32)
+    meet(count)
+    swap_a = to_sib(pre_a.at[1 - c], got_a.at[c])
+    swap_a.start()
+    got_a[c] = pre_a[c]
     col = lax.broadcasted_iota(jnp.int32, (1, D), 1)
     odd = jnp.where(col >= HALF, 1, 0)
     low = col - HALF * odd
@@ -285,45 +295,38 @@
     quad = jnp.where(low >= 48, 1, 0) + jnp.where(low >= 96, 1, 0) + jnp.where(low >= 144, 1, 0)
     origin = low + 144 * quad + 96 * odd + 48 * half
     perm[...] = jnp.where(lax.broadcasted_iota(jnp.int32, (D, D), 0) == origin, 1.0, 0.0).astype(BF)
-    q = lax.rem(z, 4)
-    for cc in range(2):
-        cols = slice(HALF * cc, HALF * cc + HALF)
-        pre[cc, :, 0:HALF] = w_out[:, cols].astype(F32)
-        pre[cc, :, HALF:D] = w_value[:, cols].astype(F32)
-    par = lax.rem(z, 2)
     for i in range(2):
         mine = dot(w_up[:, pl.ds(pl.multiple_of(D * (2 * par + i), D), D)], perm[...])
         for cc in range(2):
-            pre[cc, :, D + HALF * i : D + HALF * i + HALF] = mine[:, HALF * cc : HALF * cc + HALF]
-    meet(count)
-    swap_pre = to_sib(pre.at[1 - c], got.at[c])
-    swap_tok = to_sib(tokens, tok.at[:, c])
-    swap_tab = to_sib(table.at[pl.ds(6 * (1 - c), 6)], e.at[:, c])
-    swap_og = to_sib(out_grad, og.at[:, c])
-    swap_pre.start()
-    got[c] = pre[c]
-    tok[:, c] = tokens[...]
-    og[:, c] = out_grad[...]
-    for b in range(2):
-        rows = pl.ds(pl.multiple_of(48 * par, 16), 48)
-        wz[4 + 2 * par + b, x, y] = w_down[rows, HALF * b : HALF * b + HALF]
+            pre_b[cc, :, HALF * i : HALF * i + HALF] = mine[:, HALF * cc : HALF * cc + HALF]
+    swap_b = to_sib(pre_b.at[1 - c], got_b.at[c])
+    swap_b.start()
+    got_b[c] = pre_b[c]
     bufs = (
         (wv, "x"), (wo, "y"), (wz.at[2 * par], "x"), (wz.at[2 * par + 1], "y"),
         (wz.at[4 + 2 * par], "x"), (wz.at[5 + 2 * par], "y"),
     )
     g1 = [gather_one(buf, first, pool) for buf, first in bufs]
     g2 = [Spread(buf, first, pool) for buf, first in bufs]
-    swap_pre.wait_recv()
-    shard = got[...].reshape(48, 2 * D).astype(BF)
+    swap_a.wait_recv()
+    shard = got_a[...].reshape(48, D).astype(BF)
     wo[x, y] = shard[:, 0:HALF]
     wv[x, y] = shard[:, HALF:D]
+    start(g1[0:2])
+    swap_tok = to_sib(tokens, tok.at[:, c])
+    swap_tab = to_sib(table.at[pl.ds(6 * (1 - c), 6)], e.at[:, c])
+    swap_og = to_sib(out_grad, og.at[:, c])
+    start([swap_tok, swap_tab, swap_og])
+    tok[:, c] = tokens[...]
+    og[:, c] = out_grad[...]
+    for b in range(2):
+        rows = pl.ds(pl.multiple_of(48 * par, 16), 48)
+        wz[4 + 2 * par + b, x, y] = w_down[rows, HALF * b : HALF * b + HALF]
+    swap_b.wait_recv()
+    shard = got_b[...].reshape(48, D).astype(BF)
     for i in range(2):
-        wz[2 * par + i, x, y] = shard[:, D + HALF * i : D + HALF * i + HALF]
-    order = (2, 3, 0, 1, 4, 5)
-    for i in order:
-        start([g1[i]])
-    start([swap_tok, swap_tab, swap_og])
-
+        wz[2 * par + i, x, y] = shard[:, HALF * i : HALF * i + HALF]
+    start(g1[2:4])
     share = [
         [
             remote(
@@ -333,9 +336,10 @@
         ]
         for i in range(2)
     ]
-    for i in order:
+    for i in range(4):
         wait_recv([g1[i]])
         g2[i].start()
+    start(g1[4:6])
     swap_tok.wait_recv()
     values = tok[...].reshape(256, D).astype(F32)
     gm = gain_mix[...].reshape(1, D)
@@ -355,11 +359,11 @@
         return carry
 
     lax.fori_loop(0, HH, exps, 0)
-    for i in order:
+    for i in range(4):
         g2[i].relay()
-    for way in range(2):
-        g2[2 + way].end()
-        share[0][way].start()
+    for i in (4, 5):
+        wait_recv([g1[i]])
+        g2[i].start()
     g2[0].end()
     v = dot(normed[...], wv[...].reshape(D, HALF)).astype(BF).astype(F32)
     vall = flip(v) * jnp.concatenate(masks, axis=1)
@@ -403,20 +407,25 @@
             start(s1y.far)
         elif k > 0:
             s1y.near[k // 2].start()
+    for way in range(2):
+        g2[2 + way].end()
+        share[0][way].start()
     g2[1].end()
     swap_wo = to_sib(wo, wo)
     swap_wo.start()
+    g2[4].relay()
+    g2[5].relay()
+    s1x.relay()
+    s1y.relay()
     for way in range(2):
         g2[4 + way].end()
         share[1][way].start()
-    s1x.relay()
-    s1y.relay()
     s2x = scatter_two(mx, rx2, "x", pool)
     s2y = scatter_two(my, ry2, "y", pool)
     for pattern in g2:
         pattern.sent()
     wait_send(g1)
-    wait_send([swap_pre, swap_tok, swap_tab, swap_og])
+    wait_send([swap_a, swap_b, swap_tok, swap_tab, swap_og])
     s1x.end(mx)
     start([s2x])
     s1y.end(my)
@@ -451,8 +460,12 @@
     swap_og.wait_recv()
     grad = og[...].reshape(256, D)
     wait_recv(share[0])
+
+    def up_rows(hf):
+        return jnp.concatenate([wz[2 * hf + i].reshape(D, HALF) for i in range(2)], axis=1)
+
     for hf in range(2):
-        hp = jnp.concatenate([dot(nf[...], wz[2 * hf + i].reshape(D, HALF)) for i in range(2)], axis=1)
+        hp = dot(nf[...], up_rows(hf))
         t = jnp.tanh(GELU_C * (hp + GELU_A * hp * hp * hp))
         hid[hf] = (0.5 * hp * (1.0 + t)).astype(BF)
         act[hf] = 0.5 * (1.0 + t) + 0.5 * hp * (1.0 - t * t) * (
@@ -489,10 +502,7 @@
         return at(lax.rem(z + k, 8), x, y, c)
 
     def down_part(d):
-        return down_sum.at[
-            pl.ds(pl.multiple_of(48 * (lax.rem(d, 4) // 2), 16), 48),
-            pl.ds(pl.multiple_of(HALF * lax.rem(d, 2), 128), HALF),
-        ]
+        return down_sum.at[lax.rem(d, 4)]
 
     def rest_part(d):
         return rest.at[pl.ds(pl.multiple_of(16 * lax.rem(d, 4), 16), 16)]
@@ -528,14 +538,14 @@
     s1x.sent()
     s1y.sent()
     wait_send([s2x, s2y] + share[0] + [swap_wo, swap_mix])
+    def down_cols(hf):
+        pair = [jnp.concatenate([down_rows(2 * hf + i, b) for b in range(2)], axis=1) for i in range(2)]
+        return jnp.concatenate(pair, axis=0)
+
     for hf in range(2):
-        for i in range(2):
-            m = 2 * hf + i
-            cols = slice(HALF * i, HALF * i + HALF)
-            hg = dot_nt(grad[:, 0:HALF], down_rows(m, 0)) + dot_nt(grad[:, HALF:D], down_rows(m, 1))
-            pgr[hf, :, cols] = (act[hf, :, cols] * hg).astype(BF)
-            more = dot_nt(pgr[hf, :, cols], wz[m].reshape(D, HALF)).reshape(2, 2, 64, D)
-            fng[...] = more if m == 0 else fng[...] + more
+        pgr[hf] = (act[hf] * dot_nt(grad, down_cols(hf))).astype(BF)
+        more = dot_nt(pgr[hf], up_rows(hf)).reshape(2, 2, 64, D)
+        fng[...] = more if hf == 0 else fng[...] + more
     swap_fng = to_sib(fng, fng_r)
     swap_fng.start()
     for hf in range(2):
@@ -600,8 +610,7 @@
     for i in range(2):
         dwo[pl.ds(2 * i, 2)] = dot(flip(mixed[i]), bg_c).astype(BF).reshape(2, 4, 48, HALF)
     for hf in range(2):
-        down_w = [jnp.concatenate([down_rows(2 * hf, b), down_rows(2 * hf + 1, b)], axis=0) for b in range(2)]
-        more = jnp.concatenate([dot(hid[hf], w) for w in down_w], axis=1).reshape(2, 2, 64, D)
+        more = dot(hid[hf], down_cols(hf)).reshape(2, 2, 64, D)
         part[...] = more if hf == 0 else part[...] + more
     swap_part = to_sib(part.at[:, 1 - c], part_r)
     swap_part.start()
@@ -693,45 +702,92 @@
         total = dw_part(0, h)[...].astype(F32) + dnear[h].astype(F32) + dlast[h].astype(F32)
         dws[pl.ds(2 * h, 2)] = total.astype(BF)
     w1[2].start()
+    w1[3].start()
     step(1, 0)
     for i in range(2, 4):
         a2[i].end()
+    w1[0].relay()
+    w1[1].relay()
     step(0, 1)
     value_part(1)
     vg = jnp.concatenate([flip(vgt[b]) for b in range(2)], axis=0).astype(BF)
     dwv[...] = dot(flip(normed[...]), vg).astype(BF).reshape(4, 4, 48, HALF)
     w1[4].start()
     w1[5].start()
-    w1[3].start()
     swap_part.wait_send()
     part[...] = dot_nt(vg, wv[...].reshape(D, HALF)).reshape(2, 2, 64, D)
     swap_ng = to_sib(part, ng_r)
     swap_ng.start()
-    w1[0].relay()
-    w1[1].relay()
+    xv = tok[...].reshape(256, D).astype(F32)
+    rms = rms_of(xv)
+    gain_m = jnp.sum(part[...].reshape(256, D) * xv * rms, axis=0, keepdims=True)
+
+    def packed(gains):
+        high = gains.astype(BF).astype(F32)
+        rows = [high, gains - high]
+        rows = [r[:, HALF * i : HALF * i + HALF] for i in range(2) for r in rows]
+        return jnp.concatenate(rows + [jnp.zeros((8, HALF), F32)], axis=0).astype(BF)
+
+    def unpacked(rows):
+        return jnp.concatenate([rows[0:2] + rows[2:4], rows[4:6] + rows[6:8]], axis=1)
+
+    gs[...] = packed(jnp.concatenate([gain_m, 0.5 * gain_f], axis=0))
+    gr[x, y] = gs[...]
+    gain1 = gather_one(gr, "x", pool)
+    gain2 = gather_two(gr, "x", pool)
+    start([gain1])
     for pattern in a2:
         pattern.sent()
     step(2, 0)
     w1[2].relay()
     w1[3].relay()
+    w1[4].relay()
+    w1[5].relay()
+    wait_recv([gain1])
+    start([gain2])
     step(1, 1)
+    for i in (0, 1, 3, 4, 5, 2):
+        middle_sum(i)
+    step(3, 0)
     swap_ng.wait_recv()
     full = (part[...] + ng_r[...]).reshape(256, D)
-    xv = tok[...].reshape(256, D).astype(F32)
-    rms = rms_of(xv)
-    gain_m = jnp.sum(full * xv * rms, axis=0, keepdims=True)
     weighted = full * gm
     inner = jnp.mean(weighted * xv, axis=-1, keepdims=True)
     fng[...] = (rms * weighted - xv * (rms * rms * rms) * inner).reshape(2, 2, 64, D)
     ig_s[...] = mgrad[:, c] + fng[:, c]
     save(ig_s, input_grad)
-    gains = jnp.concatenate([gain_m, gain_f], axis=0)
-    high = gains.astype(BF).astype(F32)
-    gs[...] = jnp.concatenate([high, gains - high, jnp.zeros((12, D), F32)], axis=0).astype(BF)
-    gr[x, y] = gs[...]
-    gain1 = gather_one(gr, "x", pool)
-    gain2 = gather_two(gr, "x", pool)
-    start([gain1])
+    for i in range(2):
+        total = last_sum(i).astype(BF)
+        for a in range(2):
+            down_sum[2 * a + i, 0:48] = total[48 * a : 48 * a + 48]
+    total = last_sum(3).astype(BF)
+    for r in range(3):
+        down_sum[r, 48:64] = total[16 * r : 16 * r + 16]
+    down_sum[3, 48:64] = jnp.zeros((16, HALF), BF)
+    z_down1 = z_first(down_part, zr_down, (1, 2, 7))
+    start([z_down1])
+    rest[0:32] = last_sum(4).astype(BF)
+    rest[32:48] = last_sum(5).astype(BF)
+    wait_recv([gain2])
+    rest[48:64] = packed(unpacked(jnp.sum(gr[...].reshape(16, 16, HALF).astype(F32), axis=0)))
+    z_rest1 = z_first(rest_part, zr_rest, (7, 6, 1))
+    start([z_rest1])
+    half_up[...] = last_sum(2).astype(BF)
+    z_up2 = z_swap(half_up, other_up)
+    z_up2.start()
+    step(2, 1)
+    for pattern in w1[:3]:
+        pattern.sent()
+    wait_send(near + last)
+    wait_recv([z_down1])
+    z_half(down_part, zr_down, half_down)
+    z_down2 = z_swap(half_down, other_down)
+    z_down2.start()
+    wait_recv([z_rest1])
+    z_half(rest_part, zr_rest, half_rest)
+    z_rest2 = z_swap(half_rest, other_rest)
+    z_rest2.start()
+    step(3, 1)
 
     def rows_of(src, base, cc):
         return src[0, pl.ds(pl.multiple_of(base + 24 * cc, 8), 24)]
@@ -752,57 +808,16 @@
     swap_tg = [
         to_sib(tgs.at[pl.ds(3 * hf, 3)], tg_r.at[pl.ds(3 * hf, 3)]) for hf in range(2)
     ]
-    w1[4].relay()
-    w1[5].relay()
-    step(3, 0)
-    middle_sum(0)
-    middle_sum(1)
-    step(2, 1)
-    middle_sum(2)
-    middle_sum(3)
-    wait_recv([gain1])
-    start([gain2])
-    middle_sum(4)
-    middle_sum(5)
-    for i in range(2):
-        down_sum[:, HALF * i : HALF * i + HALF] = last_sum(i).astype(BF)
-    z_down1 = z_first(down_part, zr_down, (1, 2, 7))
-    start([z_down1])
-    half_up[...] = last_sum(2).astype(BF)
-    z_up2 = z_swap(half_up, other_up)
-    z_up2.start()
-    for pattern in w1[:3]:
-        pattern.sent()
-    wait_send(near + last)
-    step(3, 1)
-    rest[0:48, 0:HALF] = last_sum(3).astype(BF)
-    rest[0:32, HALF:D] = last_sum(4).astype(BF)
-    rest[32:48, HALF:D] = last_sum(5).astype(BF)
-    wait_recv([gain2])
-    gtot = jnp.sum(gr[...].reshape(16, 16, D).astype(F32), axis=0)
-    gains = gtot[0:2] + gtot[2:4]
-    high = gains.astype(BF).astype(F32)
-    rest[48:64] = jnp.concatenate([high, gains - high, jnp.zeros((12, D), F32)], axis=0).astype(BF)
-    z_rest1 = z_first(rest_part, zr_rest, (7, 6, 1))
-    start([z_rest1])
-    wait_recv([z_down1])
-    z_half(down_part, zr_down, half_down)
-    z_down2 = z_swap(half_down, other_down)
-    z_down2.start()
-    finish_ring(0)
     z_up2.wait_recv()
     z_up3 = z_last(half_up, other_up, zs_up, (1, 7, 2))
     start([z_up3])
-    wait_recv([z_rest1])
-    z_half(rest_part, zr_rest, half_rest)
-    z_rest2 = z_swap(half_rest, other_rest)
-    z_rest2.start()
     z_down2.wait_recv()
     z_down3 = z_last(half_down, other_down, zs_down, (1, 7, 6))
     start([z_down3])
-    for pattern in w1[3:]:
-        pattern.sent()
-    wait_send(w2 + [z_down1, z_rest1, gain1, gain2])
+    z_rest2.wait_recv()
+    z_rest3 = z_last(half_rest, other_rest, zs_rest, (1, 7, 6))
+    start([z_rest3])
+    finish_ring(0)
     finish_ring(1)
     wait_recv([z_up3])
     for m in range(4):
@@ -812,43 +827,48 @@
         ref[:, D : 2 * D] = rows_of(act, 48, cc)
     swap_up = to_sib(post_up.at[1], post_up.at[2])
     swap_up.start()
-    z_rest2.wait_recv()
-    z_rest3 = z_last(half_rest, other_rest, zs_rest, (1, 7, 6))
-    start([z_rest3])
-    wait_recv([z_down3])
-    for m in range(4):
-        rows, cols = slice(48 * (m // 2), 48 * (m // 2) + 48), slice(HALF * (m % 2), HALF * (m % 2) + HALF)
-        down_s[rows, cols] = zs_down[m].astype(F32)
-    save(down_s, d_down)
+    for pattern in w1[3:]:
+        pattern.sent()
+    wait_send(w2 + [z_down1, z_rest1, gain1, gain2])
     first_core = (c == 0).astype(F32)
 
     def by_core(ref):
         own, got = ref[0], ref[2]
         return own * first_core + got * (1.0 - first_core), got * first_core + own * (1.0 - first_core)
 
+    wait_recv([z_rest3])
+    for r in range(3):
+        act[0, 96 + 16 * r : 112 + 16 * r, HALF:D] = zs_rest[r].astype(F32)
+    gains = unpacked(zs_rest[3].astype(F32))
+    wait_recv([z_down3])
+    for r in range(3):
+        act[0, 96 + 16 * r : 112 + 16 * r, 0:HALF] = zs_down[r, 48:64].astype(F32)
+    for i, cc in enumerate((c, 1 - c)):
+        post_rest[i, 0:24] = rows_of(act, 96, cc)
+        post_rest[i, 24:32] = jnp.concatenate([gains, jnp.zeros((6, D), F32)], axis=0)
+    swap_rest = to_sib(post_rest.at[1], post_rest.at[2])
+    swap_rest.start()
+    for m in range(4):
+        rows, cols = slice(48 * (m // 2), 48 * (m // 2) + 48), slice(HALF * (m % 2), HALF * (m % 2) + HALF)
+        down_s[rows, cols] = zs_down[m, 0:48].astype(F32)
+    save(down_s, d_down)
+    for hf in range(2):
+        swap_tg[hf].wait_recv()
+        save(tg_r.at[pl.ds(3 * hf, 3)], tg.at[1 - c, pl.ds(3 * hf, 3)])
     swap_up.wait_recv()
     pair = by_core(post_up)
     for m in range(4):
         block = jnp.concatenate([p[:, HALF * m : HALF * m + HALF] for p in pair], axis=1).astype(BF)
         up_s_out[:, D * m : D * m + D] = dot_nt(block, perm[...])
     save(up_s_out, d_up)
-    wait_recv([z_rest3])
-    act[0, 0:64] = zs_rest[...].reshape(64, D).astype(F32)
-    for cc, ref in ((c, post_rest.at[0]), (1 - c, post_rest.at[1])):
-        ref[...] = rows_of(act, 0, cc)
-    swap_rest = to_sib(post_rest.at[1], post_rest.at[2])
-    swap_rest.start()
-    gsum_s[...] = jnp.concatenate([act[0, 48:50] + act[0, 50:52], jnp.zeros((6, D), F32)], axis=0)
+    swap_rest.wait_recv()
+    gsum_s[...] = post_rest[0, 24:32] + post_rest[2, 24:32]
     save(gsum_s, gsum)
-    for hf in range(2):
-        swap_tg[hf].wait_recv()
-        save(tg_r.at[pl.ds(3 * hf, 3)], tg.at[1 - c, pl.ds(3 * hf, 3)])
-    swap_rest.wait_recv()
     pair = by_core(post_rest)
     for cc in range(2):
         cols = slice(HALF * cc, HALF * cc + HALF)
-        two_s[0, :, cols] = pair[cc][:, 0:HALF]
-        two_s[1, :, cols] = pair[cc][:, HALF:D]
+        two_s[0, :, cols] = pair[cc][0:24, 0:HALF]
+        two_s[1, :, cols] = pair[cc][0:24, HALF:D]
     save(two_s.at[0], d_out)
     save(two_s.at[1], d_value)
     for copy in saved:
@@ -891,7 +911,7 @@
         in_specs=[pl.BlockSpec(memory_space=pltpu.SMEM)] + [IN_VMEM] * 8 + [pl.BlockSpec(memory_space=pl.ANY)],
         out_specs=[ANY] * 8,
         scratch_shapes=[
-            vmem(D, D), vmem(2, 24, 2 * D, kind=F32), vmem(2, 24, 2 * D, kind=F32),
+            vmem(D, D), vmem(2, 24, D, kind=F32), vmem(2, 24, D, kind=F32), vmem(2, 24, D, kind=F32), vmem(2, 24, D, kind=F32),
             vmem(2, 2, 64, D), vmem(2, 2, 64, D), vmem(HH, 2, 64, 2048),
             vmem(4, 4, 48, HALF), vmem(2, 4, 4, 48, HALF), vmem(8, 4, 4, 48, HALF),
             vmem(4, 4, ROWS, 128), vmem(4, 4, ROWS, 128), vmem(3, 4, ROWS, 128), vmem(3, 4, ROWS, 128),
@@ -906,13 +926,13 @@
             vmem(2, 3, 4, 96, HALF), vmem(3, 3, 4, 48, HALF), vmem(2, 4, 96, HALF), vmem(3, 4, 48, HALF),
             vmem(2, 3, 96, HALF), vmem(3, 3, 48, HALF),
             vmem(2, 2, 4, 48, HALF), vmem(2, 2, 4, 48, HALF), vmem(2, 2, 4, 48, HALF), vmem(2, 2, 4, 48, HALF),
-            vmem(16, D), vmem(4, 4, 16, D),
+            vmem(16, HALF), vmem(4, 4, 16, HALF),
             vmem(2, 4, 3, 128, 256), vmem(2, 4, 3, 128, 256), vmem(2, 4, 3, 128, 256), vmem(2, 4, 3, 128, 256),
             vmem(HH, 64, 256, kind=F32), vmem(HH, 64, 256, kind=F32), vmem(2, HALF, 128, kind=F32),
-            vmem(2, 2, 64, D, kind=F32), vmem(96, D), vmem(64, D), vmem(3, 48, HALF), vmem(3, 16, D),
-            vmem(48, HALF), vmem(48, HALF), vmem(16, D), vmem(48, HALF), vmem(48, HALF), vmem(16, D),
-            vmem(4, 48, HALF), vmem(4, 48, HALF), vmem(4, 16, D),
-            vmem(3, 24, 2 * D, kind=F32), vmem(3, 24, D, kind=F32), vmem(2, 64, D), vmem(2, 64, D, kind=F32),
+            vmem(2, 2, 64, D, kind=F32), vmem(4, 64, HALF), vmem(64, HALF), vmem(3, 64, HALF), vmem(3, 16, HALF),
+            vmem(48, HALF), vmem(64, HALF), vmem(16, HALF), vmem(48, HALF), vmem(64, HALF), vmem(16, HALF),
+            vmem(4, 48, HALF), vmem(4, 64, HALF), vmem(4, 16, HALF),
+            vmem(3, 24, 2 * D, kind=F32), vmem(3, 32, D, kind=F32), vmem(2, 64, D), vmem(2, 64, D, kind=F32),
             vmem(96, D, kind=F32), vmem(24, 4 * D, kind=F32), vmem(HH, 64, 256, kind=F32),
             vmem(8, D, kind=F32), vmem(2, 24, D, kind=F32),
             pltpu.SemaphoreType.DMA((SEMS,)),

time: 141 us -> 137 us (0.972); the launches traced: 141 us -> 135 us
  Pallas kernels: 140 us -> 134 us
    pallas_call x1, Pallas kernels: 137 us -> 131 us  [per_device(): pl.pallas_call(layer, name='layer', out_shape=shapes, in_specs=[pl.BlockS...]
where the time goes in v5:
time: 137 us; the launch traced here: 135 us
  Pallas kernels  134 us (98%)
    pallas_call x1, Pallas kernels, per_device(): pl.pallas_call(layer, name='layer', out_shape=shapes, in_specs=[pl.BlockS...  131 us
    pallas_call x1, Pallas kernels, per_device(): pl.pallas_call(finish, name='finish', out_shape=shapes[:6] + [shapes[7],...  3.29 us

profile of v5, /device:TPU:1, one launch (start us, length us, event | category | flops | bytes accessed | tf_op | source)
XLA Modules:
  0.0 134.9 jit_solution(12238118990721514617)
XLA Ops:
  0.6 130.9 %layer.1 = (bf16[2,64,768]{2,1,0:T(8,128)(2,1)}, f32[2,64,768]{2,1,0:T(8,128)}, f32[24,768]{1,0:T(8,128)}, f32[24,768]{1,0:T(8,128)}, f32[24,3072]{1,0:T(8,128)}...) custom-call(s32[2]{0:T(128)} %lengths.1, bf16[2,64,768]{2,1,0:T(8,128)(2,1)} %tokens.1, ...), custom_call_target="tpu_custom_call" | custom-call | tf_op jit(solution)/shard_map/layer/pallas_call | solution.py:907
  131.6 3.3 %finish.1 = (bf16[2,64,768]{2,1,0:T(8,128)(2,1)}, f32[2,64,768]{2,1,0:T(8,128)}, f32[24,768]{1,0:T(8,128)}, f32[24,768]{1,0:T(8,128)}, f32[24,3072]{1,0:T(8,128)...) custom-call(bf16[2,64,768]{2,1,0:T(8,128)(2,1)} %get-tuple-element.26.out, ...), custom_call_target="tpu_custom_call" | custom-call | tf_op jit(solution)/shard_map/finish/pallas_call | solution.py:944

commit v6 on v5

--- a/solution.py
+++ b/solution.py
@@ -250,7 +250,7 @@
     out, input_grad, d_value, d_out, d_up, d_down, gsum, tg,
     perm, pre_a, pre_b, got_a, got_b, tok, og, e, wv, wo_all, wz,
     ux, uy, rx, ry, mx, my, rx2, ry2, mt, rr, mix, vt, vals, mcol, normed, middle, nf, bgs, hid, pgr, act,
-    part, part_r, fng, fng_r, mgrad, dwu, dwda, dwdb, dws, dwo, dwv, gx, gy,
+    part, part_r, fng, fng_b, fng_r, mgrad, dwu, dwda, dwdb, dws, dwo, dwv, gx, gy,
     rd, rl, md, ml, rd2, rl2, dfar, dnear, dlast, dsum, gs, gr, up_s, up_r, dn_s, dn_r, tgs, tg_r, vgt, ng_r,
     down_sum, rest, zr_down, zr_rest, half_up, half_down, half_rest, other_up, other_down, other_rest,
     zs_up, zs_down, zs_rest, post_up, post_rest,
@@ -546,7 +546,8 @@
         pgr[hf] = (act[hf] * dot_nt(grad, down_cols(hf))).astype(BF)
         more = dot_nt(pgr[hf], up_rows(hf)).reshape(2, 2, 64, D)
         fng[...] = more if hf == 0 else fng[...] + more
-    swap_fng = to_sib(fng, fng_r)
+    fng_b[...] = fng[...].astype(BF)
+    swap_fng = to_sib(fng_b, fng_r)
     swap_fng.start()
     for hf in range(2):
         grad_w = dot(flip(nf[...]), pgr[hf]).astype(BF)
@@ -554,7 +555,7 @@
             dwu[2 * hf + i] = grad_w[:, HALF * i : HALF * i + HALF].reshape(4, 4, 48, HALF)
     start(far)
     swap_fng.wait_recv()
-    full = (fng[...] + fng_r[...]).reshape(256, D)
+    full = (fng_b[...].astype(F32) + fng_r[...].astype(F32)).reshape(256, D)
     mid_v = middle[...]
     rms = rms_of(mid_v)
     gain_f = jnp.sum(full * mid_v * rms, axis=0, keepdims=True)
@@ -681,11 +682,11 @@
         buf = (gx, gy)[hf]
         for hh in range(3):
             total = jnp.zeros((128, 128), F32)
-            for k in range(16):
-                cols = slice(128 * k, 128 * k + 128)
-                total = total + dot_nt(
-                    buf[k // 4, k % 4, 128 * hh : 128 * hh + 128], e[3 * hf + hh, :, :, cols].reshape(128, 128)
-                )
+            rows = slice(128 * hh, 128 * hh + 128)
+            for k in range(0, 16, 4):
+                g = jnp.concatenate([buf[k // 4, i, rows] for i in range(4)], axis=1)
+                cols = slice(128 * k, 128 * k + 512)
+                total = total + dot_nt(g, e[3 * hf + hh, :, :, cols].reshape(128, 512))
             rows = slice(64 * (3 * hf + hh), 64 * (3 * hf + hh) + 64)
             for b in range(2):
                 vgt[b, rows] = total[64 * b : 64 * b + 64] * masks[b]
@@ -920,7 +921,7 @@
             vmem(HH, 128, 128), vmem(2, 128, 128, kind=F32), vmem(256, D), vmem(256, D, kind=F32), vmem(256, D),
             vmem(256, D), vmem(2, 256, D), vmem(2, 256, D), vmem(2, 256, D, kind=F32),
             vmem(2, 2, 64, D, kind=F32), vmem(2, 64, D, kind=F32), vmem(2, 2, 64, D, kind=F32),
-            vmem(2, 2, 64, D, kind=F32), vmem(2, 2, 64, D, kind=F32),
+            vmem(2, 2, 64, D), vmem(2, 2, 64, D), vmem(2, 2, 64, D, kind=F32),
             vmem(4, 4, 4, 48, HALF), vmem(4, 4, 96, HALF), vmem(4, 4, 96, HALF), vmem(4, 4, 48, HALF), vmem(4, 4, 48, HALF),
             vmem(4, 4, 48, HALF), vmem(4, 4, ROWS, 128), vmem(4, 4, ROWS, 128),
             vmem(2, 3, 4, 96, HALF), vmem(3, 3, 4, 48, HALF), vmem(2, 4, 96, HALF), vmem(3, 4, 48, HALF),

time: 137 us -> 136 us (level); the launches traced: 135 us -> 136 us
  no operation moved by 1% of the time
where the time goes in v6:
time: 136 us
  Pallas kernels  135 us (99%)
    pallas_call x1, Pallas kernels, per_device(): pl.pallas_call(layer, name='layer', out_shape=shapes, in_specs=[pl.BlockS...  132 us
    pallas_call x1, Pallas kernels, per_device(): pl.pallas_call(finish, name='finish', out_shape=shapes[:6] + [shapes[7],...  3.29 us

profile of v6, /device:TPU:1, one launch (start us, length us, event | category | flops | bytes accessed | tf_op | source)
XLA Modules:
  0.0 135.9 jit_solution(833640492945997580)
XLA Ops:
  0.6 132.0 %layer.1 = (bf16[2,64,768]{2,1,0:T(8,128)(2,1)}, f32[2,64,768]{2,1,0:T(8,128)}, f32[24,768]{1,0:T(8,128)}, f32[24,768]{1,0:T(8,128)}, f32[24,3072]{1,0:T(8,128)}...) custom-call(s32[2]{0:T(128)} %lengths.1, bf16[2,64,768]{2,1,0:T(8,128)(2,1)} %tokens.1, ...), custom_call_target="tpu_custom_call" | custom-call | tf_op jit(solution)/shard_map/layer/pallas_call | solution.py:908
  132.6 3.3 %finish.1 = (bf16[2,64,768]{2,1,0:T(8,128)(2,1)}, f32[2,64,768]{2,1,0:T(8,128)}, f32[24,768]{1,0:T(8,128)}, f32[24,768]{1,0:T(8,128)}, f32[24,3072]{1,0:T(8,128)...) custom-call(bf16[2,64,768]{2,1,0:T(8,128)(2,1)} %get-tuple-element.26.out, ...), custom_call_target="tpu_custom_call" | custom-call | tf_op jit(solution)/shard_map/finish/pallas_call | solution.py:945
